TPU v7x, 32 devices: a whole 2x2x4 slice. The times are simulated.
32 devices in a mesh: slab: 8 (over z, core), clus: 4 (over y, x).
Axes of the slice: x: 2, y: 2, z: 4, core: 2. Of those that a mesh axis runs over, the one named last changes fastest.
Arguments:
- incident: float32 [8, 128, 200], P(None, ('slab', 'clus')), may hold values from -6 to 6
- history: float32 [16, 128, 200], P(None, ('slab', 'clus')), may hold values from -6 to 6
- near_blocks: bfloat16 [128, 12, 200, 200], P(('slab', 'clus')), may hold values from -0.09375 to 0.09375
- near_idx: int32 [128, 12], P(('slab', 'clus')), may hold values from 0 to 127, as said below
- near_cnt: int32 [128], P(('slab', 'clus')), may hold values from 3 to 12
- near_lag: int32 [128, 12], P(('slab', 'clus')), may hold values from 1 to 15
- near_frac: float32 [128, 12], P(('slab', 'clus')), may hold values from 0 to 1
- inverses: bfloat16 [128, 200, 200], P(('slab', 'clus')), may hold values from -0.4375 to 0.4375
- rays: bfloat16 [128, 512, 200], P(('slab', 'clus')), may hold values from -0.4375 to 0.4375
- shift: float32 [128, 512], P(('slab', 'clus')), may hold values from -1 to 1
- far_idx: int32 [32, 8], replicated, may hold values from 0 to 31, as said below
- far_lag: int32 [32, 8], replicated, may hold values from 1 to 16
- trans: bfloat16 [32, 8, 512], replicated, may hold values from -0.5 to 0.5
Outputs:
- currents: float32 [8, 128, 200], P(None, ('slab', 'clus'))
Inputs may be any that keep to these rules, and one draw needn't show every extreme that they name: `near_idx`: every entry is a cluster whose slab (cluster number divided by 16) differs by at most one from the slab of the entry's row. `far_idx`: every entry is a group whose slab (group number divided by the number of devices along clus) differs by two or more from the slab of the entry's row.
All inputs are finite; a program needn't handle non-finite values.
Results may differ from a plain program's by a relative error of at most 0.0045.
Values sent between devices are 32-bit elements; how exact they have to be, the bound alone decides.
No kernel may reach another device: no remote copies, remote signals or barrier semaphores. Data moves between devices by JAX's collectives and lax.ppermute only.
A program may use at most 128 MiB of HBM per device.

v0:
```python
import jax
import jax.numpy as jnp
from jax import lax
from jax.sharding import PartitionSpec as P


def extended(block, sides, width):
    for axis, dim in sides:
        count = lax.axis_size(axis)
        forward = [(i, i + 1) for i in range(count - 1)]
        backward = [(target, source) for source, target in forward]
        low = lax.ppermute(
            lax.slice_in_dim(block, block.shape[dim] - width, None, axis=dim), axis, forward
        )
        high = lax.ppermute(lax.slice_in_dim(block, 0, width, axis=dim), axis, backward)
        block = jnp.concatenate([low, block, high], axis=dim)
    return block


def project_out(rays, shift, current):
    ray_vals = jnp.einsum(
        "cdu,cu->cd", rays, current.astype(jnp.bfloat16), preferred_element_type=jnp.float32
    )
    return jnp.sum(ray_vals * shift, axis=0)


def widen_history(history, slab_size):
    gathered = lax.all_gather(history, "clus", axis=1, tiled=True)
    return extended(gathered, (("slab", 1),), slab_size)


def widen_step(current, slab_size):
    gathered = lax.all_gather(current, "clus", axis=0, tiled=True)
    return extended(gathered, (("slab", 0),), slab_size)


def local(
    incident,
    history,
    near_blocks,
    near_idx,
    near_cnt,
    near_lag,
    near_frac,
    inverses,
    rays,
    shift,
    far_idx,
    far_lag,
    trans,
):
    lag_count = history.shape[0]
    step_count = incident.shape[0]
    local_count = history.shape[1]
    dir_count = rays.shape[1]
    slab_count = lax.axis_size("slab")
    clus_count = lax.axis_size("clus")
    slab_size = local_count * clus_count
    group_count = slab_count * clus_count
    slab_index = lax.axis_index("slab")
    myself = slab_index * clus_count + lax.axis_index("clus")
    near_local = near_idx - (slab_index - 1) * slab_size
    neighbours = widen_history(history, slab_size)
    near_time = jnp.concatenate(
        [neighbours, jnp.zeros((step_count,) + neighbours.shape[1:], jnp.float32)], axis=0
    )
    hist_rays = jnp.einsum(
        "cdu,tcu->tcd", rays, history.astype(jnp.bfloat16), preferred_element_type=jnp.float32
    )
    own_hist = jnp.sum(hist_rays * shift[None], axis=1)
    own_time = jnp.concatenate([own_hist, jnp.zeros((step_count, dir_count), jnp.float32)], axis=0)
    spectra_all = lax.all_gather(own_hist[:, None, :], ("slab", "clus"), axis=1, tiled=True)
    spectra_all = jnp.concatenate(
        [spectra_all, jnp.zeros((step_count, group_count, dir_count), jnp.float32)], axis=0
    )
    idx_row = lax.dynamic_index_in_dim(far_idx, myself, 0, keepdims=False)
    lag_row = lax.dynamic_index_in_dim(far_lag, myself, 0, keepdims=False)
    trans_row = lax.dynamic_index_in_dim(trans, myself, 0, keepdims=False).astype(jnp.float32)
    live_slot = jnp.arange(near_idx.shape[1])[None, :] < near_cnt[:, None]
    near_weight = near_frac[..., None]
    outputs = []
    for step_index in range(step_count):
        lag_slot = step_index - near_lag + lag_count
        first_lag = near_time[lag_slot, near_local]
        second = near_time[lag_slot - 1, near_local]
        blended = jnp.where(
            live_slot[..., None], (1.0 - near_weight) * first_lag + near_weight * second, 0.0
        ).astype(jnp.bfloat16)
        near_field = jnp.einsum(
            "cjuv,cjv->cu", near_blocks, blended, preferred_element_type=jnp.float32
        )
        picked = spectra_all[step_index - lag_row + lag_count, idx_row]
        incoming = jnp.sum(trans_row * picked, axis=0)
        inbound = (shift * incoming[None, :]).astype(jnp.bfloat16)
        far_field = jnp.einsum("cdu,cd->cu", rays, inbound, preferred_element_type=jnp.float32)
        right_side = (incident[step_index] - near_field - far_field).astype(jnp.bfloat16)
        current = jnp.einsum("cuv,cv->cu", inverses, right_side, preferred_element_type=jnp.float32)
        outputs.append(current)
        if step_index + 1 < step_count:
            spectrum = project_out(rays, shift, current)
            own_time = own_time.at[lag_count + step_index].set(spectrum)
            near_time = near_time.at[lag_count + step_index].set(widen_step(current, slab_size))
            fresh_rays = lax.all_gather(spectrum[None, :], ("slab", "clus"), axis=0, tiled=True)
            spectra_all = spectra_all.at[lag_count + step_index].set(fresh_rays)
    return jnp.stack(outputs, axis=0)


def solution(mesh):
    in_specs = (
        P(None, ("slab", "clus"), None),
        P(None, ("slab", "clus"), None),
        P(("slab", "clus"), None, None, None),
        P(("slab", "clus"), None),
        P(("slab", "clus")),
        P(("slab", "clus"), None),
        P(("slab", "clus"), None),
        P(("slab", "clus"), None, None),
        P(("slab", "clus"), None, None),
        P(("slab", "clus"), None),
        P(),
        P(),
        P(),
    )
    out_specs = P(None, ("slab", "clus"), None)
    return jax.shard_map(local, mesh=mesh, in_specs=in_specs, out_specs=out_specs, check_vma=False)
```

profile of v0, /device:TPU:0, one launch (start us, length us, event | category | flops | bytes accessed | tf_op | source)
XLA Modules:
  0.0 673.9 jit_solution(2319160175493874688)
XLA Ops:
  10.1 10.4 %all_gather.48 = f32[16,16,200]{2,0,1:T(8,128)S(1)} all-gather(f32[16,4,200]{2,0,1:T(8,128)S(1)} %copy.16), channel_id=1, replica_groups=mesh['slab'=8,'clus'=4] {'clus'}, dimensions={1}, use_global_device_ids=true | all-gather | bytes 256000 | tf_op jit(solution)/shard_map/all_gather | solution.py:28
  29.5 3.7 fusion.22
  33.2 33.6 %all-gather.24.cloned.1.call-done = f32[16,16384]{1,0:T(8,128)} async-done(((f32[16,512]{1,0:T(8,128)}), f32[16,16384]{1,0:T(8,128)}) %all-gather.24.cloned.1.call-update) | async-done | bytes 1048592 | tf_op jit(solution)/shard_map/all_gather | solution.py:72
  72.6 8.1 %all-gather.8 = f32[4,4,200]{2,1,0:T(4,128)S(1)} all-gather(f32[1,4,200]{2,1,0:T(4,128)S(1)} %bitcast.498), channel_id=1, replica_groups=mesh['slab'=8,'clus'=4] {'clus'}, dimensions={0}, use_global_device_ids=true | all-gather | bytes 16000 | tf_op jit(solution)/shard_map/all_gather | solution.py:33
  83.6 68.1 %all-gather.9 = f32[32,1,512]{2,1,0:T(1,128)S(1)} all-gather(f32[1,1,512]{2,1,0:T(1,128)S(1)} %bitcast.505), channel_id=3, replica_groups=mesh['slab'=8,'clus'=4] {'slab','clus'}, dimensions={0}, use_global_device_ids=true | all-gather | bytes 67584 | tf_op jit(solution)/shard_map/all_gather | solution.py:103
  156.8 3.7 fusion.20
  160.8 6.4 all-gather.10
  170.1 66.0 %all-gather.11 = f32[32,1,512]{2,1,0:T(1,128)S(1)} all-gather(f32[1,1,512]{2,1,0:T(1,128)S(1)} %bitcast.506), channel_id=4, replica_groups=mesh['slab'=8,'clus'=4] {'slab','clus'}, dimensions={0}, use_global_device_ids=true | all-gather | bytes 67584 | tf_op jit(solution)/shard_map/all_gather | solution.py:103
  241.1 3.7 fusion.18
  245.1 6.7 all-gather.12
  254.6 65.7 %all-gather.13 = f32[32,1,512]{2,1,0:T(1,128)S(1)} all-gather(f32[1,1,512]{2,1,0:T(1,128)S(1)} %bitcast.507), channel_id=5, replica_groups=mesh['slab'=8,'clus'=4] {'slab','clus'}, dimensions={0}, use_global_device_ids=true | all-gather | bytes 67584 | tf_op jit(solution)/shard_map/all_gather | solution.py:103
  325.3 3.7 fusion.16
  329.3 6.9 %all-gather.14 = f32[4,4,200]{2,1,0:T(4,128)S(1)} all-gather(f32[1,4,200]{2,1,0:T(4,128)S(1)} %bitcast.501), channel_id=1, replica_groups=mesh['slab'=8,'clus'=4] {'clus'}, dimensions={0}, use_global_device_ids=true | all-gather | bytes 16000 | tf_op jit(solution)/shard_map/all_gather | solution.py:33
  339.1 65.6 %all-gather.15 = f32[32,1,512]{2,1,0:T(1,128)S(1)} all-gather(f32[1,1,512]{2,1,0:T(1,128)S(1)} %bitcast.508), channel_id=6, replica_groups=mesh['slab'=8,'clus'=4] {'slab','clus'}, dimensions={0}, use_global_device_ids=true | all-gather | bytes 67584 | tf_op jit(solution)/shard_map/all_gather | solution.py:103
  409.8 3.7 fusion.14
  413.7 7.2 %all-gather.16 = f32[4,4,200]{2,1,0:T(4,128)S(1)} all-gather(f32[1,4,200]{2,1,0:T(4,128)S(1)} %bitcast.502), channel_id=1, replica_groups=mesh['slab'=8,'clus'=4] {'clus'}, dimensions={0}, use_global_device_ids=true | all-gather | bytes 16000 | tf_op jit(solution)/shard_map/all_gather | solution.py:33
  423.8 65.1 %all-gather.17 = f32[32,1,512]{2,1,0:T(1,128)S(1)} all-gather(f32[1,1,512]{2,1,0:T(1,128)S(1)} %bitcast.509), channel_id=7, replica_groups=mesh['slab'=8,'clus'=4] {'slab','clus'}, dimensions={0}, use_global_device_ids=true | all-gather | bytes 67584 | tf_op jit(solution)/shard_map/all_gather | solution.py:103
  494.0 3.7 fusion.12
  498.0 7.5 %all-gather.18 = f32[4,4,200]{2,1,0:T(4,128)S(1)} all-gather(f32[1,4,200]{2,1,0:T(4,128)S(1)} %bitcast.503), channel_id=1, replica_groups=mesh['slab'=8,'clus'=4] {'clus'}, dimensions={0}, use_global_device_ids=true | all-gather | bytes 16000 | tf_op jit(solution)/shard_map/all_gather | solution.py:33
  508.3 64.8 %all-gather.19 = f32[32,1,512]{2,1,0:T(1,128)S(1)} all-gather(f32[1,1,512]{2,1,0:T(1,128)S(1)} %bitcast.510), channel_id=8, replica_groups=mesh['slab'=8,'clus'=4] {'slab','clus'}, dimensions={0}, use_global_device_ids=true | all-gather | bytes 67584 | tf_op jit(solution)/shard_map/all_gather | solution.py:103
  578.2 3.7 fusion.10
  582.2 7.8 %all-gather.20 = f32[4,4,200]{2,1,0:T(4,128)S(1)} all-gather(f32[1,4,200]{2,1,0:T(4,128)S(1)} %bitcast.504), channel_id=1, replica_groups=mesh['slab'=8,'clus'=4] {'clus'}, dimensions={0}, use_global_device_ids=true | all-gather | bytes 16000 | tf_op jit(solution)/shard_map/all_gather | solution.py:33
  592.9 64.5 %all-gather.21 = f32[32,1,512]{2,1,0:T(1,128)S(1)} all-gather(f32[1,1,512]{2,1,0:T(1,128)S(1)} %bitcast.511), channel_id=9, replica_groups=mesh['slab'=8,'clus'=4] {'slab','clus'}, dimensions={0}, use_global_device_ids=true | all-gather | bytes 67584 | tf_op jit(solution)/shard_map/all_gather | solution.py:103
  662.5 3.7 fusion.8
  (222 shorter events, 75.3 us)
Async XLA Ops:
  6.5 16.8 %copy-start.8 = (s32[4,12]{1,0:T(4,128)S(1)}, s32[4,12]{1,0:T(4,128)}, u32[]{:S(2)}) copy-start(s32[4,12]{1,0:T(4,128)} %param.44) | copy-start | bytes 580
  6.5 16.8 %copy-start.7 = (s32[4,12]{1,0:T(4,128)S(1)}, s32[4,12]{1,0:T(4,128)}, u32[]{:S(2)}) copy-start(s32[4,12]{1,0:T(4,128)} %param.46) | copy-start | bytes 580
  6.5 17.6 %copy-start.6 = (s32[32,8]{0,1:T(8,128)S(1)}, s32[32,8]{0,1:T(8,128)}, u32[]{:S(2)}) copy-start(s32[32,8]{0,1:T(8,128)} %param.51) | copy-start | bytes 3076
  6.5 17.6 %copy-start.5 = (s32[32,8]{0,1:T(8,128)S(1)}, s32[32,8]{0,1:T(8,128)}, u32[]{:S(2)}) copy-start(s32[32,8]{0,1:T(8,128)} %param.52) | copy-start | bytes 3076
  6.5 18.1 %copy-start.3 = (f32[4,12]{1,0:T(4,128)S(1)}, f32[4,12]{1,0:T(4,128)}, u32[]{:S(2)}) copy-start(f32[4,12]{1,0:T(4,128)} %param.47) | copy-start | bytes 580
  6.6 18.1 %copy-start.10 = (s32[4]{0:T(128)S(1)}, s32[4]{0:T(128)}, u32[]{:S(2)}) copy-start(s32[4]{0:T(128)} %param.45) | copy-start | bytes 52
  6.6 60.3 %all-gather.24.cloned.1.call-start = ((), (), s32[]{:S(2)}) async-start(), calls=%async_computation | async-start | bytes 1081344 | tf_op jit(solution)/shard_map/all_gather | solution.py:72
  20.7 4.0 collective-permute-start
  22.1 5.2 collective-permute-start.1
  80.8 74.0 %collective-permute-start.2 = (f32[16,200]{1,0:T(8,128)S(1)}, f32[16,200]{1,0:T(8,128)S(1)}, u32[]{:S(2)}, u32[]{:S(2)}) collective-permute-start(f32[16,200]{1,0:T(8,128)S(1)} %reshape.947), channel_id=1, source_target_pairs={{0,4},{4,8},{8,12},{12,16},{16,20},{20,24},{24,28},{1,5},{5,9},{9,... | collective-permute-start | bytes 38408 | tf_op jit(solution)/shard_map/ppermute | solution.py:12
  82.1 72.7 %collective-permute-start.3 = (f32[16,200]{1,0:T(8,128)S(1)}, f32[16,200]{1,0:T(8,128)S(1)}, u32[]{:S(2)}, u32[]{:S(2)}) collective-permute-start(f32[16,200]{1,0:T(8,128)S(1)} %reshape.947), channel_id=1, source_target_pairs={{4,0},{8,4},{12,8},{16,12},{20,16},{24,20},{28,24},{5,1},{9,5},{13... | collective-permute-start | bytes 38408 | tf_op jit(solution)/shard_map/ppermute | solution.py:15
  167.2 71.7 %collective-permute-start.4 = (f32[16,200]{1,0:T(8,128)S(1)}, f32[16,200]{1,0:T(8,128)S(1)}, u32[]{:S(2)}, u32[]{:S(2)}) collective-permute-start(f32[16,200]{1,0:T(8,128)S(1)} %reshape.951), channel_id=1, source_target_pairs={{0,4},{4,8},{8,12},{12,16},{16,20},{20,24},{24,28},{1,5},{5,9},{9,... | collective-permute-start | bytes 38408 | tf_op jit(solution)/shard_map/ppermute | solution.py:12
  168.5 70.5 %collective-permute-start.5 = (f32[16,200]{1,0:T(8,128)S(1)}, f32[16,200]{1,0:T(8,128)S(1)}, u32[]{:S(2)}, u32[]{:S(2)}) collective-permute-start(f32[16,200]{1,0:T(8,128)S(1)} %reshape.951), channel_id=1, source_target_pairs={{4,0},{8,4},{12,8},{16,12},{20,16},{24,20},{28,24},{5,1},{9,5},{13... | collective-permute-start | bytes 38408 | tf_op jit(solution)/shard_map/ppermute | solution.py:15
  251.7 71.5 %collective-permute-start.6 = (f32[16,200]{1,0:T(8,128)S(1)}, f32[16,200]{1,0:T(8,128)S(1)}, u32[]{:S(2)}, u32[]{:S(2)}) collective-permute-start(f32[16,200]{1,0:T(8,128)S(1)} %reshape.955), channel_id=1, source_target_pairs={{0,4},{4,8},{8,12},{12,16},{16,20},{20,24},{24,28},{1,5},{5,9},{9,... | collective-permute-start | bytes 38408 | tf_op jit(solution)/shard_map/ppermute | solution.py:12
  253.0 70.2 %collective-permute-start.7 = (f32[16,200]{1,0:T(8,128)S(1)}, f32[16,200]{1,0:T(8,128)S(1)}, u32[]{:S(2)}, u32[]{:S(2)}) collective-permute-start(f32[16,200]{1,0:T(8,128)S(1)} %reshape.955), channel_id=1, source_target_pairs={{4,0},{8,4},{12,8},{16,12},{20,16},{24,20},{28,24},{5,1},{9,5},{13... | collective-permute-start | bytes 38408 | tf_op jit(solution)/shard_map/ppermute | solution.py:15
  336.3 71.4 %collective-permute-start.8 = (f32[16,200]{1,0:T(8,128)S(1)}, f32[16,200]{1,0:T(8,128)S(1)}, u32[]{:S(2)}, u32[]{:S(2)}) collective-permute-start(f32[16,200]{1,0:T(8,128)S(1)} %reshape.959), channel_id=1, source_target_pairs={{0,4},{4,8},{8,12},{12,16},{16,20},{20,24},{24,28},{1,5},{5,9},{9,... | collective-permute-start | bytes 38408 | tf_op jit(solution)/shard_map/ppermute | solution.py:12
  337.6 70.1 %collective-permute-start.9 = (f32[16,200]{1,0:T(8,128)S(1)}, f32[16,200]{1,0:T(8,128)S(1)}, u32[]{:S(2)}, u32[]{:S(2)}) collective-permute-start(f32[16,200]{1,0:T(8,128)S(1)} %reshape.959), channel_id=1, source_target_pairs={{4,0},{8,4},{12,8},{16,12},{20,16},{24,20},{28,24},{5,1},{9,5},{13... | collective-permute-start | bytes 38408 | tf_op jit(solution)/shard_map/ppermute | solution.py:15
  421.0 70.9 %collective-permute-start.10 = (f32[16,200]{1,0:T(8,128)S(1)}, f32[16,200]{1,0:T(8,128)S(1)}, u32[]{:S(2)}, u32[]{:S(2)}) collective-permute-start(f32[16,200]{1,0:T(8,128)S(1)} %reshape.963), channel_id=1, source_target_pairs={{0,4},{4,8},{8,12},{12,16},{16,20},{20,24},{24,28},{1,5},{5,9},{9,... | collective-permute-start | bytes 38408 | tf_op jit(solution)/shard_map/ppermute | solution.py:12
  422.3 69.6 %collective-permute-start.11 = (f32[16,200]{1,0:T(8,128)S(1)}, f32[16,200]{1,0:T(8,128)S(1)}, u32[]{:S(2)}, u32[]{:S(2)}) collective-permute-start(f32[16,200]{1,0:T(8,128)S(1)} %reshape.963), channel_id=1, source_target_pairs={{4,0},{8,4},{12,8},{16,12},{20,16},{24,20},{28,24},{5,1},{9,5},{13... | collective-permute-start | bytes 38408 | tf_op jit(solution)/shard_map/ppermute | solution.py:15
  505.5 70.6 %collective-permute-start.12 = (f32[16,200]{1,0:T(8,128)S(1)}, f32[16,200]{1,0:T(8,128)S(1)}, u32[]{:S(2)}, u32[]{:S(2)}) collective-permute-start(f32[16,200]{1,0:T(8,128)S(1)} %reshape.967), channel_id=1, source_target_pairs={{0,4},{4,8},{8,12},{12,16},{16,20},{20,24},{24,28},{1,5},{5,9},{9,... | collective-permute-start | bytes 38408 | tf_op jit(solution)/shard_map/ppermute | solution.py:12
  506.8 69.3 %collective-permute-start.13 = (f32[16,200]{1,0:T(8,128)S(1)}, f32[16,200]{1,0:T(8,128)S(1)}, u32[]{:S(2)}, u32[]{:S(2)}) collective-permute-start(f32[16,200]{1,0:T(8,128)S(1)} %reshape.967), channel_id=1, source_target_pairs={{4,0},{8,4},{12,8},{16,12},{20,16},{24,20},{28,24},{5,1},{9,5},{13... | collective-permute-start | bytes 38408 | tf_op jit(solution)/shard_map/ppermute | solution.py:15
  590.0 70.4 %collective-permute-start.14 = (f32[16,200]{1,0:T(8,128)S(1)}, f32[16,200]{1,0:T(8,128)S(1)}, u32[]{:S(2)}, u32[]{:S(2)}) collective-permute-start(f32[16,200]{1,0:T(8,128)S(1)} %reshape.971), channel_id=1, source_target_pairs={{0,4},{4,8},{8,12},{12,16},{16,20},{20,24},{24,28},{1,5},{5,9},{9,... | collective-permute-start | bytes 38408 | tf_op jit(solution)/shard_map/ppermute | solution.py:12
  591.3 69.1 %collective-permute-start.15 = (f32[16,200]{1,0:T(8,128)S(1)}, f32[16,200]{1,0:T(8,128)S(1)}, u32[]{:S(2)}, u32[]{:S(2)}) collective-permute-start(f32[16,200]{1,0:T(8,128)S(1)} %reshape.971), channel_id=1, source_target_pairs={{4,0},{8,4},{12,8},{16,12},{20,16},{24,20},{28,24},{5,1},{9,5},{13... | collective-permute-start | bytes 38408 | tf_op jit(solution)/shard_map/ppermute | solution.py:15
  660.4 5.9 copy-start.9
  (4 other events, 12.0 us)
Sparse Core Ops, SparseCore 0:
  10.3 56.4 all-gather.23
where the time goes:
time: 676 us; the launch traced here: 674 us
  blocking collectives  521 us (77%)
  matrix products  37.2 us (6%)
  local copies, waits for them, and re-layouts  36.2 us (5%)
  waiting for transfers between devices  36.2 us (5%)
  starting transfers between devices  20.7 us (3%)
  between operations  14.2 us (2%)
  other arithmetic  8.53 us (1%)
    all_gather x7, blocking collectives, local(): lax.all_gather(spectrum[None, :], ('slab', 'clus'), axis=0, tiled=True)  460 us
    all_gather x7, blocking collectives, widen_step(): gathered = lax.all_gather(current, 'clus', axis=0, tiled=True)  50.6 us
    all_gather x1, waiting for transfers between devices, local(): lax.all_gather(own_hist[:, None, :], ('slab', 'clus'), axis=1, tiled=True)  33.6 us
    dot_general x8, matrix products, local(): jnp.einsum('cjuv,cjv->cu', near_blocks, blended, preferred_element_type=j...  29.9 us
  transfers between devices with their start and end apart: 17, of which 2 were waited for; matrix products, arithmetic and copies ran while one was open for 5% of the time, Pallas kernels for 0%

commit v1 on v0

v1 whole, which is shorter than its diff:
```python
import jax
import jax.numpy as jnp
from jax import lax
from jax.sharding import PartitionSpec as P


def local(
    incident,
    history,
    near_blocks,
    near_idx,
    near_cnt,
    near_lag,
    near_frac,
    inverses,
    rays,
    shift,
    far_idx,
    far_lag,
    trans,
):
    lag_count, local_count, unknowns = history.shape
    step_count = incident.shape[0]
    dir_count = rays.shape[1]
    slab_count = lax.axis_size("slab")
    clus_count = lax.axis_size("clus")
    group_count = slab_count * clus_count
    slab_index = lax.axis_index("slab")
    myself = slab_index * clus_count + lax.axis_index("clus")
    slot = local_count * unknowns
    half = group_count // 2
    order = [(i + half) % group_count for i in range(group_count)]
    group_slab = jnp.arange(group_count) // clus_count
    is_near = jnp.abs(group_slab - slab_index) <= 1

    gathered = lax.all_gather(history, "clus", axis=1, tiled=True)
    up = [(i, i + 1) for i in range(slab_count - 1)]
    down = [(b, a) for a, b in up]
    low = lax.ppermute(gathered, "slab", up)
    high = lax.ppermute(gathered, "slab", down)
    near_hist = jnp.concatenate([low, gathered, high], axis=1)
    slab_size = local_count * clus_count
    near_time = jnp.concatenate(
        [near_hist, jnp.zeros((step_count,) + near_hist.shape[1:], jnp.float32)], axis=0
    )
    near_local = near_idx - (slab_index - 1) * slab_size

    hist_rays = jnp.einsum(
        "cdu,tcu->tcd", rays, history.astype(jnp.bfloat16), preferred_element_type=jnp.float32
    )
    own_time = [jnp.sum(hist_rays[k] * shift, axis=0) for k in range(lag_count)]

    listed = far_idx == myself
    trans_wide = trans.astype(jnp.float32)
    weights = []
    for lag in range(1, lag_count + 1):
        chosen = (listed & (far_lag == lag))[..., None]
        weights.append(jnp.sum(jnp.where(chosen, trans_wide, 0.0), axis=1))

    live_slot = jnp.arange(near_idx.shape[1])[None, :] < near_cnt[:, None]
    near_weight = near_frac[..., None]
    outputs = []
    current = history[lag_count - 1]
    for step_index in range(step_count):
        outgoing = sum(
            weights[lag - 1] * own_time[step_index - lag + lag_count][None, :]
            for lag in range(1, lag_count + 1)
        )
        outgoing = jnp.pad(outgoing, ((0, 0), (0, slot - dir_count)))
        message = jnp.where(is_near[:, None], current.reshape(1, slot), outgoing)
        message = jnp.roll(message, -half, axis=0)
        arrived = lax.all_to_all(
            message, ("slab", "clus"), 0, 0, tiled=True, axis_index_groups=[order]
        )
        arrived = jnp.roll(arrived, half, axis=0)
        incoming = jnp.sum(jnp.where(is_near[:, None], 0.0, arrived[:, :dir_count]), axis=0)
        if step_index > 0:
            padded = jnp.pad(arrived, ((clus_count, clus_count), (0, 0)))
            fresh = lax.dynamic_slice_in_dim(
                padded, slab_index * clus_count, 3 * clus_count, axis=0
            ).reshape(3 * slab_size, unknowns)
            near_time = near_time.at[lag_count + step_index - 1].set(fresh)
        lag_slot = step_index - near_lag + lag_count
        first_lag = near_time[lag_slot, near_local]
        second = near_time[lag_slot - 1, near_local]
        blended = jnp.where(
            live_slot[..., None], (1.0 - near_weight) * first_lag + near_weight * second, 0.0
        ).astype(jnp.bfloat16)
        near_field = jnp.einsum(
            "cjuv,cjv->cu", near_blocks, blended, preferred_element_type=jnp.float32
        )
        inbound = (shift * incoming[None, :]).astype(jnp.bfloat16)
        far_field = jnp.einsum("cdu,cd->cu", rays, inbound, preferred_element_type=jnp.float32)
        right_side = (incident[step_index] - near_field - far_field).astype(jnp.bfloat16)
        current = jnp.einsum("cuv,cv->cu", inverses, right_side, preferred_element_type=jnp.float32)
        outputs.append(current)
        if step_index + 1 < step_count:
            ray_vals = jnp.einsum(
                "cdu,cu->cd", rays, current.astype(jnp.bfloat16), preferred_element_type=jnp.float32
            )
            own_time.append(jnp.sum(ray_vals * shift, axis=0))
    return jnp.stack(outputs, axis=0)


def solution(mesh):
    both = ("slab", "clus")
    in_specs = (
        P(None, both, None),
        P(None, both, None),
        P(both, None, None, None),
        P(both, None),
        P(both),
        P(both, None),
        P(both, None),
        P(both, None, None),
        P(both, None, None),
        P(both, None),
        P(),
        P(),
        P(),
    )
    out_specs = P(None, both, None)
    return jax.shard_map(local, mesh=mesh, in_specs=in_specs, out_specs=out_specs, check_vma=False)
```

time: 676 us -> 251 us (0.37)
  blocking collectives: 521 us -> 10.4 us
  local copies, waits for them, and re-layouts: 36.2 us -> 71.1 us
  other arithmetic: 8.53 us -> 31.2 us
  waiting for transfers between devices: 36.2 us -> 58.7 us
  between operations: 14.2 us -> 2.35 us
  starting transfers between devices: 20.7 us -> 31.6 us
    all_gather x15 -> x1, blocking collectives: 521 us -> 10.4 us  [local(): gathered = lax.all_gather(history, 'clus', axis=1, tiled=True)]
    all_to_all x0 -> x8, waiting for transfers between devices: none -> 58.7 us  [local(): lax.all_to_all(message, ('slab', 'clus'), 0, 0, tiled=True, axis_index_gr...]
    all_gather x1 -> x0, waiting for transfers between devices: 33.6 us -> none  [local(): lax.all_gather(own_hist[:, None, :], ('slab', 'clus'), axis=1, tiled=True)]
    all_to_all x0 -> x8, starting transfers between devices: none -> 26.6 us  [local(): lax.all_to_all(message, ('slab', 'clus'), 0, 0, tiled=True, axis_index_gr...]
    ppermute x16 -> x2, starting transfers between devices: 20.7 us -> 5.03 us  [the longest x1 3.74 us: local(): low = lax.ppermute(gathered, 'slab', up)]
    gather x8 -> x0, local copies, waits for them, and re-layouts: 10.2 us -> none  [local(): picked = spectra_all[step_index - lag_row + lag_count, idx_row]]
    broadcast_in_dim x0 -> x8, local copies, waits for them, and re-layouts: none -> 8.09 us  [local(): message = jnp.where(is_near[:, None], current.reshape(1, slot), outgoing)]
  transfers between devices with their start and end apart: 17 -> 10, of which waited for: 2 -> 8; matrix products, arithmetic and copies ran while one was open for 5% -> 6% of each run, Pallas kernels for 0% -> 0%
where the time goes in v1:
time: 251 us; the launch traced here: 249 us
  local copies, waits for them, and re-layouts  71.1 us (28%)
  waiting for transfers between devices  58.7 us (23%)
  matrix products  43.2 us (17%)
  starting transfers between devices  31.6 us (13%)
  other arithmetic  31.2 us (12%)
  blocking collectives  10.4 us (4%)
    all_to_all x8, waiting for transfers between devices, local(): lax.all_to_all(message, ('slab', 'clus'), 0, 0, tiled=True, axis_index_gr...  58.7 us
    dot_general x8, matrix products, local(): jnp.einsum('cjuv,cjv->cu', near_blocks, blended, preferred_element_type=j...  30 us
    all_to_all x8, starting transfers between devices, local(): lax.all_to_all(message, ('slab', 'clus'), 0, 0, tiled=True, axis_index_gr...  26.6 us
    gather x16, local copies, waits for them, and re-layouts, local(): second = near_time[lag_slot - 1, near_local]  11.6 us
    gather x16, local copies, waits for them, and re-layouts, local(): first_lag = near_time[lag_slot, near_local]  11.6 us
    all_gather x1, blocking collectives, local(): gathered = lax.all_gather(history, 'clus', axis=1, tiled=True)  10.4 us
    unnamed x298, local copies, waits for them, and re-layouts  8.72 us
    broadcast_in_dim x8, local copies, waits for them, and re-layouts, local(): message = jnp.where(is_near[:, None], current.reshape(1, slot), outgoing)  8.09 us
  transfers between devices with their start and end apart: 10, of which 8 were waited for; matrix products, arithmetic and copies ran while one was open for 6% of the time, Pallas kernels for 0%

profile of v1, /device:TPU:0, one launch (start us, length us, event | category | flops | bytes accessed | tf_op | source)
XLA Modules:
  0.0 248.7 jit_solution(727541481224242354)
XLA Ops:
  0.9 10.4 %all_gather.3 = f32[16,16,200]{2,0,1:T(8,128)S(1)} all-gather(f32[16,4,200]{2,0,1:T(8,128)S(1)} %copy.48), channel_id=1, replica_groups=mesh['slab'=8,'clus'=4] {'clus'}, dimensions={1}, use_global_device_ids=true | all-gather | bytes 256000 | tf_op jit(solution)/shard_map/all_gather | solution.py:36
  12.9 3.7 %collective-permute-start = (f32[16,16,200]{2,1,0:T(8,128)S(1)}, f32[16,16,200]{2,1,0:T(8,128)}, u32[]{:S(2)}, u32[]{:S(2)}) collective-permute-start(f32[16,16,200]{2,1,0:T(8,128)S(1)} %copy.49), channel_id=1, source_target_pairs={{0,4},{4,8},{8,12},{12,16},{16,20},{20,24},{24,28},{1,5},{5,9},{9,... | collective-permute-start | bytes 614408 | tf_op jit(solution)/shard_map/ppermute | solution.py:39
  25.7 4.2 %all-to-all-start = ((f32[32,1,800]{2,1,0:T(1,128)}), f32[32,1,800]{2,1,0:T(1,128)S(1)}, u32[]{:S(2)}, u32[]{:S(2)}) async-start(f32[32,1,800]{2,1,0:T(1,128)} %all_to_all.48), calls=%async_computation | async-start | bytes 229376 | tf_op jit(solution)/shard_map/all_to_all | solution.py:72
  30.8 7.3 %all-to-all-done = f32[32,1,800]{2,1,0:T(1,128)S(1)} async-done(((f32[32,1,800]{2,1,0:T(1,128)}), f32[32,1,800]{2,1,0:T(1,128)S(1)}, u32[]{:S(2)}, u32[]{:S(2)}) %all-to-all-start) | async-done | bytes 102432 | tf_op jit(solution)/shard_map/all_to_all | solution.py:72
  42.5 3.8 %fusion.53 = f32[4,1,200,1]{2,1,3,0:T(1,128)S(1)} fusion(bf16[4,12,200,200]{3,2,1,0:T(8,128)(2,1)} %param.29, bf16[4,12,200,1]{2,1,0,3:T(8,128)(2,1)S(1)} %fusion.55), kind=kOutput, calls=%fused_computation.166 | convolution fusion | flops 3840000 | bytes 3862400 | tf_op jit(solution)/shard_map/cjuv,cjv->cu/dot_general | solution.py:89
  52.5 3.3 %all-to-all-start.1 = ((f32[32,1,800]{2,1,0:T(1,128)}), f32[32,1,800]{2,1,0:T(1,128)}, u32[]{:S(2)}, u32[]{:S(2)}) async-start(f32[32,1,800]{2,1,0:T(1,128)} %copy.70), calls=%async_computation.1 | async-start | bytes 229376 | tf_op jit(solution)/shard_map/all_to_all | solution.py:72
  56.4 7.6 %all-to-all-done.1 = f32[32,1,800]{2,1,0:T(1,128)} async-done(((f32[32,1,800]{2,1,0:T(1,128)}), f32[32,1,800]{2,1,0:T(1,128)}, u32[]{:S(2)}, u32[]{:S(2)}) %all-to-all-start.1) | async-done | bytes 102432 | tf_op jit(solution)/shard_map/all_to_all | solution.py:72
  72.9 3.7 %fusion.51 = f32[4,1,200,1]{2,1,3,0:T(1,128)S(1)} fusion(bf16[4,12,200,200]{3,2,1,0:T(8,128)(2,1)} %param.29, bf16[4,12,200,1]{2,1,0,3:T(8,128)(2,1)S(1)} %fusion.56), kind=kOutput, calls=%fused_computation.164 | convolution fusion | flops 3840000 | bytes 3862400 | tf_op jit(solution)/shard_map/cjuv,cjv->cu/dot_general | solution.py:89
  83.0 3.3 %all-to-all-start.2 = ((f32[32,1,800]{2,1,0:T(1,128)}), f32[32,1,800]{2,1,0:T(1,128)}, u32[]{:S(2)}, u32[]{:S(2)}) async-start(f32[32,1,800]{2,1,0:T(1,128)} %copy.73), calls=%async_computation.2 | async-start | bytes 229376 | tf_op jit(solution)/shard_map/all_to_all | solution.py:72
  87.5 6.9 %all-to-all-done.2 = f32[32,1,800]{2,1,0:T(1,128)} async-done(((f32[32,1,800]{2,1,0:T(1,128)}), f32[32,1,800]{2,1,0:T(1,128)}, u32[]{:S(2)}, u32[]{:S(2)}) %all-to-all-start.2) | async-done | bytes 102432 | tf_op jit(solution)/shard_map/all_to_all | solution.py:72
  103.4 3.7 %fusion.49 = f32[4,1,200,1]{2,1,3,0:T(1,128)S(1)} fusion(bf16[4,12,200,200]{3,2,1,0:T(8,128)(2,1)} %param.29, bf16[4,12,200,1]{2,1,0,3:T(8,128)(2,1)S(1)} %fusion.57), kind=kOutput, calls=%fused_computation.162 | convolution fusion | flops 3840000 | bytes 3862400 | tf_op jit(solution)/shard_map/cjuv,cjv->cu/dot_general | solution.py:89
  113.5 3.4 %all-to-all-start.3 = ((f32[32,1,800]{2,1,0:T(1,128)}), f32[32,1,800]{2,1,0:T(1,128)}, u32[]{:S(2)}, u32[]{:S(2)}) async-start(f32[32,1,800]{2,1,0:T(1,128)} %copy.76), calls=%async_computation.3 | async-start | bytes 229376 | tf_op jit(solution)/shard_map/all_to_all | solution.py:72
  118.2 6.7 %all-to-all-done.3 = f32[32,1,800]{2,1,0:T(1,128)} async-done(((f32[32,1,800]{2,1,0:T(1,128)}), f32[32,1,800]{2,1,0:T(1,128)}, u32[]{:S(2)}, u32[]{:S(2)}) %all-to-all-start.3) | async-done | bytes 102432 | tf_op jit(solution)/shard_map/all_to_all | solution.py:72
  133.8 3.7 %fusion.47 = f32[4,1,200,1]{2,1,3,0:T(1,128)S(1)} fusion(bf16[4,12,200,200]{3,2,1,0:T(8,128)(2,1)} %param.29, bf16[4,12,200,1]{2,1,0,3:T(8,128)(2,1)S(1)} %fusion.58), kind=kOutput, calls=%fused_computation.160 | convolution fusion | flops 3840000 | bytes 3862400 | tf_op jit(solution)/shard_map/cjuv,cjv->cu/dot_general | solution.py:89
  143.5 3.3 %all-to-all-start.4 = ((f32[32,1,800]{2,1,0:T(1,128)}), f32[32,1,800]{2,1,0:T(1,128)}, u32[]{:S(2)}, u32[]{:S(2)}) async-start(f32[32,1,800]{2,1,0:T(1,128)} %copy.79), calls=%async_computation.4 | async-start | bytes 229376 | tf_op jit(solution)/shard_map/all_to_all | solution.py:72
  147.4 7.6 %all-to-all-done.4 = f32[32,1,800]{2,1,0:T(1,128)} async-done(((f32[32,1,800]{2,1,0:T(1,128)}), f32[32,1,800]{2,1,0:T(1,128)}, u32[]{:S(2)}, u32[]{:S(2)}) %all-to-all-start.4) | async-done | bytes 102432 | tf_op jit(solution)/shard_map/all_to_all | solution.py:72
  163.8 3.7 %fusion.45 = f32[4,1,200,1]{2,1,3,0:T(1,128)S(1)} fusion(bf16[4,12,200,200]{3,2,1,0:T(8,128)(2,1)} %param.29, bf16[4,12,200,1]{2,1,0,3:T(8,128)(2,1)S(1)} %fusion.59), kind=kOutput, calls=%fused_computation.158 | convolution fusion | flops 3840000 | bytes 3862400 | tf_op jit(solution)/shard_map/cjuv,cjv->cu/dot_general | solution.py:89
  172.1 3.3 %all-to-all-start.5 = ((f32[32,1,800]{2,1,0:T(1,128)}), f32[32,1,800]{2,1,0:T(1,128)}, u32[]{:S(2)}, u32[]{:S(2)}) async-start(f32[32,1,800]{2,1,0:T(1,128)} %copy.82), calls=%async_computation.5 | async-start | bytes 229376 | tf_op jit(solution)/shard_map/all_to_all | solution.py:72
  176.0 7.6 %all-to-all-done.5 = f32[32,1,800]{2,1,0:T(1,128)} async-done(((f32[32,1,800]{2,1,0:T(1,128)}), f32[32,1,800]{2,1,0:T(1,128)}, u32[]{:S(2)}, u32[]{:S(2)}) %all-to-all-start.5) | async-done | bytes 102432 | tf_op jit(solution)/shard_map/all_to_all | solution.py:72
  192.5 3.7 %fusion.43 = f32[4,1,200,1]{2,1,3,0:T(1,128)S(1)} fusion(bf16[4,12,200,200]{3,2,1,0:T(8,128)(2,1)} %param.29, bf16[4,12,200,1]{2,1,0,3:T(8,128)(2,1)S(1)} %fusion.60), kind=kOutput, calls=%fused_computation.156 | convolution fusion | flops 3840000 | bytes 3862400 | tf_op jit(solution)/shard_map/cjuv,cjv->cu/dot_general | solution.py:89
  204.7 7.6 %all-to-all-done.6 = f32[32,1,800]{2,1,0:T(1,128)} async-done(((f32[32,1,800]{2,1,0:T(1,128)}), f32[32,1,800]{2,1,0:T(1,128)}, u32[]{:S(2)}, u32[]{:S(2)}) %all-to-all-start.6) | async-done | bytes 102432 | tf_op jit(solution)/shard_map/all_to_all | solution.py:72
  221.2 3.7 %fusion.41 = f32[4,1,200,1]{2,1,3,0:T(1,128)S(1)} fusion(bf16[4,12,200,200]{3,2,1,0:T(8,128)(2,1)} %param.29, bf16[4,12,200,1]{2,1,0,3:T(8,128)(2,1)S(1)} %fusion.61), kind=kOutput, calls=%fused_computation.154 | convolution fusion | flops 3840000 | bytes 3862400 | tf_op jit(solution)/shard_map/cjuv,cjv->cu/dot_general | solution.py:89
  233.1 7.6 %all-to-all-done.7 = f32[32,1,800]{2,1,0:T(1,128)S(1)} async-done(((f32[32,1,800]{2,1,0:T(1,128)}), f32[32,1,800]{2,1,0:T(1,128)S(1)}, u32[]{:S(2)}, u32[]{:S(2)}) %all-to-all-start.7) | async-done | bytes 102432 | tf_op jit(solution)/shard_map/all_to_all | solution.py:72
  243.4 3.7 %fusion.39 = f32[4,1,200,1]{2,1,3,0:T(1,128)S(1)} fusion(bf16[4,12,200,200]{3,2,1,0:T(8,128)(2,1)} %param.29, bf16[4,12,200,1]{2,1,0,3:T(8,128)(2,1)S(1)} %fusion.62), kind=kOutput, calls=%fused_computation.152 | convolution fusion | flops 3840000 | bytes 3862400 | tf_op jit(solution)/shard_map/cjuv,cjv->cu/dot_general | solution.py:89
  (536 shorter events, 122.7 us)
Async XLA Ops:
  0.0 21.2 %copy-start = (bf16[4,512,200]{1,2,0:T(8,128)(2,1)S(1)}, bf16[4,512,200]{1,2,0:T(8,128)(2,1)}, u32[]{:S(2)}) copy-start(bf16[4,512,200]{1,2,0:T(8,128)(2,1)} %param.35) | copy-start | bytes 2457604
  11.6 27.0 %collective-permute-start.1 = (f32[16,16,200]{2,1,0:T(8,128)S(1)}, f32[16,16,200]{2,1,0:T(8,128)S(1)}, u32[]{:S(2)}, u32[]{:S(2)}) collective-permute-start(f32[16,16,200]{2,1,0:T(8,128)S(1)} %copy.49), channel_id=1, source_target_pairs={{4,0},{8,4},{12,8},{16,12},{20,16},{24,20},{28,24},{5,1},{9,5},{13... | collective-permute-start | bytes 614408 | tf_op jit(solution)/shard_map/ppermute | solution.py:40
  12.9 26.4 %collective-permute-start = (f32[16,16,200]{2,1,0:T(8,128)S(1)}, f32[16,16,200]{2,1,0:T(8,128)}, u32[]{:S(2)}, u32[]{:S(2)}) collective-permute-start(f32[16,16,200]{2,1,0:T(8,128)S(1)} %copy.49), channel_id=1, source_target_pairs={{0,4},{4,8},{8,12},{12,16},{16,20},{20,24},{24,28},{1,5},{5,9},{9,... | collective-permute-start | bytes 614408 | tf_op jit(solution)/shard_map/ppermute | solution.py:39
  18.2 46.7 %copy-start.73 = (pred[32]{0:T(512)(128)(4,1)}, pred[32]{0:T(512)(128)(4,1)S(1)}, u32[]{:S(2)}) copy-start(pred[32]{0:T(512)(128)(4,1)S(1)} %fusion.188) | copy-start | bytes 100
  21.7 29.0 %copy-start.5 = (f32[512]{0:T(512)}, f32[512]{0:T(512)S(1)}, u32[]{:S(2)}) copy-start(f32[512]{0:T(512)S(1)} %get-tuple-element.105) | copy-start | bytes 6148
  21.7 29.0 %copy-start.7 = (f32[512]{0:T(512)}, f32[512]{0:T(512)S(1)}, u32[]{:S(2)}) copy-start(f32[512]{0:T(512)S(1)} %get-tuple-element.113) | copy-start | bytes 6148
  21.7 29.0 %copy-start.10 = (f32[512]{0:T(512)}, f32[512]{0:T(512)S(1)}, u32[]{:S(2)}) copy-start(f32[512]{0:T(512)S(1)} %get-tuple-element.114) | copy-start | bytes 6148
  21.7 29.0 %copy-start.14 = (f32[512]{0:T(512)}, f32[512]{0:T(512)S(1)}, u32[]{:S(2)}) copy-start(f32[512]{0:T(512)S(1)} %get-tuple-element.115) | copy-start | bytes 6148
  21.7 29.0 %copy-start.19 = (f32[512]{0:T(512)}, f32[512]{0:T(512)S(1)}, u32[]{:S(2)}) copy-start(f32[512]{0:T(512)S(1)} %get-tuple-element.116) | copy-start | bytes 6148
  21.7 29.0 %copy-start.25 = (f32[512]{0:T(512)}, f32[512]{0:T(512)S(1)}, u32[]{:S(2)}) copy-start(f32[512]{0:T(512)S(1)} %get-tuple-element.117) | copy-start | bytes 6148
  21.7 29.0 %copy-start.32 = (f32[512]{0:T(512)}, f32[512]{0:T(512)S(1)}, u32[]{:S(2)}) copy-start(f32[512]{0:T(512)S(1)} %get-tuple-element.118) | copy-start | bytes 6148
  21.7 29.0 %copy-start.39 = (f32[512]{0:T(512)}, f32[512]{0:T(512)S(1)}, u32[]{:S(2)}) copy-start(f32[512]{0:T(512)S(1)} %get-tuple-element.119) | copy-start | bytes 6148
  21.7 29.0 %copy-start.46 = (f32[512]{0:T(512)}, f32[512]{0:T(512)S(1)}, u32[]{:S(2)}) copy-start(f32[512]{0:T(512)S(1)} %get-tuple-element.120) | copy-start | bytes 6148
  21.8 29.0 %copy-start.67 = (f32[512]{0:T(512)}, f32[512]{0:T(512)S(1)}, u32[]{:S(2)}) copy-start(f32[512]{0:T(512)S(1)} %get-tuple-element.112) | copy-start | bytes 6148
  21.8 29.0 %copy-start.87 = (f32[512]{0:T(512)}, f32[512]{0:T(512)S(1)}, u32[]{:S(2)}) copy-start(f32[512]{0:T(512)S(1)} %get-tuple-element.111) | copy-start | bytes 6148
  21.8 29.0 %copy-start.98 = (f32[512]{0:T(512)}, f32[512]{0:T(512)S(1)}, u32[]{:S(2)}) copy-start(f32[512]{0:T(512)S(1)} %get-tuple-element.110) | copy-start | bytes 6148
  25.7 12.4 %all-to-all-start = ((f32[32,1,800]{2,1,0:T(1,128)}), f32[32,1,800]{2,1,0:T(1,128)S(1)}, u32[]{:S(2)}, u32[]{:S(2)}) async-start(f32[32,1,800]{2,1,0:T(1,128)} %all_to_all.48), calls=%async_computation | async-start | bytes 229376 | tf_op jit(solution)/shard_map/all_to_all | solution.py:72
  52.5 11.4 %all-to-all-start.1 = ((f32[32,1,800]{2,1,0:T(1,128)}), f32[32,1,800]{2,1,0:T(1,128)}, u32[]{:S(2)}, u32[]{:S(2)}) async-start(f32[32,1,800]{2,1,0:T(1,128)} %copy.70), calls=%async_computation.1 | async-start | bytes 229376 | tf_op jit(solution)/shard_map/all_to_all | solution.py:72
  83.0 11.4 %all-to-all-start.2 = ((f32[32,1,800]{2,1,0:T(1,128)}), f32[32,1,800]{2,1,0:T(1,128)}, u32[]{:S(2)}, u32[]{:S(2)}) async-start(f32[32,1,800]{2,1,0:T(1,128)} %copy.73), calls=%async_computation.2 | async-start | bytes 229376 | tf_op jit(solution)/shard_map/all_to_all | solution.py:72
  113.5 11.4 %all-to-all-start.3 = ((f32[32,1,800]{2,1,0:T(1,128)}), f32[32,1,800]{2,1,0:T(1,128)}, u32[]{:S(2)}, u32[]{:S(2)}) async-start(f32[32,1,800]{2,1,0:T(1,128)} %copy.76), calls=%async_computation.3 | async-start | bytes 229376 | tf_op jit(solution)/shard_map/all_to_all | solution.py:72
  143.5 11.4 %all-to-all-start.4 = ((f32[32,1,800]{2,1,0:T(1,128)}), f32[32,1,800]{2,1,0:T(1,128)}, u32[]{:S(2)}, u32[]{:S(2)}) async-start(f32[32,1,800]{2,1,0:T(1,128)} %copy.79), calls=%async_computation.4 | async-start | bytes 229376 | tf_op jit(solution)/shard_map/all_to_all | solution.py:72
  172.1 11.4 %all-to-all-start.5 = ((f32[32,1,800]{2,1,0:T(1,128)}), f32[32,1,800]{2,1,0:T(1,128)}, u32[]{:S(2)}, u32[]{:S(2)}) async-start(f32[32,1,800]{2,1,0:T(1,128)} %copy.82), calls=%async_computation.5 | async-start | bytes 229376 | tf_op jit(solution)/shard_map/all_to_all | solution.py:72
  200.8 11.4 %all-to-all-start.6 = ((f32[32,1,800]{2,1,0:T(1,128)}), f32[32,1,800]{2,1,0:T(1,128)}, u32[]{:S(2)}, u32[]{:S(2)}) async-start(f32[32,1,800]{2,1,0:T(1,128)} %copy.85), calls=%async_computation.6 | async-start | bytes 229376 | tf_op jit(solution)/shard_map/all_to_all | solution.py:72
  229.9 10.8 %all-to-all-start.7 = ((f32[32,1,800]{2,1,0:T(1,128)}), f32[32,1,800]{2,1,0:T(1,128)S(1)}, u32[]{:S(2)}, u32[]{:S(2)}) async-start(f32[32,1,800]{2,1,0:T(1,128)} %copy.88), calls=%async_computation.7 | async-start | bytes 229376 | tf_op jit(solution)/shard_map/all_to_all | solution.py:72
  (124 other events, 531.5 us)

commit v2 on v1

v2 whole, which is shorter than its diff:
```python
import functools

import jax
import jax.numpy as jnp
from jax import lax
from jax.experimental import pallas as pl
from jax.experimental.pallas import tpu as pltpu
from jax.sharding import PartitionSpec as P

LANE = 128
PACK = 16
KEPT = 6
CHUNK = 3
VMEM_LIMIT = 24 * 1024 * 1024
HBM = pl.BlockSpec(memory_space=pltpu.HBM)
ANY = pl.BlockSpec(memory_space=pl.ANY)
VMEM = pl.BlockSpec(memory_space=pltpu.VMEM)
SMEM = pl.BlockSpec(memory_space=pltpu.SMEM)


def rows_of(wide, count):
    return jnp.concatenate([wide[:, r * LANE : (r + 1) * LANE] for r in range(count)], axis=0)


def padded(wide, width):
    return jnp.concatenate(
        [wide, jnp.zeros((wide.shape[0], width - wide.shape[1]), wide.dtype)], axis=1
    )


def dot(left, right):
    return jnp.dot(left, right, preferred_element_type=jnp.float32)


def dot_t(left, right):
    return lax.dot_general(
        left, right, (((1,), (1,)), ((), ())), preferred_element_type=jnp.float32
    )


def pack_kernel(history, packed):
    lags, clusters, unknowns = history.shape
    halves = packed.shape[1] // clusters
    for half in range(halves):
        low, high = half * LANE, min(unknowns, (half + 1) * LANE)
        part = history[:, :, low:high]
        if high - low < LANE:
            part = jnp.concatenate(
                [part, jnp.zeros((lags, clusters, LANE - (high - low)), jnp.float32)], axis=2
            )
        packed[:, half * clusters : (half + 1) * clusters, :] = part


def in_hbm(*arrays):
    return [pltpu.with_memory_space_constraint(array, pltpu.HBM) for array in arrays]


def in_vmem(*arrays):
    return [pltpu.with_memory_space_constraint(array, pltpu.VMEM) for array in arrays]


def start_all(pairs, sems):
    copies = []
    for number, (source, target) in enumerate(pairs):
        copy = pltpu.make_async_copy(source, target, sems.at[number])
        copy.start()
        copies.append(copy)
    return copies


def wait_all(copies):
    for copy in copies:
        copy.wait()


def any_of(flags):
    found = flags[0]
    for flag in flags[1:]:
        found = found | flag
    return found


def row_of(cluster_number, clusters, halves):
    place = lax.rem(cluster_number, clusters)
    return (cluster_number - place) * halves + place


def begin_kernel(
    clus_count,
    rays_in, history_in, shift_in, trans_in, far_idx_in, far_lag_in, near_idx_in, near_cnt_in,
    near_lag_in, near_frac_in, blocks,
    spectra, message, weights, fresh_weights, kept, kept_weight, near_plan, old_plan,
    rays, history, shift, trans, far_idx, far_lag, near_idx, near_cnt, near_lag, near_frac, sem,
    sems,
):
    small = start_all(
        (
            (near_idx_in, near_idx), (near_cnt_in, near_cnt), (near_lag_in, near_lag),
            (near_frac_in, near_frac), (far_idx_in, far_idx), (far_lag_in, far_lag),
        ),
        sems,
    )
    large = start_all(
        ((history_in, history), (rays_in, rays), (shift_in, shift), (trans_in, trans)),
        sems.at[pl.ds(6, 4)],
    )
    lags, clusters, unknowns = history.shape
    dir_rows = spectra.shape[1]
    entries, groups = far_idx.shape
    slots = near_idx.shape[1]
    halves = message.shape[1] // clusters
    myself = lax.axis_index("slab") * clus_count + lax.axis_index("clus")

    def kept_copy(place, entry):
        source = blocks.at[lax.div(entry, slots), lax.rem(entry, slots)]
        return pltpu.make_async_copy(source, kept.at[place], sem)

    for place in range(3 * KEPT + 1):
        near_plan[place] = 0
    kept_weight[...] = jnp.zeros(kept_weight.shape, jnp.float32)
    message[...] = jnp.zeros(message.shape, jnp.float32)
    fresh_weights[...] = jnp.zeros(fresh_weights.shape, jnp.float32)
    wait_all(small)
    near_plan[0] = 0
    for cluster in range(clusters):
        fresh = [
            (slot < near_cnt[cluster]) & (near_lag[cluster, slot] == 1) for slot in range(slots)
        ]

        @pl.when(any_of(fresh))
        def _(cluster=cluster, fresh=fresh):
            for slot in range(slots):

                @pl.when(fresh[slot])
                def _(slot=slot):
                    count = near_plan[0]
                    entry = jnp.int32(cluster * slots + slot)
                    near_plan[3 * count + 1] = entry
                    near_plan[3 * count + 2] = jnp.int32(cluster)
                    near_plan[3 * count + 3] = row_of(near_idx[cluster, slot], clusters, halves)
                    row = jnp.zeros((1, kept_weight.shape[1]), jnp.float32)
                    kept_weight[pl.ds(count, 1), :] = row + (1.0 - near_frac[cluster, slot])
                    near_plan[0] = count + 1

                    @pl.when(count < KEPT)
                    def _():
                        kept_copy(count, entry).start()

    wait_all(large)
    total = jnp.zeros((lags, dir_rows * LANE), jnp.float32)
    for cluster in range(clusters):
        past = history[:, cluster, :].astype(jnp.bfloat16)
        total += dot(past, rays[cluster]) * shift[cluster : cluster + 1, :]
    for lag in range(lags):
        spectra[lag] = rows_of(total[lag : lag + 1], dir_rows)

    def one(group, counts):
        listed = [far_idx[column, group] == myself for column in range(entries)]

        def add(counts):
            place, old_count = counts
            for column in range(entries):
                lag = far_lag[column, group]

                @pl.when(listed[column])
                def _(place=place, lag=lag, column=column, old_count=old_count):
                    row = trans[group, column : column + 1, :].astype(jnp.float32)
                    weight = rows_of(row, dir_rows)
                    weights[place] = weight
                    message[group, :dir_rows, :] += weight * spectra[lags - lag]

                    @pl.when(lag == 1)
                    def _():
                        fresh_weights[group] += weight

                    @pl.when(lag > 1)
                    def _():
                        old_plan[3 * old_count + 1] = group
                        old_plan[3 * old_count + 2] = place
                        old_plan[3 * old_count + 3] = lag

                place = place + jnp.where(listed[column], 1, 0)
                old_count = old_count + jnp.where(listed[column] & (lag > 1), 1, 0)
            return place, old_count

        return lax.cond(any_of(listed), add, lambda counts: counts, counts)

    counts = lax.fori_loop(0, groups, one, (jnp.int32(0), jnp.int32(0)))
    old_plan[0] = counts[1]

    def finish(place, carry):
        kept_copy(place, near_plan[3 * place + 1]).wait()
        return carry

    lax.fori_loop(0, jnp.minimum(near_plan[0], KEPT), finish, 0)


def near_kernel(step, last, clus_count, lags, *refs):
    (
        near_idx_in, near_cnt_in, near_lag_in, near_frac_in, old_plan_in, incident_in, weights,
        past_spectra, blocks,
    ) = refs[:9]
    newer, refs = refs[9 : 9 + step], refs[9 + step :]
    if step:
        table_in, base, blended, known = refs[:4]
        refs = refs[4:]
    else:
        mid, core_swap, chip_swap, base, blended, known, table_out = refs[:7]
        refs = refs[7:]
    (
        table, held, tall, field, spectra, incident, near_idx, near_cnt, near_lag, near_frac,
        old_plan, sems, more_sems, out_sem,
    ) = refs
    clusters, slots = near_idx.shape
    unknowns = incident.shape[1]
    halves = tall.shape[2] // LANE
    side_rows = table.shape[1] // 3
    slab = lax.axis_index("slab")
    now = lags + max(step - 1, 0)
    chunks = [(first, min(CHUNK, slots - first)) for first in range(0, slots, CHUNK)]

    def block_copy(cluster, number):
        first, size = chunks[number]
        return pltpu.make_async_copy(
            blocks.at[cluster, pl.ds(first, size)],
            held.at[pl.ds(cluster * slots + first, size)],
            sems.at[cluster * len(chunks) + number],
        )

    if step:
        wide_pairs = [(table_in.at[pl.ds(0, now)], table.at[pl.ds(0, now)])]
    else:
        odd = lax.rem(slab, 2)
        wide_pairs = []
        for source, side in ((mid, 1), (core_swap, 2 - 2 * odd), (chip_swap, 2 * odd)):
            start = pl.multiple_of(side * side_rows, side_rows)
            wide_pairs.append((source, table.at[pl.ds(0, lags), pl.ds(start, side_rows)]))
    small = start_all(
        (
            (near_cnt_in, near_cnt), (near_idx_in, near_idx), (near_lag_in, near_lag),
            (near_frac_in, near_frac),
        ),
        more_sems,
    )
    wide = start_all(wide_pairs, more_sems.at[pl.ds(4, 3)])
    pairs = [(incident_in.at[step], incident)]
    if not last:
        pairs.append((old_plan_in, old_plan))
    others = start_all(pairs, more_sems.at[pl.ds(7, 2)])
    for cluster in range(clusters):
        block_copy(cluster, 0).start()
    tall[...] = jnp.zeros(tall.shape, jnp.float32)
    if not last:
        spectra[:lags] = past_spectra[...]
        for back, source in enumerate(newer):
            spectra[lags + back] = source[...]
        known[...] = jnp.zeros(known.shape, jnp.float32)
    wait_all(small)
    most = near_cnt[0]
    for cluster in range(1, clusters):
        most = jnp.maximum(most, near_cnt[cluster])
    for number in range(1, len(chunks)):
        for cluster in range(clusters):

            @pl.when(chunks[number][0] < near_cnt[cluster])
            def _():
                block_copy(cluster, number).start()

    wait_all(wide)
    if not step:
        keep = pltpu.make_async_copy(
            table.at[pl.ds(0, lags)], table_out.at[pl.ds(0, lags)], out_sem
        )
        keep.start()
    first_row = (slab - 1) * side_rows
    newest = lags + step - 2 if step else lags - 1
    for cluster in range(clusters):
        for slot in range(slots):
            row = row_of(near_idx[cluster, slot], clusters, halves) - first_row
            lag_slot = step - near_lag[cluster, slot] + lags
            frac = near_frac[cluster, slot]
            weight = jnp.where(lag_slot > newest, 0.0, 1.0 - frac)
            first_slot = jnp.minimum(lag_slot, newest)
            for half in range(halves):
                at = pl.ds(row + half * clusters, 1)
                tall[cluster, slot : slot + 1, half * LANE : (half + 1) * LANE] = (
                    weight * table[first_slot, at, :] + frac * table[lag_slot - 1, at, :]
                )
    for cluster in range(clusters):
        blended[cluster * slots : (cluster + 1) * slots, :] = tall[cluster, :slots, :]
    wait_all(others)
    if not last:

        def one(place, carry):
            before, total = carry
            group = old_plan[3 * place + 1]
            slot = step + 1 + lags - old_plan[3 * place + 3]
            term = weights[old_plan[3 * place + 2]] * spectra[slot]
            total = jnp.where(group == before, total, 0.0) + term
            known[group] = total
            return group, total

        lax.fori_loop(
            0, old_plan[0], one, (jnp.int32(-1), jnp.zeros(known.shape[1:], jnp.float32))
        )
    which = lax.broadcasted_iota(jnp.int32, (tall.shape[1], unknowns), 0)

    def part(number, cluster):
        first, size = chunks[number]
        values = tall[cluster].astype(jnp.bfloat16)[:, :unknowns]
        sums = jnp.zeros((tall.shape[1], unknowns), jnp.float32)
        for slot in range(first, first + size):
            counts = slot < near_cnt[cluster]
            if step:
                counts = counts & (near_lag[cluster, slot] > 1)
            product = dot_t(values, held[cluster * slots + slot])
            sums = jnp.where(which == jnp.where(counts, slot, -1), product, sums)
        return sums

    for cluster in range(clusters):
        block_copy(cluster, 0).wait()
    for cluster in range(clusters):
        field[cluster] = part(0, cluster)
    for number in range(1, len(chunks)):

        @pl.when(chunks[number][0] < most)
        def _():
            for cluster in range(clusters):

                @pl.when(chunks[number][0] < near_cnt[cluster])
                def _():
                    block_copy(cluster, number).wait()

            for cluster in range(clusters):
                field[cluster] += part(number, cluster)

    for cluster in range(clusters):
        total = jnp.sum(field[cluster], axis=0, keepdims=True)
        base[cluster : cluster + 1, :] = incident[cluster : cluster + 1, :] - total
    if not step:
        keep.wait()


def march_kernel(step, last, clus_count, slab_count, lags, *refs):
    (
        near_plan_in, base, blended, known, kept, kept_weight, rays, inverses, shift,
        fresh_weights, arrived, blocks,
    ) = refs[:12]
    if last:
        _, output = refs[12:14]
        refs = refs[14:]
    elif step:
        _, _, output, table, spectrum, message = refs[12:18]
        refs = refs[18:]
    else:
        output, spectrum, message = refs[12:15]
        refs = refs[15:]
    near_plan, current, values, extra, field, sem, sems = refs
    clusters, unknowns = base.shape
    slots = blocks.shape[1]
    groups, dir_rows = fresh_weights.shape[:2]
    rows_each = arrived.shape[0] // groups
    halves = rows_each // clusters
    side_rows = clus_count * rows_each
    slab = lax.axis_index("slab")
    which = lax.broadcasted_iota(jnp.int32, (clusters, unknowns), 0)
    plan_copy = pltpu.make_async_copy(near_plan_in, near_plan, sems.at[0])
    plan_copy.start()
    kept_copies = []
    if step and not last:
        for side in range(3):
            other = jnp.clip(slab + (side - 1), 0, slab_count - 1)
            copy = pltpu.make_async_copy(
                arrived.at[pl.ds(pl.multiple_of(other * side_rows, side_rows), side_rows)],
                table.at[lags + step - 1, pl.ds(side * side_rows, side_rows)],
                sems.at[1 + side],
            )
            copy.start()
            kept_copies.append(copy)

    def is_near(group):
        return jnp.abs(group // clus_count - slab) <= 1

    sums = [jnp.zeros((dir_rows, LANE), jnp.float32) for _ in range(4)]
    for group in range(groups):
        first = group * rows_each
        sums[group % 4] += jnp.where(is_near(group), 0.0, arrived[first : first + dir_rows, :])
    incoming = (sums[0] + sums[1]) + (sums[2] + sums[3])
    row_in = jnp.concatenate([incoming[r : r + 1] for r in range(dir_rows)], axis=1)
    inbound = (shift[...] * row_in).astype(jnp.bfloat16)
    far = jnp.zeros((clusters, unknowns), jnp.float32)
    for cluster in range(clusters):
        far = jnp.where(which == cluster, dot_t(inbound, rays[cluster]), far)
    remaining = base[...] - far

    def fresh_row(place):
        entry, row = near_plan[3 * place + 1], near_plan[3 * place + 3]
        newest = jnp.concatenate(
            [arrived[pl.ds(row + half * clusters, 1), :] for half in range(halves)], axis=1
        )
        return blended[pl.ds(entry, 1), :] + kept_weight[pl.ds(place, 1), :] * newest

    plan_copy.wait()
    if step:
        count = near_plan[0]
        values[...] = jnp.zeros(values.shape, jnp.float32)
        for place in range(KEPT):
            values[place : place + 1, :] = fresh_row(place)
        rows = values[...].astype(jnp.bfloat16)[:, :unknowns]
        for place in range(KEPT):
            product = dot_t(rows, kept[place])[place : place + 1]
            cluster = jnp.where(place < count, near_plan[3 * place + 2], -1)
            remaining = remaining - jnp.where(which == cluster, product, 0.0)
        field[...] = remaining

        @pl.when(count > KEPT)
        def _():
            def one(place, carry):
                entry = near_plan[3 * place + 1]
                cluster = near_plan[3 * place + 2]
                source = blocks.at[cluster, entry - cluster * slots]
                copy = pltpu.make_async_copy(source, extra, sem)
                copy.start()
                row = jnp.broadcast_to(fresh_row(place), (8, halves * LANE))
                copy.wait()
                product = dot_t(row.astype(jnp.bfloat16)[:, :unknowns], extra[...])
                field[pl.ds(cluster, 1), :] -= product[:1]
                return carry

            lax.fori_loop(KEPT, count, one, 0)

        remaining = field[...]

    right_side = remaining.astype(jnp.bfloat16)
    solved = jnp.zeros((clusters, unknowns), jnp.float32)
    for cluster in range(clusters):
        solved = jnp.where(which == cluster, dot_t(right_side, inverses[cluster]), solved)
    current[...] = solved
    out_copy = pltpu.make_async_copy(current, output.at[step], sems.at[4])
    out_copy.start()
    if not last:
        own = rows_of(padded(solved, halves * LANE), halves)
        rounded = solved.astype(jnp.bfloat16)
        which_dir = lax.broadcasted_iota(jnp.int32, (clusters, dir_rows * LANE), 0)
        ray_vals = jnp.zeros((clusters, dir_rows * LANE), jnp.float32)
        for cluster in range(clusters):
            ray_vals = jnp.where(which_dir == cluster, dot(rounded, rays[cluster]), ray_vals)
        newest = rows_of(jnp.sum(ray_vals * shift[...], axis=0, keepdims=True), dir_rows)
        spectrum[...] = newest
        for group in range(groups):
            far_sum = known[group] + fresh_weights[group] * newest
            message[group, :dir_rows, :] = jnp.where(is_near(group), own[:dir_rows], far_sum)
            message[group, dir_rows:, :] = own[dir_rows:]
    out_copy.wait()
    wait_all(kept_copies)


def exchange(block, axis, bit):
    count = lax.axis_size(axis)
    return lax.ppermute(block, axis, [(i, i ^ bit) for i in range(count)])


def local(
    incident,
    history,
    near_blocks,
    near_idx,
    near_cnt,
    near_lag,
    near_frac,
    inverses,
    rays,
    shift,
    far_idx,
    far_lag,
    trans,
):
    f32, i32, bf16 = jnp.float32, jnp.int32, jnp.bfloat16
    shaped = jax.ShapeDtypeStruct
    lags, clusters, unknowns = history.shape
    steps = incident.shape[0]
    slots = near_idx.shape[1]
    groups, entries, dirs = trans.shape
    dir_rows = dirs // LANE
    halves = pl.cdiv(unknowns, LANE)
    msg_rows = halves * clusters
    wide = halves * LANE
    near_entries = clusters * slots
    far_entries = groups * entries
    slab_count = lax.axis_size("slab")
    clus_count = lax.axis_size("clus")
    clus_index = lax.axis_index("clus")
    params = pltpu.CompilerParams(vmem_limit_bytes=VMEM_LIMIT)
    rays = jnp.swapaxes(rays, 1, 2)

    packed = pl.pallas_call(
        pack_kernel,
        out_shape=shaped((lags, msg_rows, LANE), f32),
        in_specs=[VMEM],
        out_specs=VMEM,
        compiler_params=params,
        name="pack_history",
    )(*in_hbm(history))
    pieces = [packed] + [exchange(packed, "clus", bit) for bit in range(1, clus_count)]
    stacked = jnp.stack(pieces, axis=0)
    mid = jnp.stack(
        [lax.dynamic_index_in_dim(stacked, clus_index ^ c, 0, False) for c in range(clus_count)],
        axis=1,
    )

    smem_lists = [
        pltpu.SMEM((clusters, slots), i32),
        pltpu.SMEM((clusters,), i32),
        pltpu.SMEM((clusters, slots), i32),
        pltpu.SMEM((clusters, slots), f32),
    ]
    dma = pltpu.SemaphoreType.DMA
    near_lists = in_hbm(near_idx, near_cnt, near_lag, near_frac)
    (blocks,) = in_hbm(near_blocks)
    spectra, message, weights, fresh_weights, kept, kept_weight, near_plan, old_plan = (
        pl.pallas_call(
            functools.partial(begin_kernel, clus_count),
            out_shape=(
                shaped((lags, dir_rows, LANE), f32),
                shaped((groups, msg_rows, LANE), f32),
                shaped((far_entries, dir_rows, LANE), f32),
                shaped((groups, dir_rows, LANE), f32),
                shaped((KEPT, unknowns, unknowns), bf16),
                shaped((near_entries, wide), f32),
                shaped((3 * near_entries + 4,), i32),
                shaped((3 * far_entries + 4,), i32),
            ),
            in_specs=[HBM] * 11,
            out_specs=[VMEM] * 6 + [SMEM] * 2,
            scratch_shapes=[
                pltpu.VMEM(rays.shape, bf16),
                pltpu.VMEM(history.shape, f32),
                pltpu.VMEM(shift.shape, f32),
                pltpu.VMEM(trans.shape, trans.dtype),
                pltpu.SMEM((entries, groups), i32),
                pltpu.SMEM((entries, groups), i32),
                *smem_lists,
                dma,
                dma((10,)),
            ],
            compiler_params=params,
            name="past_spectra",
        )(
            *in_hbm(rays, history, shift, trans, far_idx.T, far_lag.T),
            *near_lists,
            blocks,
        )
    )
    mid, message = lax.optimization_barrier((mid, message))
    mid = mid.reshape(lags, clus_count * msg_rows, LANE)
    core_swap = lax.ppermute(mid, "slab", [(i, i ^ 1) for i in range(slab_count)])
    chips = [(i, i + 1) for i in range(1, slab_count - 1, 2)]
    chip_swap = lax.ppermute(mid, "slab", chips + [(b, a) for a, b in chips])

    table_shape = (lags + steps, 3 * clus_count * msg_rows, LANE)
    tall_rows = -(-slots // PACK) * PACK
    newer = []
    for step in range(steps):
        last = step == steps - 1
        arrived = lax.all_to_all(message, ("slab", "clus"), 0, 0, tiled=True)
        arrived = arrived.reshape(groups * msg_rows, LANE)
        out_shape = [
            shaped((clusters, unknowns), f32),
            shaped((near_entries, wide), f32),
            shaped((groups, dir_rows, LANE), f32),
        ]
        currents_in = in_hbm(table) if step else in_hbm(mid, core_swap, chip_swap)
        results = pl.pallas_call(
            functools.partial(near_kernel, step, last, clus_count, lags),
            out_shape=out_shape if step else out_shape + [pltpu.HBM(table_shape, f32)],
            in_specs=[HBM] * 6 + [VMEM] * 2 + [HBM] + [VMEM] * step + [HBM] * len(currents_in),
            out_specs=[VMEM] * 3 + ([] if step else [HBM]),
            scratch_shapes=[
                pltpu.VMEM(table_shape, f32),
                pltpu.VMEM((near_entries, unknowns, unknowns), bf16),
                pltpu.VMEM((clusters, tall_rows, wide), f32),
                pltpu.VMEM((clusters, tall_rows, unknowns), f32),
                pltpu.VMEM((lags + steps, dir_rows, LANE), f32),
                pltpu.VMEM((clusters, unknowns), f32),
                *smem_lists,
                pltpu.SMEM(old_plan.shape, i32),
                dma((near_entries,)),
                dma((9,)),
                dma,
            ],
            compiler_params=params,
            cost_estimate=pl.CostEstimate(
                flops=2 * near_blocks.size, bytes_accessed=3 * near_blocks.size, transcendentals=0
            ),
            name=f"known_near_field_{step}",
        )(
            *near_lists,
            *in_hbm(old_plan, incident),
            *in_vmem(weights, spectra),
            blocks,
            *in_vmem(*newer),
            *currents_in,
        )
        base, blended, known = results[:3]
        if not step:
            table = results[3]
        out_shape = [pltpu.HBM(incident.shape, f32)]
        changed = []
        if step:
            changed.append(output)
        if step and not last:
            changed.append(table)
            out_shape.append(pltpu.HBM(table_shape, f32))
        whole = len(out_shape)
        if not last:
            out_shape += [shaped((dir_rows, LANE), f32), shaped(message.shape, f32)]
        results = pl.pallas_call(
            functools.partial(march_kernel, step, last, clus_count, slab_count, lags),
            out_shape=out_shape,
            in_specs=[HBM] + [VMEM] * 10 + [HBM] * (1 + len(changed)),
            out_specs=[HBM] * whole + [VMEM] * (len(out_shape) - whole),
            scratch_shapes=[
                pltpu.SMEM(near_plan.shape, i32),
                pltpu.VMEM((clusters, unknowns), f32),
                pltpu.VMEM((8, wide), f32),
                pltpu.VMEM((unknowns, unknowns), bf16),
                pltpu.VMEM((clusters, unknowns), f32),
                dma,
                dma((5,)),
            ],
            input_output_aliases={12 + number: number for number in range(len(changed))},
            compiler_params=params,
            name=f"march_{step}",
        )(
            *in_hbm(near_plan),
            *in_vmem(
                base, blended, known, kept, kept_weight, rays, inverses, shift, fresh_weights,
                arrived,
            ),
            blocks,
            *in_hbm(*changed),
        )
        output = results[0]
        if last:
            return output
        if step:
            table = results[1]
        spectrum, message = results[-2:]
        newer.append(spectrum)


def solution(mesh):
    both = ("slab", "clus")
    in_specs = (
        P(None, both, None),
        P(None, both, None),
        P(both, None, None, None),
        P(both, None),
        P(both),
        P(both, None),
        P(both, None),
        P(both, None, None),
        P(both, None, None),
        P(both, None),
        P(),
        P(),
        P(),
    )
    out_specs = P(None, both, None)
    return jax.shard_map(local, mesh=mesh, in_specs=in_specs, out_specs=out_specs, check_vma=False)
```

time: 251 us -> 125 us (0.50)
  local copies, waits for them, and re-layouts: 71.1 us -> 0.81 us
  Pallas kernels: 0 us -> 57.2 us
  matrix products: 43.2 us -> 0 us
  other arithmetic: 31.2 us -> 0.04 us
  waiting for transfers between devices: 58.7 us -> 33.9 us
  blocking collectives: 10.4 us -> 0 us
    pallas_call x0 -> x18, Pallas kernels: none -> 57.2 us  [the longest x8 33.1 us: local(): pl.pallas_call(functools.partial(near_kernel, step, last, clus_count, lag...]
    dot_general x32 -> x0, matrix products: 43.2 us -> none  [the longest x8 30 us: local(): jnp.einsum('cjuv,cjv->cu', near_blocks, blended, preferred_element_type=j...]
    all_to_all x8, waiting for transfers between devices: 58.7 us -> 33.3 us  [local(): arrived = lax.all_to_all(message, ('slab', 'clus'), 0, 0, tiled=True)]
    gather x32 -> x0, local copies, waits for them, and re-layouts: 23.2 us -> none  [the longest x16 11.6 us: local(): second = near_time[lag_slot - 1, near_local]]
    convert_element_type x25 -> x0, other arithmetic: 16.5 us -> none  [the longest x8 5.96 us: local(): blended = jnp.where(live_slot[..., None], (1.0 - near_weight) * first_lag...]
    all_gather x1 -> x0, blocking collectives: 10.4 us -> none  [local(): gathered = lax.all_gather(history, 'clus', axis=1, tiled=True)]
    broadcast_in_dim x8 -> x0, local copies, waits for them, and re-layouts: 8.09 us -> none  [local(): message = jnp.where(is_near[:, None], current.reshape(1, slot), outgoing)]
    unnamed x298 -> x16, local copies, waits for them, and re-layouts: 8.72 us -> 0.78 us
  transfers between devices with their start and end apart: 10 -> 13, of which waited for: 8 -> 10; matrix products, arithmetic and copies ran while one was open for 6% -> 0% of each run, Pallas kernels for 0% -> 29%
where the time goes in v2:
time: 125 us; the launch traced here: 124 us
  Pallas kernels  57.2 us (46%)
  waiting for transfers between devices  33.9 us (27%)
  starting transfers between devices  31.9 us (26%)
    all_to_all x8, waiting for transfers between devices, local(): arrived = lax.all_to_all(message, ('slab', 'clus'), 0, 0, tiled=True)  33.3 us
    pallas_call x8, Pallas kernels, local(): pl.pallas_call(functools.partial(near_kernel, step, last, clus_count, lag...  33.1 us
    all_to_all x8, starting transfers between devices, local(): arrived = lax.all_to_all(message, ('slab', 'clus'), 0, 0, tiled=True)  23.1 us
    pallas_call x8, Pallas kernels, local(): pl.pallas_call(functools.partial(march_kernel, step, last, clus_count, sl...  19.8 us
    ppermute x3, starting transfers between devices, exchange(): return lax.ppermute(block, axis, [(i, i ^ bit) for i in range(count)])  4.6 us
    ppermute x1, starting transfers between devices, local(): lax.ppermute(mid, 'slab', [(i, i ^ 1) for i in range(slab_count)])  3.49 us
    pallas_call x1, Pallas kernels, local(): pl.pallas_call(functools.partial(begin_kernel, clus_count), out_shape=(sh...  3.48 us
  transfers between devices with their start and end apart: 13, of which 10 were waited for; matrix products, arithmetic and copies ran while one was open for 0% of the time, Pallas kernels for 29%

profile of v2, /device:TPU:0, one launch (start us, length us, event | category | flops | bytes accessed | tf_op | source)
XLA Modules:
  0.0 124.3 jit_solution(10272064608466106707)
XLA Ops:
  0.9 4.0 %collective-permute-start.2 = (f32[16,8,128]{2,1,0:T(8,128)S(1)}, f32[16,8,128]{2,1,0:T(8,128)S(1)}, u32[]{:S(2)}, u32[]{:S(2)}) collective-permute-start(f32[16,8,128]{2,1,0:T(8,128)S(1)} %pack_history.1), channel_id=1, source_target_pairs={{0,3},{1,2},{2,1},{3,0},{4,7},{5,6},{6,5},{7,4},{8,11},{9,10},{10,... | collective-permute-start | bytes 196616 | tf_op jit(solution)/shard_map/ppermute | solution.py:460
  5.5 3.5 %past_spectra.1 = (f32[16,4,128]{2,1,0:T(4,128)S(1)}, f32[32,8,128]{2,1,0:T(8,128)}, f32[256,4,128]{2,1,0:T(4,128)S(1)}, f32[32,4,128]{2,1,0:T(4,128)S(1)}, bf16...) custom-call(bf16[4,200,512]{2,1,0:T(8,128)(2,1)} %bitcast.24, ...), custom_call_target="tpu_custom_call" | custom-call | tf_op jit(solution)/shard_map/past_spectra/pallas_call | solution.py:521
  10.4 3.5 %collective-permute-start.3 = (f32[16,32,128]{2,1,0:T(8,128)S(1)}, f32[16,32,128]{2,1,0:T(8,128)S(1)}, u32[]{:S(2)}, u32[]{:S(2)}) collective-permute-start(f32[16,32,128]{2,1,0:T(8,128)S(1)} %bitcast.43), channel_id=1, source_target_pairs={{0,4},{4,0},{8,12},{12,8},{16,20},{20,16},{24,28},{28,24},{1,5},{5... | collective-permute-start | bytes 786440 | tf_op jit(solution)/shard_map/ppermute | solution.py:556
  13.9 4.8 %all-to-all-start = ((f32[32,8,128]{2,1,0:T(8,128)}), f32[32,8,128]{2,1,0:T(8,128)S(1)}, u32[]{:S(2)}, u32[]{:S(2)}) async-start(f32[32,8,128]{2,1,0:T(8,128)} %get-tuple-element.79), calls=%async_computation | async-start | bytes 262144 | tf_op jit(solution)/shard_map/all_to_all | solution.py:565
  19.5 4.3 %known_near_field_0.1 = (f32[4,200]{1,0:T(4,128)S(1)}, f32[48,256]{1,0:T(8,128)S(1)}, f32[32,4,128]{2,1,0:T(4,128)S(1)}, f32[24,96,128]{2,1,0:T(8,128)}) custom-call(s32[4,12]{1,0:T(4,128)} %refs_0_.15, s32[4]{0:T(128)} %refs_1_.15, s32[4,12]{1,0:T(4,128)} %refs_2_.15, f32[4,12]{1,0:T(4,128)} %refs_3_.15, s32[772]{0:T(1024)} %copy-done.3, ...), custom_call_target="tpu_custom_call" | custom-call | flops 3840000 | bytes 5760000 | tf_op jit(solution)/shard_map/known_near_field_0/pallas_call | solution.py:573
  23.9 3.2 %all-to-all-done = f32[32,8,128]{2,1,0:T(8,128)S(1)} async-done(((f32[32,8,128]{2,1,0:T(8,128)}), f32[32,8,128]{2,1,0:T(8,128)S(1)}, u32[]{:S(2)}, u32[]{:S(2)}) %all-to-all-start) | async-done | bytes 131104 | tf_op jit(solution)/shard_map/all_to_all | solution.py:565
  29.5 2.6 %all-to-all-start.1 = ((f32[32,8,128]{2,1,0:T(8,128)}), f32[32,8,128]{2,1,0:T(8,128)S(1)}, u32[]{:S(2)}, u32[]{:S(2)}) async-start(f32[32,8,128]{2,1,0:T(8,128)} %get-tuple-element.85), calls=%async_computation.1 | async-start | bytes 262144 | tf_op jit(solution)/shard_map/all_to_all | solution.py:565
  32.1 4.1 %known_near_field_1.1 = (f32[4,200]{1,0:T(4,128)S(1)}, f32[48,256]{1,0:T(8,128)S(1)}, f32[32,4,128]{2,1,0:T(4,128)S(1)}) custom-call(s32[4,12]{1,0:T(4,128)} %refs_0_.15, s32[4]{0:T(128)} %refs_1_.15, s32[4,12]{1,0:T(4,128)} %refs_2_.15, f32[4,12]{1,0:T(4,128)} %refs_3_.15, s32[772]{0:T(1024)} %copy-done.3, f32[8,4,200]{2,1,0:T(4,128)} %refs_5_.15, ...), custom_call_target="tpu_custom_call" | custom-call | flops 3840000 | bytes 5760000 | tf_op jit(solution)/shard_map/known_near_field_1/pallas_call | solution.py:573
  36.2 4.3 %all-to-all-done.1 = f32[32,8,128]{2,1,0:T(8,128)S(1)} async-done(((f32[32,8,128]{2,1,0:T(8,128)}), f32[32,8,128]{2,1,0:T(8,128)S(1)}, u32[]{:S(2)}, u32[]{:S(2)}) %all-to-all-start.1) | async-done | bytes 131104 | tf_op jit(solution)/shard_map/all_to_all | solution.py:565
  45.7 4.1 %known_near_field_2.1 = (f32[4,200]{1,0:T(4,128)S(1)}, f32[48,256]{1,0:T(8,128)S(1)}, f32[32,4,128]{2,1,0:T(4,128)S(1)}) custom-call(s32[4,12]{1,0:T(4,128)} %refs_0_.15, s32[4]{0:T(128)} %refs_1_.15, s32[4,12]{1,0:T(4,128)} %refs_2_.15, f32[4,12]{1,0:T(4,128)} %refs_3_.15, s32[772]{0:T(1024)} %copy-done.3, f32[8,4,200]{2,1,0:T(4,128)} %refs_5_.15, ...), custom_call_target="tpu_custom_call" | custom-call | flops 3840000 | bytes 5760000 | tf_op jit(solution)/shard_map/known_near_field_2/pallas_call | solution.py:573
  49.8 4.3 %all-to-all-done.2 = f32[32,8,128]{2,1,0:T(8,128)S(1)} async-done(((f32[32,8,128]{2,1,0:T(8,128)}), f32[32,8,128]{2,1,0:T(8,128)S(1)}, u32[]{:S(2)}, u32[]{:S(2)}) %all-to-all-start.2) | async-done | bytes 131104 | tf_op jit(solution)/shard_map/all_to_all | solution.py:565
  59.3 4.1 %known_near_field_3.1 = (f32[4,200]{1,0:T(4,128)S(1)}, f32[48,256]{1,0:T(8,128)S(1)}, f32[32,4,128]{2,1,0:T(4,128)S(1)}) custom-call(s32[4,12]{1,0:T(4,128)} %refs_0_.15, s32[4]{0:T(128)} %refs_1_.15, s32[4,12]{1,0:T(4,128)} %refs_2_.15, f32[4,12]{1,0:T(4,128)} %refs_3_.15, s32[772]{0:T(1024)} %copy-done.3, f32[8,4,200]{2,1,0:T(4,128)} %refs_5_.15, ...), custom_call_target="tpu_custom_call" | custom-call | flops 3840000 | bytes 5760000 | tf_op jit(solution)/shard_map/known_near_field_3/pallas_call | solution.py:573
  63.3 4.3 %all-to-all-done.3 = f32[32,8,128]{2,1,0:T(8,128)S(1)} async-done(((f32[32,8,128]{2,1,0:T(8,128)}), f32[32,8,128]{2,1,0:T(8,128)S(1)}, u32[]{:S(2)}, u32[]{:S(2)}) %all-to-all-start.3) | async-done | bytes 131104 | tf_op jit(solution)/shard_map/all_to_all | solution.py:565
  72.9 4.2 %known_near_field_4.1 = (f32[4,200]{1,0:T(4,128)S(1)}, f32[48,256]{1,0:T(8,128)S(1)}, f32[32,4,128]{2,1,0:T(4,128)S(1)}) custom-call(s32[4,12]{1,0:T(4,128)} %refs_0_.15, s32[4]{0:T(128)} %refs_1_.15, s32[4,12]{1,0:T(4,128)} %refs_2_.15, f32[4,12]{1,0:T(4,128)} %refs_3_.15, s32[772]{0:T(1024)} %copy-done.3, f32[8,4,200]{2,1,0:T(4,128)} %refs_5_.15, ...), custom_call_target="tpu_custom_call" | custom-call | flops 3840000 | bytes 5760000 | tf_op jit(solution)/shard_map/known_near_field_4/pallas_call | solution.py:573
  77.1 4.2 %all-to-all-done.4 = f32[32,8,128]{2,1,0:T(8,128)S(1)} async-done(((f32[32,8,128]{2,1,0:T(8,128)}), f32[32,8,128]{2,1,0:T(8,128)S(1)}, u32[]{:S(2)}, u32[]{:S(2)}) %all-to-all-start.4) | async-done | bytes 131104 | tf_op jit(solution)/shard_map/all_to_all | solution.py:565
  83.8 2.8 %all-to-all-start.5 = ((f32[32,8,128]{2,1,0:T(8,128)}), f32[32,8,128]{2,1,0:T(8,128)S(1)}, u32[]{:S(2)}, u32[]{:S(2)}) async-start(f32[32,8,128]{2,1,0:T(8,128)} %get-tuple-element.113), calls=%async_computation.5 | async-start | bytes 262144 | tf_op jit(solution)/shard_map/all_to_all | solution.py:565
  86.6 4.1 %known_near_field_5.1 = (f32[4,200]{1,0:T(4,128)S(1)}, f32[48,256]{1,0:T(8,128)S(1)}, f32[32,4,128]{2,1,0:T(4,128)S(1)}) custom-call(s32[4,12]{1,0:T(4,128)} %refs_0_.15, s32[4]{0:T(128)} %refs_1_.15, s32[4,12]{1,0:T(4,128)} %refs_2_.15, f32[4,12]{1,0:T(4,128)} %refs_3_.15, s32[772]{0:T(1024)} %copy-done.3, f32[8,4,200]{2,1,0:T(4,128)} %refs_5_.15, ...), custom_call_target="tpu_custom_call" | custom-call | flops 3840000 | bytes 5760000 | tf_op jit(solution)/shard_map/known_near_field_5/pallas_call | solution.py:573
  90.7 4.3 %all-to-all-done.5 = f32[32,8,128]{2,1,0:T(8,128)S(1)} async-done(((f32[32,8,128]{2,1,0:T(8,128)}), f32[32,8,128]{2,1,0:T(8,128)S(1)}, u32[]{:S(2)}, u32[]{:S(2)}) %all-to-all-start.5) | async-done | bytes 131104 | tf_op jit(solution)/shard_map/all_to_all | solution.py:565
  95.0 2.6 %march_5.1 = (f32[8,4,200]{2,1,0:T(4,128)}, f32[24,96,128]{2,1,0:T(8,128)}, f32[4,128]{1,0:T(4,128)S(1)}, f32[32,8,128]{2,1,0:T(8,128)}) custom-call(s32[148]{0:T(256)} %copy-done.4, f32[4,200]{1,0:T(4,128)S(1)} %get-tuple-element.110.refs_1_, f32[48,256]{1,0:T(8,128)S(1)} %get-tuple-element.111.refs_2_, ...), custom_call_target="tpu_custom_call", output_to_operand_aliasing={{0}: (12, {}), {1}: (13, {})} | custom-call | tf_op jit(solution)/shard_map/march_5/pallas_call | solution.py:617
  97.6 2.6 %all-to-all-start.6 = ((f32[32,8,128]{2,1,0:T(8,128)}), f32[32,8,128]{2,1,0:T(8,128)S(1)}, u32[]{:S(2)}, u32[]{:S(2)}) async-start(f32[32,8,128]{2,1,0:T(8,128)} %get-tuple-element.120), calls=%async_computation.6 | async-start | bytes 262144 | tf_op jit(solution)/shard_map/all_to_all | solution.py:565
  100.2 4.1 %known_near_field_6.1 = (f32[4,200]{1,0:T(4,128)S(1)}, f32[48,256]{1,0:T(8,128)S(1)}, f32[32,4,128]{2,1,0:T(4,128)S(1)}) custom-call(s32[4,12]{1,0:T(4,128)} %refs_0_.15, s32[4]{0:T(128)} %refs_1_.15, s32[4,12]{1,0:T(4,128)} %refs_2_.15, f32[4,12]{1,0:T(4,128)} %refs_3_.15, s32[772]{0:T(1024)} %copy-done.3, f32[8,4,200]{2,1,0:T(4,128)} %refs_5_.15, ...), custom_call_target="tpu_custom_call" | custom-call | flops 3840000 | bytes 5760000 | tf_op jit(solution)/shard_map/known_near_field_6/pallas_call | solution.py:573
  104.3 4.3 %all-to-all-done.6 = f32[32,8,128]{2,1,0:T(8,128)S(1)} async-done(((f32[32,8,128]{2,1,0:T(8,128)}), f32[32,8,128]{2,1,0:T(8,128)S(1)}, u32[]{:S(2)}, u32[]{:S(2)}) %all-to-all-start.6) | async-done | bytes 131104 | tf_op jit(solution)/shard_map/all_to_all | solution.py:565
  113.8 4.2 %known_near_field_7.1 = (f32[4,200]{1,0:T(4,128)S(1)}, f32[48,256]{1,0:T(8,128)S(1)}, f32[32,4,128]{2,1,0:T(4,128)S(1)}) custom-call(s32[4,12]{1,0:T(4,128)} %refs_0_.15, s32[4]{0:T(128)} %refs_1_.15, s32[4,12]{1,0:T(4,128)} %refs_2_.15, f32[4,12]{1,0:T(4,128)} %refs_3_.15, s32[772]{0:T(1024)} %copy-done.3, f32[8,4,200]{2,1,0:T(4,128)} %refs_5_.15, ...), custom_call_target="tpu_custom_call" | custom-call | flops 3840000 | bytes 5760000 | tf_op jit(solution)/shard_map/known_near_field_7/pallas_call | solution.py:573
  118.0 4.2 %all-to-all-done.7 = f32[32,8,128]{2,1,0:T(8,128)S(1)} async-done(((f32[32,8,128]{2,1,0:T(8,128)}), f32[32,8,128]{2,1,0:T(8,128)S(1)}, u32[]{:S(2)}, u32[]{:S(2)}) %all-to-all-start.7) | async-done | bytes 131104 | tf_op jit(solution)/shard_map/all_to_all | solution.py:565
  (39 shorter events, 31.2 us)
Async XLA Ops:
  0.9 8.1 %collective-permute-start.2 = (f32[16,8,128]{2,1,0:T(8,128)S(1)}, f32[16,8,128]{2,1,0:T(8,128)S(1)}, u32[]{:S(2)}, u32[]{:S(2)}) collective-permute-start(f32[16,8,128]{2,1,0:T(8,128)S(1)} %pack_history.1), channel_id=1, source_target_pairs={{0,3},{1,2},{2,1},{3,0},{4,7},{5,6},{6,5},{7,4},{8,11},{9,10},{10,... | collective-permute-start | bytes 196616 | tf_op jit(solution)/shard_map/ppermute | solution.py:460
  4.8 4.3 %collective-permute-start.1 = (f32[16,8,128]{2,1,0:T(8,128)S(1)}, f32[16,8,128]{2,1,0:T(8,128)S(1)}, u32[]{:S(2)}, u32[]{:S(2)}) collective-permute-start(f32[16,8,128]{2,1,0:T(8,128)S(1)} %pack_history.1), channel_id=1, source_target_pairs={{0,2},{1,3},{2,0},{3,1},{4,6},{5,7},{6,4},{7,5},{8,10},{9,11},{10,... | collective-permute-start | bytes 196616 | tf_op jit(solution)/shard_map/ppermute | solution.py:460
  5.3 4.3 %collective-permute-start = (f32[16,8,128]{2,1,0:T(8,128)S(1)}, f32[16,8,128]{2,1,0:T(8,128)S(1)}, u32[]{:S(2)}, u32[]{:S(2)}) collective-permute-start(f32[16,8,128]{2,1,0:T(8,128)S(1)} %pack_history.1), channel_id=1, source_target_pairs={{0,1},{1,0},{2,3},{3,2},{4,5},{5,4},{6,7},{7,6},{8,9},{9,8},{10,11... | collective-permute-start | bytes 196616 | tf_op jit(solution)/shard_map/ppermute | solution.py:460
  8.9 0.7 copy-start.3
  9.0 0.7 copy-start.4
  9.7 9.8 %copy-start.5 = (f32[16,4,8,128]{3,2,1,0:T(8,128)}, f32[16,4,8,128]{3,2,1,0:T(8,128)S(1)}, u32[]{:S(2)}) copy-start(f32[16,4,8,128]{3,2,1,0:T(8,128)S(1)} %pad_maximum_fusion.1) | copy-start | bytes 786436
  9.7 9.0 %collective-permute-start.4 = (f32[16,32,128]{2,1,0:T(8,128)S(1)}, f32[16,32,128]{2,1,0:T(8,128)S(1)}, u32[]{:S(2)}, u32[]{:S(2)}) collective-permute-start(f32[16,32,128]{2,1,0:T(8,128)S(1)} %bitcast.42), channel_id=1, source_target_pairs={{4,8},{12,16},{20,24},{8,4},{16,12},{24,20},{5,9},{13,17},{21,25},... | collective-permute-start | bytes 786440 | tf_op jit(solution)/shard_map/ppermute | solution.py:558
  10.4 8.3 %collective-permute-start.3 = (f32[16,32,128]{2,1,0:T(8,128)S(1)}, f32[16,32,128]{2,1,0:T(8,128)S(1)}, u32[]{:S(2)}, u32[]{:S(2)}) collective-permute-start(f32[16,32,128]{2,1,0:T(8,128)S(1)} %bitcast.43), channel_id=1, source_target_pairs={{0,4},{4,0},{8,12},{12,8},{16,20},{20,16},{24,28},{28,24},{1,5},{5... | collective-permute-start | bytes 786440 | tf_op jit(solution)/shard_map/ppermute | solution.py:556
  13.9 13.2 %all-to-all-start = ((f32[32,8,128]{2,1,0:T(8,128)}), f32[32,8,128]{2,1,0:T(8,128)S(1)}, u32[]{:S(2)}, u32[]{:S(2)}) async-start(f32[32,8,128]{2,1,0:T(8,128)} %get-tuple-element.79), calls=%async_computation | async-start | bytes 262144 | tf_op jit(solution)/shard_map/all_to_all | solution.py:565
  18.7 0.8 copy-start.6
  18.7 0.8 copy-start.7
  19.5 7.6 %copy-start = (bf16[4,512,200]{1,2,0:T(8,128)(2,1)S(1)}, bf16[4,512,200]{1,2,0:T(8,128)(2,1)}, u32[]{:S(2)}) copy-start(bf16[4,512,200]{1,2,0:T(8,128)(2,1)} %param.21) | copy-start | bytes 2457604
  19.5 7.6 %copy-start.1 = (bf16[4,200,200]{2,1,0:T(8,128)(2,1)S(1)}, bf16[4,200,200]{2,1,0:T(8,128)(2,1)}, u32[]{:S(2)}) copy-start(bf16[4,200,200]{2,1,0:T(8,128)(2,1)} %refs_7_.15) | copy-start | bytes 960004
  19.5 7.6 %copy-start.2 = (f32[4,512]{1,0:T(4,128)S(1)}, f32[4,512]{1,0:T(4,128)}, u32[]{:S(2)}) copy-start(f32[4,512]{1,0:T(4,128)} %refs_8_.31) | copy-start | bytes 24580
  29.5 11.1 %all-to-all-start.1 = ((f32[32,8,128]{2,1,0:T(8,128)}), f32[32,8,128]{2,1,0:T(8,128)S(1)}, u32[]{:S(2)}, u32[]{:S(2)}) async-start(f32[32,8,128]{2,1,0:T(8,128)} %get-tuple-element.85), calls=%async_computation.1 | async-start | bytes 262144 | tf_op jit(solution)/shard_map/all_to_all | solution.py:565
  43.1 11.0 %all-to-all-start.2 = ((f32[32,8,128]{2,1,0:T(8,128)}), f32[32,8,128]{2,1,0:T(8,128)S(1)}, u32[]{:S(2)}, u32[]{:S(2)}) async-start(f32[32,8,128]{2,1,0:T(8,128)} %get-tuple-element.92), calls=%async_computation.2 | async-start | bytes 262144 | tf_op jit(solution)/shard_map/all_to_all | solution.py:565
  56.7 11.0 %all-to-all-start.3 = ((f32[32,8,128]{2,1,0:T(8,128)}), f32[32,8,128]{2,1,0:T(8,128)S(1)}, u32[]{:S(2)}, u32[]{:S(2)}) async-start(f32[32,8,128]{2,1,0:T(8,128)} %get-tuple-element.99), calls=%async_computation.3 | async-start | bytes 262144 | tf_op jit(solution)/shard_map/all_to_all | solution.py:565
  70.3 11.0 %all-to-all-start.4 = ((f32[32,8,128]{2,1,0:T(8,128)}), f32[32,8,128]{2,1,0:T(8,128)S(1)}, u32[]{:S(2)}, u32[]{:S(2)}) async-start(f32[32,8,128]{2,1,0:T(8,128)} %get-tuple-element.106), calls=%async_computation.4 | async-start | bytes 262144 | tf_op jit(solution)/shard_map/all_to_all | solution.py:565
  83.8 11.2 %all-to-all-start.5 = ((f32[32,8,128]{2,1,0:T(8,128)}), f32[32,8,128]{2,1,0:T(8,128)S(1)}, u32[]{:S(2)}, u32[]{:S(2)}) async-start(f32[32,8,128]{2,1,0:T(8,128)} %get-tuple-element.113), calls=%async_computation.5 | async-start | bytes 262144 | tf_op jit(solution)/shard_map/all_to_all | solution.py:565
  97.6 11.0 %all-to-all-start.6 = ((f32[32,8,128]{2,1,0:T(8,128)}), f32[32,8,128]{2,1,0:T(8,128)S(1)}, u32[]{:S(2)}, u32[]{:S(2)}) async-start(f32[32,8,128]{2,1,0:T(8,128)} %get-tuple-element.120), calls=%async_computation.6 | async-start | bytes 262144 | tf_op jit(solution)/shard_map/all_to_all | solution.py:565
  111.2 11.0 %all-to-all-start.7 = ((f32[32,8,128]{2,1,0:T(8,128)}), f32[32,8,128]{2,1,0:T(8,128)S(1)}, u32[]{:S(2)}, u32[]{:S(2)}) async-start(f32[32,8,128]{2,1,0:T(8,128)} %get-tuple-element.127), calls=%async_computation.7 | async-start | bytes 262144 | tf_op jit(solution)/shard_map/all_to_all | solution.py:565

commit v3 on v2

--- a/solution.py
+++ b/solution.py
@@ -89,20 +89,20 @@
     clus_count,
     rays_in, history_in, shift_in, trans_in, far_idx_in, far_lag_in, near_idx_in, near_cnt_in,
     near_lag_in, near_frac_in, blocks,
-    spectra, message, weights, fresh_weights, kept, kept_weight, near_plan, old_plan,
-    rays, history, shift, trans, far_idx, far_lag, near_idx, near_cnt, near_lag, near_frac, sem,
-    sems,
+    spectra, message, weights, fresh_weights, kept, kept_weight, kept_plan, near_plan, old_plan,
+    rays, history, shift, trans, far_idx, far_lag, near_idx, near_cnt, near_lag, near_frac,
+    far_list, sem, sems,
 ):
     small = start_all(
         (
+            (far_idx_in, far_idx), (far_lag_in, far_lag), (trans_in, trans),
             (near_idx_in, near_idx), (near_cnt_in, near_cnt), (near_lag_in, near_lag),
-            (near_frac_in, near_frac), (far_idx_in, far_idx), (far_lag_in, far_lag),
+            (near_frac_in, near_frac),
         ),
         sems,
     )
     large = start_all(
-        ((history_in, history), (rays_in, rays), (shift_in, shift), (trans_in, trans)),
-        sems.at[pl.ds(6, 4)],
+        ((history_in, history), (shift_in, shift), (rays_in, rays)), sems.at[pl.ds(7, 3)]
     )
     lags, clusters, unknowns = history.shape
     dir_rows = spectra.shape[1]
@@ -118,6 +118,8 @@
     for place in range(3 * KEPT + 1):
         near_plan[place] = 0
     kept_weight[...] = jnp.zeros(kept_weight.shape, jnp.float32)
+    kept_plan[...] = jnp.zeros(kept_plan.shape, jnp.int32)
+    lane = lax.broadcasted_iota(jnp.int32, (1, LANE), 1)
     message[...] = jnp.zeros(message.shape, jnp.float32)
     fresh_weights[...] = jnp.zeros(fresh_weights.shape, jnp.float32)
     wait_all(small)
@@ -135,9 +137,10 @@
                 def _(slot=slot):
                     count = near_plan[0]
                     entry = jnp.int32(cluster * slots + slot)
+                    place = row_of(near_idx[cluster, slot], clusters, halves)
                     near_plan[3 * count + 1] = entry
                     near_plan[3 * count + 2] = jnp.int32(cluster)
-                    near_plan[3 * count + 3] = row_of(near_idx[cluster, slot], clusters, halves)
+                    near_plan[3 * count + 3] = place
                     row = jnp.zeros((1, kept_weight.shape[1]), jnp.float32)
                     kept_weight[pl.ds(count, 1), :] = row + (1.0 - near_frac[cluster, slot])
                     near_plan[0] = count + 1
@@ -145,15 +148,12 @@
                     @pl.when(count < KEPT)
                     def _():
                         kept_copy(count, entry).start()
-
-    wait_all(large)
-    total = jnp.zeros((lags, dir_rows * LANE), jnp.float32)
-    for cluster in range(clusters):
-        past = history[:, cluster, :].astype(jnp.bfloat16)
-        total += dot(past, rays[cluster]) * shift[cluster : cluster + 1, :]
-    for lag in range(lags):
-        spectra[lag] = rows_of(total[lag : lag + 1], dir_rows)
-
+                        fields = jnp.where(lane == 0, entry, jnp.where(lane == 1, cluster, place))
+                        kept_plan[pl.ds(count, 1), :] = fields
+
+    kept_plan[...] = jnp.where(
+        lax.broadcasted_iota(jnp.int32, kept_plan.shape, 1) == 3, near_plan[0], kept_plan[...]
+    )
     def one(group, counts):
         listed = [far_idx[column, group] == myself for column in range(entries)]
 
@@ -167,7 +167,8 @@
                     row = trans[group, column : column + 1, :].astype(jnp.float32)
                     weight = rows_of(row, dir_rows)
                     weights[place] = weight
-                    message[group, :dir_rows, :] += weight * spectra[lags - lag]
+                    far_list[2 * place] = group
+                    far_list[2 * place + 1] = lag
 
                     @pl.when(lag == 1)
                     def _():
@@ -187,6 +188,21 @@
 
     counts = lax.fori_loop(0, groups, one, (jnp.int32(0), jnp.int32(0)))
     old_plan[0] = counts[1]
+
+    wait_all(large)
+    total = jnp.zeros((lags, dir_rows * LANE), jnp.float32)
+    for cluster in range(clusters):
+        past = history[:, cluster, :].astype(jnp.bfloat16)
+        total += dot(past, rays[cluster]) * shift[cluster : cluster + 1, :]
+    for lag in range(lags):
+        spectra[lag] = rows_of(total[lag : lag + 1], dir_rows)
+
+    def add_past(place, carry):
+        group, lag = far_list[2 * place], far_list[2 * place + 1]
+        message[group, :dir_rows, :] += weights[place] * spectra[lags - lag]
+        return carry
+
+    lax.fori_loop(0, counts[0], add_past, 0)
 
     def finish(place, carry):
         kept_copy(place, near_plan[3 * place + 1]).wait()
@@ -343,18 +359,18 @@
 
 def march_kernel(step, last, clus_count, slab_count, lags, *refs):
     (
-        near_plan_in, base, blended, known, kept, kept_weight, rays, inverses, shift,
+        near_plan_in, kept_plan, base, blended, known, kept, kept_weight, rays, inverses, shift,
         fresh_weights, arrived, blocks,
-    ) = refs[:12]
+    ) = refs[:13]
     if last:
-        _, output = refs[12:14]
-        refs = refs[14:]
+        _, output = refs[13:15]
+        refs = refs[15:]
     elif step:
-        _, _, output, table, spectrum, message = refs[12:18]
-        refs = refs[18:]
+        _, _, output, table, spectrum, message = refs[13:19]
+        refs = refs[19:]
     else:
-        output, spectrum, message = refs[12:15]
-        refs = refs[15:]
+        output, spectrum, message = refs[13:16]
+        refs = refs[16:]
     near_plan, current, values, extra, field, sem, sems = refs
     clusters, unknowns = base.shape
     slots = blocks.shape[1]
@@ -364,8 +380,6 @@
     side_rows = clus_count * rows_each
     slab = lax.axis_index("slab")
     which = lax.broadcasted_iota(jnp.int32, (clusters, unknowns), 0)
-    plan_copy = pltpu.make_async_copy(near_plan_in, near_plan, sems.at[0])
-    plan_copy.start()
     kept_copies = []
     if step and not last:
         for side in range(3):
@@ -393,35 +407,39 @@
         far = jnp.where(which == cluster, dot_t(inbound, rays[cluster]), far)
     remaining = base[...] - far
 
-    def fresh_row(place):
-        entry, row = near_plan[3 * place + 1], near_plan[3 * place + 3]
+    def fresh_row(place, entry, row):
         newest = jnp.concatenate(
             [arrived[pl.ds(row + half * clusters, 1), :] for half in range(halves)], axis=1
         )
         return blended[pl.ds(entry, 1), :] + kept_weight[pl.ds(place, 1), :] * newest
 
-    plan_copy.wait()
     if step:
-        count = near_plan[0]
+        plan = kept_plan[...]
+        count = plan[0, 3]
         values[...] = jnp.zeros(values.shape, jnp.float32)
         for place in range(KEPT):
-            values[place : place + 1, :] = fresh_row(place)
+            values[place : place + 1, :] = fresh_row(place, plan[place, 0], plan[place, 2])
         rows = values[...].astype(jnp.bfloat16)[:, :unknowns]
         for place in range(KEPT):
             product = dot_t(rows, kept[place])[place : place + 1]
-            cluster = jnp.where(place < count, near_plan[3 * place + 2], -1)
+            cluster = jnp.where(place < count, plan[place, 1], -1)
             remaining = remaining - jnp.where(which == cluster, product, 0.0)
         field[...] = remaining
 
         @pl.when(count > KEPT)
         def _():
+            plan_copy = pltpu.make_async_copy(near_plan_in, near_plan, sems.at[0])
+            plan_copy.start()
+            plan_copy.wait()
+
             def one(place, carry):
                 entry = near_plan[3 * place + 1]
                 cluster = near_plan[3 * place + 2]
                 source = blocks.at[cluster, entry - cluster * slots]
                 copy = pltpu.make_async_copy(source, extra, sem)
                 copy.start()
-                row = jnp.broadcast_to(fresh_row(place), (8, halves * LANE))
+                row = fresh_row(place, entry, near_plan[3 * place + 3])
+                row = jnp.broadcast_to(row, (8, halves * LANE))
                 copy.wait()
                 product = dot_t(row.astype(jnp.bfloat16)[:, :unknowns], extra[...])
                 field[pl.ds(cluster, 1), :] -= product[:1]
@@ -517,7 +535,7 @@
     dma = pltpu.SemaphoreType.DMA
     near_lists = in_hbm(near_idx, near_cnt, near_lag, near_frac)
     (blocks,) = in_hbm(near_blocks)
-    spectra, message, weights, fresh_weights, kept, kept_weight, near_plan, old_plan = (
+    spectra, message, weights, fresh_weights, kept, kept_weight, kept_plan, near_plan, old_plan = (
         pl.pallas_call(
             functools.partial(begin_kernel, clus_count),
             out_shape=(
@@ -527,11 +545,12 @@
                 shaped((groups, dir_rows, LANE), f32),
                 shaped((KEPT, unknowns, unknowns), bf16),
                 shaped((near_entries, wide), f32),
-                shaped((3 * near_entries + 4,), i32),
-                shaped((3 * far_entries + 4,), i32),
+                shaped((8, LANE), i32),
+                pltpu.HBM((3 * near_entries + 4,), i32),
+                pltpu.HBM((3 * far_entries + 4,), i32),
             ),
             in_specs=[HBM] * 11,
-            out_specs=[VMEM] * 6 + [SMEM] * 2,
+            out_specs=[VMEM] * 7 + [SMEM] * 2,
             scratch_shapes=[
                 pltpu.VMEM(rays.shape, bf16),
                 pltpu.VMEM(history.shape, f32),
@@ -540,6 +559,7 @@
                 pltpu.SMEM((entries, groups), i32),
                 pltpu.SMEM((entries, groups), i32),
                 *smem_lists,
+                pltpu.SMEM((2 * far_entries + 2,), i32),
                 dma,
                 dma((10,)),
             ],
@@ -617,7 +637,7 @@
         results = pl.pallas_call(
             functools.partial(march_kernel, step, last, clus_count, slab_count, lags),
             out_shape=out_shape,
-            in_specs=[HBM] + [VMEM] * 10 + [HBM] * (1 + len(changed)),
+            in_specs=[HBM] + [VMEM] * 11 + [HBM] * (1 + len(changed)),
             out_specs=[HBM] * whole + [VMEM] * (len(out_shape) - whole),
             scratch_shapes=[
                 pltpu.SMEM(near_plan.shape, i32),
@@ -628,14 +648,14 @@
                 dma,
                 dma((5,)),
             ],
-            input_output_aliases={12 + number: number for number in range(len(changed))},
+            input_output_aliases={13 + number: number for number in range(len(changed))},
             compiler_params=params,
             name=f"march_{step}",
         )(
             *in_hbm(near_plan),
             *in_vmem(
-                base, blended, known, kept, kept_weight, rays, inverses, shift, fresh_weights,
-                arrived,
+                kept_plan, base, blended, known, kept, kept_weight, rays, inverses, shift,
+                fresh_weights, arrived,
             ),
             blocks,
             *in_hbm(*changed),

time: 125 us -> 120 us (0.960)
  Pallas kernels: 57.2 us -> 52.9 us
    pallas_call x8, Pallas kernels: 19.8 us -> 15.6 us  [local(): pl.pallas_call(functools.partial(march_kernel, step, last, clus_count, sl...]
  transfers between devices with their start and end apart: 13 -> 13, of which waited for: 10 -> 9; matrix products, arithmetic and copies ran while one was open for 0% -> 0% of each run, Pallas kernels for 29% -> 31%
where the time goes in v3:
time: 120 us; the launch traced here: 119 us
  Pallas kernels  52.9 us (44%)
  waiting for transfers between devices  34 us (28%)
  starting transfers between devices  31.1 us (26%)
    all_to_all x8, waiting for transfers between devices, local(): arrived = lax.all_to_all(message, ('slab', 'clus'), 0, 0, tiled=True)  33.6 us
    pallas_call x8, Pallas kernels, local(): pl.pallas_call(functools.partial(near_kernel, step, last, clus_count, lag...  32.8 us
    all_to_all x8, starting transfers between devices, local(): arrived = lax.all_to_all(message, ('slab', 'clus'), 0, 0, tiled=True)  22.7 us
    pallas_call x8, Pallas kernels, local(): pl.pallas_call(functools.partial(march_kernel, step, last, clus_count, sl...  15.6 us
    ppermute x3, starting transfers between devices, exchange(): return lax.ppermute(block, axis, [(i, i ^ bit) for i in range(count)])  4.6 us
    pallas_call x1, Pallas kernels, local(): pl.pallas_call(functools.partial(begin_kernel, clus_count), out_shape=(sh...  3.71 us
    ppermute x1, starting transfers between devices, local(): lax.ppermute(mid, 'slab', [(i, i ^ 1) for i in range(slab_count)])  3.15 us
  transfers between devices with their start and end apart: 13, of which 9 were waited for; matrix products, arithmetic and copies ran while one was open for 0% of the time, Pallas kernels for 31%

profile of v3, /device:TPU:0, one launch (start us, length us, event | category | flops | bytes accessed | tf_op | source)
XLA Modules:
  0.0 119.3 jit_solution(8173142899707108929)
XLA Ops:
  0.9 4.0 %collective-permute-start.2 = (f32[16,8,128]{2,1,0:T(8,128)S(1)}, f32[16,8,128]{2,1,0:T(8,128)S(1)}, u32[]{:S(2)}, u32[]{:S(2)}) collective-permute-start(f32[16,8,128]{2,1,0:T(8,128)S(1)} %pack_history.1), channel_id=1, source_target_pairs={{0,3},{1,2},{2,1},{3,0},{4,7},{5,6},{6,5},{7,4},{8,11},{9,10},{10,... | collective-permute-start | bytes 196616 | tf_op jit(solution)/shard_map/ppermute | solution.py:478
  5.5 3.7 %past_spectra.1 = (f32[16,4,128]{2,1,0:T(4,128)S(1)}, f32[32,8,128]{2,1,0:T(8,128)}, f32[256,4,128]{2,1,0:T(4,128)S(1)}, f32[32,4,128]{2,1,0:T(4,128)S(1)}, bf16...) custom-call(bf16[4,200,512]{2,1,0:T(8,128)(2,1)} %bitcast.24, ...), custom_call_target="tpu_custom_call" | custom-call | tf_op jit(solution)/shard_map/past_spectra/pallas_call | solution.py:539
  10.4 3.2 %collective-permute-start.3 = (f32[16,32,128]{2,1,0:T(8,128)S(1)}, f32[16,32,128]{2,1,0:T(8,128)S(1)}, u32[]{:S(2)}, u32[]{:S(2)}) collective-permute-start(f32[16,32,128]{2,1,0:T(8,128)S(1)} %bitcast.43), channel_id=1, source_target_pairs={{0,4},{4,0},{8,12},{12,8},{16,20},{20,16},{24,28},{28,24},{1,5},{5... | collective-permute-start | bytes 786440 | tf_op jit(solution)/shard_map/ppermute | solution.py:576
  13.5 4.5 %all-to-all-start = ((f32[32,8,128]{2,1,0:T(8,128)}), f32[32,8,128]{2,1,0:T(8,128)S(1)}, u32[]{:S(2)}, u32[]{:S(2)}) async-start(f32[32,8,128]{2,1,0:T(8,128)} %get-tuple-element.81), calls=%async_computation | async-start | bytes 262144 | tf_op jit(solution)/shard_map/all_to_all | solution.py:585
  18.9 4.3 %known_near_field_0.1 = (f32[4,200]{1,0:T(4,128)S(1)}, f32[48,256]{1,0:T(8,128)S(1)}, f32[32,4,128]{2,1,0:T(4,128)S(1)}, f32[24,96,128]{2,1,0:T(8,128)}) custom-call(s32[4,12]{1,0:T(4,128)} %refs_0_.15, s32[4]{0:T(128)} %refs_1_.15, s32[4,12]{1,0:T(4,128)} %refs_2_.15, f32[4,12]{1,0:T(4,128)} %refs_3_.15, s32[772]{0:T(1024)} %get-tuple-element.70.refs_4_, ...), custom_call_target="tpu_custom_call" | custom-call | flops 3840000 | bytes 5760000 | tf_op jit(solution)/shard_map/known_near_field_0/pallas_call | solution.py:593
  23.2 3.2 %all-to-all-done = f32[32,8,128]{2,1,0:T(8,128)S(1)} async-done(((f32[32,8,128]{2,1,0:T(8,128)}), f32[32,8,128]{2,1,0:T(8,128)S(1)}, u32[]{:S(2)}, u32[]{:S(2)}) %all-to-all-start) | async-done | bytes 131104 | tf_op jit(solution)/shard_map/all_to_all | solution.py:585
  28.4 2.6 %all-to-all-start.1 = ((f32[32,8,128]{2,1,0:T(8,128)}), f32[32,8,128]{2,1,0:T(8,128)S(1)}, u32[]{:S(2)}, u32[]{:S(2)}) async-start(f32[32,8,128]{2,1,0:T(8,128)} %get-tuple-element.87), calls=%async_computation.1 | async-start | bytes 262144 | tf_op jit(solution)/shard_map/all_to_all | solution.py:585
  31.0 4.0 %known_near_field_1.1 = (f32[4,200]{1,0:T(4,128)S(1)}, f32[48,256]{1,0:T(8,128)S(1)}, f32[32,4,128]{2,1,0:T(4,128)S(1)}) custom-call(s32[4,12]{1,0:T(4,128)} %refs_0_.15, s32[4]{0:T(128)} %refs_1_.15, s32[4,12]{1,0:T(4,128)} %refs_2_.15, f32[4,12]{1,0:T(4,128)} %refs_3_.15, s32[772]{0:T(1024)} %get-tuple-element.70.refs_4_, f32[8,4,200]{2,1,0:T(4,128)} %refs_5_.15, ...), custom_call_target="tpu_custom_call" | custom-call | flops 3840000 | bytes 5760000 | tf_op jit(solution)/shard_map/known_near_field_1/pallas_call | solution.py:593
  35.0 4.4 %all-to-all-done.1 = f32[32,8,128]{2,1,0:T(8,128)S(1)} async-done(((f32[32,8,128]{2,1,0:T(8,128)}), f32[32,8,128]{2,1,0:T(8,128)S(1)}, u32[]{:S(2)}, u32[]{:S(2)}) %all-to-all-start.1) | async-done | bytes 131104 | tf_op jit(solution)/shard_map/all_to_all | solution.py:585
  41.4 2.6 %all-to-all-start.2 = ((f32[32,8,128]{2,1,0:T(8,128)}), f32[32,8,128]{2,1,0:T(8,128)S(1)}, u32[]{:S(2)}, u32[]{:S(2)}) async-start(f32[32,8,128]{2,1,0:T(8,128)} %get-tuple-element.94), calls=%async_computation.2 | async-start | bytes 262144 | tf_op jit(solution)/shard_map/all_to_all | solution.py:585
  44.0 4.0 %known_near_field_2.1 = (f32[4,200]{1,0:T(4,128)S(1)}, f32[48,256]{1,0:T(8,128)S(1)}, f32[32,4,128]{2,1,0:T(4,128)S(1)}) custom-call(s32[4,12]{1,0:T(4,128)} %refs_0_.15, s32[4]{0:T(128)} %refs_1_.15, s32[4,12]{1,0:T(4,128)} %refs_2_.15, f32[4,12]{1,0:T(4,128)} %refs_3_.15, s32[772]{0:T(1024)} %get-tuple-element.70.refs_4_, f32[8,4,200]{2,1,0:T(4,128)} %refs_5_.15, ...), custom_call_target="tpu_custom_call" | custom-call | flops 3840000 | bytes 5760000 | tf_op jit(solution)/shard_map/known_near_field_2/pallas_call | solution.py:593
  48.1 4.4 %all-to-all-done.2 = f32[32,8,128]{2,1,0:T(8,128)S(1)} async-done(((f32[32,8,128]{2,1,0:T(8,128)}), f32[32,8,128]{2,1,0:T(8,128)S(1)}, u32[]{:S(2)}, u32[]{:S(2)}) %all-to-all-start.2) | async-done | bytes 131104 | tf_op jit(solution)/shard_map/all_to_all | solution.py:585
  54.5 2.6 %all-to-all-start.3 = ((f32[32,8,128]{2,1,0:T(8,128)}), f32[32,8,128]{2,1,0:T(8,128)S(1)}, u32[]{:S(2)}, u32[]{:S(2)}) async-start(f32[32,8,128]{2,1,0:T(8,128)} %get-tuple-element.101), calls=%async_computation.3 | async-start | bytes 262144 | tf_op jit(solution)/shard_map/all_to_all | solution.py:585
  57.1 4.0 %known_near_field_3.1 = (f32[4,200]{1,0:T(4,128)S(1)}, f32[48,256]{1,0:T(8,128)S(1)}, f32[32,4,128]{2,1,0:T(4,128)S(1)}) custom-call(s32[4,12]{1,0:T(4,128)} %refs_0_.15, s32[4]{0:T(128)} %refs_1_.15, s32[4,12]{1,0:T(4,128)} %refs_2_.15, f32[4,12]{1,0:T(4,128)} %refs_3_.15, s32[772]{0:T(1024)} %get-tuple-element.70.refs_4_, f32[8,4,200]{2,1,0:T(4,128)} %refs_5_.15, ...), custom_call_target="tpu_custom_call" | custom-call | flops 3840000 | bytes 5760000 | tf_op jit(solution)/shard_map/known_near_field_3/pallas_call | solution.py:593
  61.1 4.4 %all-to-all-done.3 = f32[32,8,128]{2,1,0:T(8,128)S(1)} async-done(((f32[32,8,128]{2,1,0:T(8,128)}), f32[32,8,128]{2,1,0:T(8,128)S(1)}, u32[]{:S(2)}, u32[]{:S(2)}) %all-to-all-start.3) | async-done | bytes 131104 | tf_op jit(solution)/shard_map/all_to_all | solution.py:585
  67.5 2.6 %all-to-all-start.4 = ((f32[32,8,128]{2,1,0:T(8,128)}), f32[32,8,128]{2,1,0:T(8,128)S(1)}, u32[]{:S(2)}, u32[]{:S(2)}) async-start(f32[32,8,128]{2,1,0:T(8,128)} %get-tuple-element.108), calls=%async_computation.4 | async-start | bytes 262144 | tf_op jit(solution)/shard_map/all_to_all | solution.py:585
  70.1 4.1 %known_near_field_4.1 = (f32[4,200]{1,0:T(4,128)S(1)}, f32[48,256]{1,0:T(8,128)S(1)}, f32[32,4,128]{2,1,0:T(4,128)S(1)}) custom-call(s32[4,12]{1,0:T(4,128)} %refs_0_.15, s32[4]{0:T(128)} %refs_1_.15, s32[4,12]{1,0:T(4,128)} %refs_2_.15, f32[4,12]{1,0:T(4,128)} %refs_3_.15, s32[772]{0:T(1024)} %get-tuple-element.70.refs_4_, f32[8,4,200]{2,1,0:T(4,128)} %refs_5_.15, ...), custom_call_target="tpu_custom_call" | custom-call | flops 3840000 | bytes 5760000 | tf_op jit(solution)/shard_map/known_near_field_4/pallas_call | solution.py:593
  74.2 4.3 %all-to-all-done.4 = f32[32,8,128]{2,1,0:T(8,128)S(1)} async-done(((f32[32,8,128]{2,1,0:T(8,128)}), f32[32,8,128]{2,1,0:T(8,128)S(1)}, u32[]{:S(2)}, u32[]{:S(2)}) %all-to-all-start.4) | async-done | bytes 131104 | tf_op jit(solution)/shard_map/all_to_all | solution.py:585
  83.3 4.1 %known_near_field_5.1 = (f32[4,200]{1,0:T(4,128)S(1)}, f32[48,256]{1,0:T(8,128)S(1)}, f32[32,4,128]{2,1,0:T(4,128)S(1)}) custom-call(s32[4,12]{1,0:T(4,128)} %refs_0_.15, s32[4]{0:T(128)} %refs_1_.15, s32[4,12]{1,0:T(4,128)} %refs_2_.15, f32[4,12]{1,0:T(4,128)} %refs_3_.15, s32[772]{0:T(1024)} %get-tuple-element.70.refs_4_, f32[8,4,200]{2,1,0:T(4,128)} %refs_5_.15, ...), custom_call_target="tpu_custom_call" | custom-call | flops 3840000 | bytes 5760000 | tf_op jit(solution)/shard_map/known_near_field_5/pallas_call | solution.py:593
  87.4 4.3 %all-to-all-done.5 = f32[32,8,128]{2,1,0:T(8,128)S(1)} async-done(((f32[32,8,128]{2,1,0:T(8,128)}), f32[32,8,128]{2,1,0:T(8,128)S(1)}, u32[]{:S(2)}, u32[]{:S(2)}) %all-to-all-start.5) | async-done | bytes 131104 | tf_op jit(solution)/shard_map/all_to_all | solution.py:585
  96.3 4.1 %known_near_field_6.1 = (f32[4,200]{1,0:T(4,128)S(1)}, f32[48,256]{1,0:T(8,128)S(1)}, f32[32,4,128]{2,1,0:T(4,128)S(1)}) custom-call(s32[4,12]{1,0:T(4,128)} %refs_0_.15, s32[4]{0:T(128)} %refs_1_.15, s32[4,12]{1,0:T(4,128)} %refs_2_.15, f32[4,12]{1,0:T(4,128)} %refs_3_.15, s32[772]{0:T(1024)} %get-tuple-element.70.refs_4_, f32[8,4,200]{2,1,0:T(4,128)} %refs_5_.15, ...), custom_call_target="tpu_custom_call" | custom-call | flops 3840000 | bytes 5760000 | tf_op jit(solution)/shard_map/known_near_field_6/pallas_call | solution.py:593
  100.4 4.3 %all-to-all-done.6 = f32[32,8,128]{2,1,0:T(8,128)S(1)} async-done(((f32[32,8,128]{2,1,0:T(8,128)}), f32[32,8,128]{2,1,0:T(8,128)S(1)}, u32[]{:S(2)}, u32[]{:S(2)}) %all-to-all-start.6) | async-done | bytes 131104 | tf_op jit(solution)/shard_map/all_to_all | solution.py:585
  109.4 4.1 %known_near_field_7.1 = (f32[4,200]{1,0:T(4,128)S(1)}, f32[48,256]{1,0:T(8,128)S(1)}, f32[32,4,128]{2,1,0:T(4,128)S(1)}) custom-call(s32[4,12]{1,0:T(4,128)} %refs_0_.15, s32[4]{0:T(128)} %refs_1_.15, s32[4,12]{1,0:T(4,128)} %refs_2_.15, f32[4,12]{1,0:T(4,128)} %refs_3_.15, s32[772]{0:T(1024)} %get-tuple-element.70.refs_4_, f32[8,4,200]{2,1,0:T(4,128)} %refs_5_.15, ...), custom_call_target="tpu_custom_call" | custom-call | flops 3840000 | bytes 5760000 | tf_op jit(solution)/shard_map/known_near_field_7/pallas_call | solution.py:593
  113.5 4.3 %all-to-all-done.7 = f32[32,8,128]{2,1,0:T(8,128)S(1)} async-done(((f32[32,8,128]{2,1,0:T(8,128)}), f32[32,8,128]{2,1,0:T(8,128)S(1)}, u32[]{:S(2)}, u32[]{:S(2)}) %all-to-all-start.7) | async-done | bytes 131104 | tf_op jit(solution)/shard_map/all_to_all | solution.py:585
  (35 shorter events, 26.8 us)
Async XLA Ops:
  0.9 8.3 %collective-permute-start.2 = (f32[16,8,128]{2,1,0:T(8,128)S(1)}, f32[16,8,128]{2,1,0:T(8,128)S(1)}, u32[]{:S(2)}, u32[]{:S(2)}) collective-permute-start(f32[16,8,128]{2,1,0:T(8,128)S(1)} %pack_history.1), channel_id=1, source_target_pairs={{0,3},{1,2},{2,1},{3,0},{4,7},{5,6},{6,5},{7,4},{8,11},{9,10},{10,... | collective-permute-start | bytes 196616 | tf_op jit(solution)/shard_map/ppermute | solution.py:478
  4.8 4.4 %collective-permute-start.1 = (f32[16,8,128]{2,1,0:T(8,128)S(1)}, f32[16,8,128]{2,1,0:T(8,128)S(1)}, u32[]{:S(2)}, u32[]{:S(2)}) collective-permute-start(f32[16,8,128]{2,1,0:T(8,128)S(1)} %pack_history.1), channel_id=1, source_target_pairs={{0,2},{1,3},{2,0},{3,1},{4,6},{5,7},{6,4},{7,5},{8,10},{9,11},{10,... | collective-permute-start | bytes 196616 | tf_op jit(solution)/shard_map/ppermute | solution.py:478
  5.3 4.3 %collective-permute-start = (f32[16,8,128]{2,1,0:T(8,128)S(1)}, f32[16,8,128]{2,1,0:T(8,128)S(1)}, u32[]{:S(2)}, u32[]{:S(2)}) collective-permute-start(f32[16,8,128]{2,1,0:T(8,128)S(1)} %pack_history.1), channel_id=1, source_target_pairs={{0,1},{1,0},{2,3},{3,2},{4,5},{5,4},{6,7},{7,6},{8,9},{9,8},{10,11... | collective-permute-start | bytes 196616 | tf_op jit(solution)/shard_map/ppermute | solution.py:478
  9.7 9.2 %copy-start.3 = (f32[16,4,8,128]{3,2,1,0:T(8,128)}, f32[16,4,8,128]{3,2,1,0:T(8,128)S(1)}, u32[]{:S(2)}) copy-start(f32[16,4,8,128]{3,2,1,0:T(8,128)S(1)} %pad_maximum_fusion.1) | copy-start | bytes 786436
  9.7 8.4 %collective-permute-start.4 = (f32[16,32,128]{2,1,0:T(8,128)S(1)}, f32[16,32,128]{2,1,0:T(8,128)S(1)}, u32[]{:S(2)}, u32[]{:S(2)}) collective-permute-start(f32[16,32,128]{2,1,0:T(8,128)S(1)} %bitcast.42), channel_id=1, source_target_pairs={{4,8},{12,16},{20,24},{8,4},{16,12},{24,20},{5,9},{13,17},{21,25},... | collective-permute-start | bytes 786440 | tf_op jit(solution)/shard_map/ppermute | solution.py:578
  10.4 7.7 %collective-permute-start.3 = (f32[16,32,128]{2,1,0:T(8,128)S(1)}, f32[16,32,128]{2,1,0:T(8,128)S(1)}, u32[]{:S(2)}, u32[]{:S(2)}) collective-permute-start(f32[16,32,128]{2,1,0:T(8,128)S(1)} %bitcast.43), channel_id=1, source_target_pairs={{0,4},{4,0},{8,12},{12,8},{16,20},{20,16},{24,28},{28,24},{1,5},{5... | collective-permute-start | bytes 786440 | tf_op jit(solution)/shard_map/ppermute | solution.py:576
  13.5 13.0 %all-to-all-start = ((f32[32,8,128]{2,1,0:T(8,128)}), f32[32,8,128]{2,1,0:T(8,128)S(1)}, u32[]{:S(2)}, u32[]{:S(2)}) async-start(f32[32,8,128]{2,1,0:T(8,128)} %get-tuple-element.81), calls=%async_computation | async-start | bytes 262144 | tf_op jit(solution)/shard_map/all_to_all | solution.py:585
  18.1 0.8 copy-start.4
  18.1 0.8 copy-start.5
  18.9 7.6 %copy-start = (bf16[4,512,200]{1,2,0:T(8,128)(2,1)S(1)}, bf16[4,512,200]{1,2,0:T(8,128)(2,1)}, u32[]{:S(2)}) copy-start(bf16[4,512,200]{1,2,0:T(8,128)(2,1)} %param.21) | copy-start | bytes 2457604
  18.9 7.6 %copy-start.1 = (bf16[4,200,200]{2,1,0:T(8,128)(2,1)S(1)}, bf16[4,200,200]{2,1,0:T(8,128)(2,1)}, u32[]{:S(2)}) copy-start(bf16[4,200,200]{2,1,0:T(8,128)(2,1)} %refs_8_.31) | copy-start | bytes 960004
  18.9 7.6 %copy-start.2 = (f32[4,512]{1,0:T(4,128)S(1)}, f32[4,512]{1,0:T(4,128)}, u32[]{:S(2)}) copy-start(f32[4,512]{1,0:T(4,128)} %refs_9_.15) | copy-start | bytes 24580
  28.4 11.0 %all-to-all-start.1 = ((f32[32,8,128]{2,1,0:T(8,128)}), f32[32,8,128]{2,1,0:T(8,128)S(1)}, u32[]{:S(2)}, u32[]{:S(2)}) async-start(f32[32,8,128]{2,1,0:T(8,128)} %get-tuple-element.87), calls=%async_computation.1 | async-start | bytes 262144 | tf_op jit(solution)/shard_map/all_to_all | solution.py:585
  41.4 11.0 %all-to-all-start.2 = ((f32[32,8,128]{2,1,0:T(8,128)}), f32[32,8,128]{2,1,0:T(8,128)S(1)}, u32[]{:S(2)}, u32[]{:S(2)}) async-start(f32[32,8,128]{2,1,0:T(8,128)} %get-tuple-element.94), calls=%async_computation.2 | async-start | bytes 262144 | tf_op jit(solution)/shard_map/all_to_all | solution.py:585
  54.5 11.0 %all-to-all-start.3 = ((f32[32,8,128]{2,1,0:T(8,128)}), f32[32,8,128]{2,1,0:T(8,128)S(1)}, u32[]{:S(2)}, u32[]{:S(2)}) async-start(f32[32,8,128]{2,1,0:T(8,128)} %get-tuple-element.101), calls=%async_computation.3 | async-start | bytes 262144 | tf_op jit(solution)/shard_map/all_to_all | solution.py:585
  67.5 11.0 %all-to-all-start.4 = ((f32[32,8,128]{2,1,0:T(8,128)}), f32[32,8,128]{2,1,0:T(8,128)S(1)}, u32[]{:S(2)}, u32[]{:S(2)}) async-start(f32[32,8,128]{2,1,0:T(8,128)} %get-tuple-element.108), calls=%async_computation.4 | async-start | bytes 262144 | tf_op jit(solution)/shard_map/all_to_all | solution.py:585
  80.7 11.0 %all-to-all-start.5 = ((f32[32,8,128]{2,1,0:T(8,128)}), f32[32,8,128]{2,1,0:T(8,128)S(1)}, u32[]{:S(2)}, u32[]{:S(2)}) async-start(f32[32,8,128]{2,1,0:T(8,128)} %get-tuple-element.115), calls=%async_computation.5 | async-start | bytes 262144 | tf_op jit(solution)/shard_map/all_to_all | solution.py:585
  93.7 11.0 %all-to-all-start.6 = ((f32[32,8,128]{2,1,0:T(8,128)}), f32[32,8,128]{2,1,0:T(8,128)S(1)}, u32[]{:S(2)}, u32[]{:S(2)}) async-start(f32[32,8,128]{2,1,0:T(8,128)} %get-tuple-element.122), calls=%async_computation.6 | async-start | bytes 262144 | tf_op jit(solution)/shard_map/all_to_all | solution.py:585
  106.8 11.0 %all-to-all-start.7 = ((f32[32,8,128]{2,1,0:T(8,128)}), f32[32,8,128]{2,1,0:T(8,128)S(1)}, u32[]{:S(2)}, u32[]{:S(2)}) async-start(f32[32,8,128]{2,1,0:T(8,128)} %get-tuple-element.129), calls=%async_computation.7 | async-start | bytes 262144 | tf_op jit(solution)/shard_map/all_to_all | solution.py:585

commit v4 on v3

--- a/solution.py
+++ b/solution.py
@@ -9,7 +9,7 @@
 
 LANE = 128
 PACK = 16
-KEPT = 6
+KEPT = 8
 CHUNK = 3
 VMEM_LIMIT = 24 * 1024 * 1024
 HBM = pl.BlockSpec(memory_space=pltpu.HBM)
@@ -633,7 +633,7 @@
             out_shape.append(pltpu.HBM(table_shape, f32))
         whole = len(out_shape)
         if not last:
-            out_shape += [shaped((dir_rows, LANE), f32), shaped(message.shape, f32)]
+            out_shape += [shaped((dir_rows, LANE), f32), pltpu.VMEM(message.shape, f32)]
         results = pl.pallas_call(
             functools.partial(march_kernel, step, last, clus_count, slab_count, lags),
             out_shape=out_shape,

time: 120 us -> 121 us (level)
  transfers between devices with their start and end apart: 13 -> 13, of which waited for: 9 -> 10; matrix products, arithmetic and copies ran while one was open for 0% -> 0% of each run, Pallas kernels for 31% -> 30%
where the time goes in v4:
time: 121 us; the launch traced here: 120 us
  Pallas kernels  52.7 us (44%)
  waiting for transfers between devices  34.6 us (29%)
  starting transfers between devices  31.2 us (26%)
    all_to_all x8, waiting for transfers between devices, local(): arrived = lax.all_to_all(message, ('slab', 'clus'), 0, 0, tiled=True)  33.8 us
    pallas_call x8, Pallas kernels, local(): pl.pallas_call(functools.partial(near_kernel, step, last, clus_count, lag...  32.6 us
    all_to_all x8, starting transfers between devices, local(): arrived = lax.all_to_all(message, ('slab', 'clus'), 0, 0, tiled=True)  22.8 us
    pallas_call x8, Pallas kernels, local(): pl.pallas_call(functools.partial(march_kernel, step, last, clus_count, sl...  16 us
    ppermute x3, starting transfers between devices, exchange(): return lax.ppermute(block, axis, [(i, i ^ bit) for i in range(count)])  4.6 us
    pallas_call x1, Pallas kernels, local(): pl.pallas_call(functools.partial(begin_kernel, clus_count), out_shape=(sh...  3.3 us
    ppermute x1, starting transfers between devices, local(): lax.ppermute(mid, 'slab', [(i, i ^ 1) for i in range(slab_count)])  3.15 us
  transfers between devices with their start and end apart: 13, of which 10 were waited for; matrix products, arithmetic and copies ran while one was open for 0% of the time, Pallas kernels for 30%

profile of v4, /device:TPU:0, one launch (start us, length us, event | category | flops | bytes accessed | tf_op | source)
XLA Modules:
  0.0 119.8 jit_solution(4066223259238320030)
XLA Ops:
  0.9 4.0 %collective-permute-start.2 = (f32[16,8,128]{2,1,0:T(8,128)S(1)}, f32[16,8,128]{2,1,0:T(8,128)S(1)}, u32[]{:S(2)}, u32[]{:S(2)}) collective-permute-start(f32[16,8,128]{2,1,0:T(8,128)S(1)} %pack_history.1), channel_id=1, source_target_pairs={{0,3},{1,2},{2,1},{3,0},{4,7},{5,6},{6,5},{7,4},{8,11},{9,10},{10,... | collective-permute-start | bytes 196616 | tf_op jit(solution)/shard_map/ppermute | solution.py:478
  5.5 3.3 %past_spectra.1 = (f32[16,4,128]{2,1,0:T(4,128)S(1)}, f32[32,8,128]{2,1,0:T(8,128)}, f32[256,4,128]{2,1,0:T(4,128)S(1)}, f32[32,4,128]{2,1,0:T(4,128)S(1)}, bf16...) custom-call(bf16[4,200,512]{2,1,0:T(8,128)(2,1)} %bitcast.24, ...), custom_call_target="tpu_custom_call" | custom-call | tf_op jit(solution)/shard_map/past_spectra/pallas_call | solution.py:539
  10.4 3.2 %collective-permute-start.3 = (f32[16,32,128]{2,1,0:T(8,128)S(1)}, f32[16,32,128]{2,1,0:T(8,128)S(1)}, u32[]{:S(2)}, u32[]{:S(2)}) collective-permute-start(f32[16,32,128]{2,1,0:T(8,128)S(1)} %bitcast.43), channel_id=1, source_target_pairs={{0,4},{4,0},{8,12},{12,8},{16,20},{20,16},{24,28},{28,24},{1,5},{5... | collective-permute-start | bytes 786440 | tf_op jit(solution)/shard_map/ppermute | solution.py:576
  13.5 4.6 %all-to-all-start = ((f32[32,8,128]{2,1,0:T(8,128)}), f32[32,8,128]{2,1,0:T(8,128)S(1)}, u32[]{:S(2)}, u32[]{:S(2)}) async-start(f32[32,8,128]{2,1,0:T(8,128)} %get-tuple-element.81), calls=%async_computation | async-start | bytes 262144 | tf_op jit(solution)/shard_map/all_to_all | solution.py:585
  19.0 4.3 %known_near_field_0.1 = (f32[4,200]{1,0:T(4,128)S(1)}, f32[48,256]{1,0:T(8,128)S(1)}, f32[32,4,128]{2,1,0:T(4,128)S(1)}, f32[24,96,128]{2,1,0:T(8,128)}) custom-call(s32[4,12]{1,0:T(4,128)} %refs_0_.15, s32[4]{0:T(128)} %refs_1_.15, s32[4,12]{1,0:T(4,128)} %refs_2_.15, f32[4,12]{1,0:T(4,128)} %refs_3_.15, s32[772]{0:T(1024)} %get-tuple-element.70.refs_4_, ...), custom_call_target="tpu_custom_call" | custom-call | flops 3840000 | bytes 5760000 | tf_op jit(solution)/shard_map/known_near_field_0/pallas_call | solution.py:593
  23.3 3.3 %all-to-all-done = f32[32,8,128]{2,1,0:T(8,128)S(1)} async-done(((f32[32,8,128]{2,1,0:T(8,128)}), f32[32,8,128]{2,1,0:T(8,128)S(1)}, u32[]{:S(2)}, u32[]{:S(2)}) %all-to-all-start) | async-done | bytes 131104 | tf_op jit(solution)/shard_map/all_to_all | solution.py:585
  28.5 2.6 %all-to-all-start.1 = ((f32[32,8,128]{2,1,0:T(8,128)}), f32[32,8,128]{2,1,0:T(8,128)S(1)}, u32[]{:S(2)}, u32[]{:S(2)}) async-start(f32[32,8,128]{2,1,0:T(8,128)} %get-tuple-element.87), calls=%async_computation.1 | async-start | bytes 262144 | tf_op jit(solution)/shard_map/all_to_all | solution.py:585
  31.1 4.0 %known_near_field_1.1 = (f32[4,200]{1,0:T(4,128)S(1)}, f32[48,256]{1,0:T(8,128)S(1)}, f32[32,4,128]{2,1,0:T(4,128)S(1)}) custom-call(s32[4,12]{1,0:T(4,128)} %refs_0_.15, s32[4]{0:T(128)} %refs_1_.15, s32[4,12]{1,0:T(4,128)} %refs_2_.15, f32[4,12]{1,0:T(4,128)} %refs_3_.15, s32[772]{0:T(1024)} %get-tuple-element.70.refs_4_, f32[8,4,200]{2,1,0:T(4,128)} %refs_5_.15, ...), custom_call_target="tpu_custom_call" | custom-call | flops 3840000 | bytes 5760000 | tf_op jit(solution)/shard_map/known_near_field_1/pallas_call | solution.py:593
  35.1 4.4 %all-to-all-done.1 = f32[32,8,128]{2,1,0:T(8,128)S(1)} async-done(((f32[32,8,128]{2,1,0:T(8,128)}), f32[32,8,128]{2,1,0:T(8,128)S(1)}, u32[]{:S(2)}, u32[]{:S(2)}) %all-to-all-start.1) | async-done | bytes 131104 | tf_op jit(solution)/shard_map/all_to_all | solution.py:585
  41.6 2.6 %all-to-all-start.2 = ((f32[32,8,128]{2,1,0:T(8,128)}), f32[32,8,128]{2,1,0:T(8,128)S(1)}, u32[]{:S(2)}, u32[]{:S(2)}) async-start(f32[32,8,128]{2,1,0:T(8,128)} %get-tuple-element.94), calls=%async_computation.2 | async-start | bytes 262144 | tf_op jit(solution)/shard_map/all_to_all | solution.py:585
  44.2 4.0 %known_near_field_2.1 = (f32[4,200]{1,0:T(4,128)S(1)}, f32[48,256]{1,0:T(8,128)S(1)}, f32[32,4,128]{2,1,0:T(4,128)S(1)}) custom-call(s32[4,12]{1,0:T(4,128)} %refs_0_.15, s32[4]{0:T(128)} %refs_1_.15, s32[4,12]{1,0:T(4,128)} %refs_2_.15, f32[4,12]{1,0:T(4,128)} %refs_3_.15, s32[772]{0:T(1024)} %get-tuple-element.70.refs_4_, f32[8,4,200]{2,1,0:T(4,128)} %refs_5_.15, ...), custom_call_target="tpu_custom_call" | custom-call | flops 3840000 | bytes 5760000 | tf_op jit(solution)/shard_map/known_near_field_2/pallas_call | solution.py:593
  48.2 4.4 %all-to-all-done.2 = f32[32,8,128]{2,1,0:T(8,128)S(1)} async-done(((f32[32,8,128]{2,1,0:T(8,128)}), f32[32,8,128]{2,1,0:T(8,128)S(1)}, u32[]{:S(2)}, u32[]{:S(2)}) %all-to-all-start.2) | async-done | bytes 131104 | tf_op jit(solution)/shard_map/all_to_all | solution.py:585
  54.7 2.6 %all-to-all-start.3 = ((f32[32,8,128]{2,1,0:T(8,128)}), f32[32,8,128]{2,1,0:T(8,128)S(1)}, u32[]{:S(2)}, u32[]{:S(2)}) async-start(f32[32,8,128]{2,1,0:T(8,128)} %get-tuple-element.101), calls=%async_computation.3 | async-start | bytes 262144 | tf_op jit(solution)/shard_map/all_to_all | solution.py:585
  57.3 4.0 %known_near_field_3.1 = (f32[4,200]{1,0:T(4,128)S(1)}, f32[48,256]{1,0:T(8,128)S(1)}, f32[32,4,128]{2,1,0:T(4,128)S(1)}) custom-call(s32[4,12]{1,0:T(4,128)} %refs_0_.15, s32[4]{0:T(128)} %refs_1_.15, s32[4,12]{1,0:T(4,128)} %refs_2_.15, f32[4,12]{1,0:T(4,128)} %refs_3_.15, s32[772]{0:T(1024)} %get-tuple-element.70.refs_4_, f32[8,4,200]{2,1,0:T(4,128)} %refs_5_.15, ...), custom_call_target="tpu_custom_call" | custom-call | flops 3840000 | bytes 5760000 | tf_op jit(solution)/shard_map/known_near_field_3/pallas_call | solution.py:593
  61.3 4.4 %all-to-all-done.3 = f32[32,8,128]{2,1,0:T(8,128)S(1)} async-done(((f32[32,8,128]{2,1,0:T(8,128)}), f32[32,8,128]{2,1,0:T(8,128)S(1)}, u32[]{:S(2)}, u32[]{:S(2)}) %all-to-all-start.3) | async-done | bytes 131104 | tf_op jit(solution)/shard_map/all_to_all | solution.py:585
  67.8 2.6 %all-to-all-start.4 = ((f32[32,8,128]{2,1,0:T(8,128)}), f32[32,8,128]{2,1,0:T(8,128)S(1)}, u32[]{:S(2)}, u32[]{:S(2)}) async-start(f32[32,8,128]{2,1,0:T(8,128)} %get-tuple-element.108), calls=%async_computation.4 | async-start | bytes 262144 | tf_op jit(solution)/shard_map/all_to_all | solution.py:585
  70.4 4.1 %known_near_field_4.1 = (f32[4,200]{1,0:T(4,128)S(1)}, f32[48,256]{1,0:T(8,128)S(1)}, f32[32,4,128]{2,1,0:T(4,128)S(1)}) custom-call(s32[4,12]{1,0:T(4,128)} %refs_0_.15, s32[4]{0:T(128)} %refs_1_.15, s32[4,12]{1,0:T(4,128)} %refs_2_.15, f32[4,12]{1,0:T(4,128)} %refs_3_.15, s32[772]{0:T(1024)} %get-tuple-element.70.refs_4_, f32[8,4,200]{2,1,0:T(4,128)} %refs_5_.15, ...), custom_call_target="tpu_custom_call" | custom-call | flops 3840000 | bytes 5760000 | tf_op jit(solution)/shard_map/known_near_field_4/pallas_call | solution.py:593
  74.5 4.3 %all-to-all-done.4 = f32[32,8,128]{2,1,0:T(8,128)S(1)} async-done(((f32[32,8,128]{2,1,0:T(8,128)}), f32[32,8,128]{2,1,0:T(8,128)S(1)}, u32[]{:S(2)}, u32[]{:S(2)}) %all-to-all-start.4) | async-done | bytes 131104 | tf_op jit(solution)/shard_map/all_to_all | solution.py:585
  83.6 4.0 %known_near_field_5.1 = (f32[4,200]{1,0:T(4,128)S(1)}, f32[48,256]{1,0:T(8,128)S(1)}, f32[32,4,128]{2,1,0:T(4,128)S(1)}) custom-call(s32[4,12]{1,0:T(4,128)} %refs_0_.15, s32[4]{0:T(128)} %refs_1_.15, s32[4,12]{1,0:T(4,128)} %refs_2_.15, f32[4,12]{1,0:T(4,128)} %refs_3_.15, s32[772]{0:T(1024)} %get-tuple-element.70.refs_4_, f32[8,4,200]{2,1,0:T(4,128)} %refs_5_.15, ...), custom_call_target="tpu_custom_call" | custom-call | flops 3840000 | bytes 5760000 | tf_op jit(solution)/shard_map/known_near_field_5/pallas_call | solution.py:593
  87.7 4.4 %all-to-all-done.5 = f32[32,8,128]{2,1,0:T(8,128)S(1)} async-done(((f32[32,8,128]{2,1,0:T(8,128)}), f32[32,8,128]{2,1,0:T(8,128)S(1)}, u32[]{:S(2)}, u32[]{:S(2)}) %all-to-all-start.5) | async-done | bytes 131104 | tf_op jit(solution)/shard_map/all_to_all | solution.py:585
  96.7 4.1 %known_near_field_6.1 = (f32[4,200]{1,0:T(4,128)S(1)}, f32[48,256]{1,0:T(8,128)S(1)}, f32[32,4,128]{2,1,0:T(4,128)S(1)}) custom-call(s32[4,12]{1,0:T(4,128)} %refs_0_.15, s32[4]{0:T(128)} %refs_1_.15, s32[4,12]{1,0:T(4,128)} %refs_2_.15, f32[4,12]{1,0:T(4,128)} %refs_3_.15, s32[772]{0:T(1024)} %get-tuple-element.70.refs_4_, f32[8,4,200]{2,1,0:T(4,128)} %refs_5_.15, ...), custom_call_target="tpu_custom_call" | custom-call | flops 3840000 | bytes 5760000 | tf_op jit(solution)/shard_map/known_near_field_6/pallas_call | solution.py:593
  100.8 4.3 %all-to-all-done.6 = f32[32,8,128]{2,1,0:T(8,128)S(1)} async-done(((f32[32,8,128]{2,1,0:T(8,128)}), f32[32,8,128]{2,1,0:T(8,128)S(1)}, u32[]{:S(2)}, u32[]{:S(2)}) %all-to-all-start.6) | async-done | bytes 131104 | tf_op jit(solution)/shard_map/all_to_all | solution.py:585
  109.8 4.1 %known_near_field_7.1 = (f32[4,200]{1,0:T(4,128)S(1)}, f32[48,256]{1,0:T(8,128)S(1)}, f32[32,4,128]{2,1,0:T(4,128)S(1)}) custom-call(s32[4,12]{1,0:T(4,128)} %refs_0_.15, s32[4]{0:T(128)} %refs_1_.15, s32[4,12]{1,0:T(4,128)} %refs_2_.15, f32[4,12]{1,0:T(4,128)} %refs_3_.15, s32[772]{0:T(1024)} %get-tuple-element.70.refs_4_, f32[8,4,200]{2,1,0:T(4,128)} %refs_5_.15, ...), custom_call_target="tpu_custom_call" | custom-call | flops 3840000 | bytes 5760000 | tf_op jit(solution)/shard_map/known_near_field_7/pallas_call | solution.py:593
  113.9 4.3 %all-to-all-done.7 = f32[32,8,128]{2,1,0:T(8,128)S(1)} async-done(((f32[32,8,128]{2,1,0:T(8,128)}), f32[32,8,128]{2,1,0:T(8,128)S(1)}, u32[]{:S(2)}, u32[]{:S(2)}) %all-to-all-start.7) | async-done | bytes 131104 | tf_op jit(solution)/shard_map/all_to_all | solution.py:585
  (35 shorter events, 27.6 us)
Async XLA Ops:
  0.9 7.9 %collective-permute-start.2 = (f32[16,8,128]{2,1,0:T(8,128)S(1)}, f32[16,8,128]{2,1,0:T(8,128)S(1)}, u32[]{:S(2)}, u32[]{:S(2)}) collective-permute-start(f32[16,8,128]{2,1,0:T(8,128)S(1)} %pack_history.1), channel_id=1, source_target_pairs={{0,3},{1,2},{2,1},{3,0},{4,7},{5,6},{6,5},{7,4},{8,11},{9,10},{10,... | collective-permute-start | bytes 196616 | tf_op jit(solution)/shard_map/ppermute | solution.py:478
  4.8 4.3 %collective-permute-start.1 = (f32[16,8,128]{2,1,0:T(8,128)S(1)}, f32[16,8,128]{2,1,0:T(8,128)S(1)}, u32[]{:S(2)}, u32[]{:S(2)}) collective-permute-start(f32[16,8,128]{2,1,0:T(8,128)S(1)} %pack_history.1), channel_id=1, source_target_pairs={{0,2},{1,3},{2,0},{3,1},{4,6},{5,7},{6,4},{7,5},{8,10},{9,11},{10,... | collective-permute-start | bytes 196616 | tf_op jit(solution)/shard_map/ppermute | solution.py:478
  5.3 4.3 %collective-permute-start = (f32[16,8,128]{2,1,0:T(8,128)S(1)}, f32[16,8,128]{2,1,0:T(8,128)S(1)}, u32[]{:S(2)}, u32[]{:S(2)}) collective-permute-start(f32[16,8,128]{2,1,0:T(8,128)S(1)} %pack_history.1), channel_id=1, source_target_pairs={{0,1},{1,0},{2,3},{3,2},{4,5},{5,4},{6,7},{7,6},{8,9},{9,8},{10,11... | collective-permute-start | bytes 196616 | tf_op jit(solution)/shard_map/ppermute | solution.py:478
  9.7 9.3 %copy-start.3 = (f32[16,4,8,128]{3,2,1,0:T(8,128)}, f32[16,4,8,128]{3,2,1,0:T(8,128)S(1)}, u32[]{:S(2)}) copy-start(f32[16,4,8,128]{3,2,1,0:T(8,128)S(1)} %pad_maximum_fusion.1) | copy-start | bytes 786436
  9.7 8.5 %collective-permute-start.4 = (f32[16,32,128]{2,1,0:T(8,128)S(1)}, f32[16,32,128]{2,1,0:T(8,128)S(1)}, u32[]{:S(2)}, u32[]{:S(2)}) collective-permute-start(f32[16,32,128]{2,1,0:T(8,128)S(1)} %bitcast.42), channel_id=1, source_target_pairs={{4,8},{12,16},{20,24},{8,4},{16,12},{24,20},{5,9},{13,17},{21,25},... | collective-permute-start | bytes 786440 | tf_op jit(solution)/shard_map/ppermute | solution.py:578
  10.4 7.8 %collective-permute-start.3 = (f32[16,32,128]{2,1,0:T(8,128)S(1)}, f32[16,32,128]{2,1,0:T(8,128)S(1)}, u32[]{:S(2)}, u32[]{:S(2)}) collective-permute-start(f32[16,32,128]{2,1,0:T(8,128)S(1)} %bitcast.43), channel_id=1, source_target_pairs={{0,4},{4,0},{8,12},{12,8},{16,20},{20,16},{24,28},{28,24},{1,5},{5... | collective-permute-start | bytes 786440 | tf_op jit(solution)/shard_map/ppermute | solution.py:576
  13.5 13.1 %all-to-all-start = ((f32[32,8,128]{2,1,0:T(8,128)}), f32[32,8,128]{2,1,0:T(8,128)S(1)}, u32[]{:S(2)}, u32[]{:S(2)}) async-start(f32[32,8,128]{2,1,0:T(8,128)} %get-tuple-element.81), calls=%async_computation | async-start | bytes 262144 | tf_op jit(solution)/shard_map/all_to_all | solution.py:585
  18.2 0.8 copy-start.4
  18.2 0.8 copy-start.5
  19.0 7.6 %copy-start = (bf16[4,512,200]{1,2,0:T(8,128)(2,1)S(1)}, bf16[4,512,200]{1,2,0:T(8,128)(2,1)}, u32[]{:S(2)}) copy-start(bf16[4,512,200]{1,2,0:T(8,128)(2,1)} %param.21) | copy-start | bytes 2457604
  19.0 7.6 %copy-start.1 = (bf16[4,200,200]{2,1,0:T(8,128)(2,1)S(1)}, bf16[4,200,200]{2,1,0:T(8,128)(2,1)}, u32[]{:S(2)}) copy-start(bf16[4,200,200]{2,1,0:T(8,128)(2,1)} %refs_8_.31) | copy-start | bytes 960004
  19.0 7.6 %copy-start.2 = (f32[4,512]{1,0:T(4,128)S(1)}, f32[4,512]{1,0:T(4,128)}, u32[]{:S(2)}) copy-start(f32[4,512]{1,0:T(4,128)} %refs_9_.15) | copy-start | bytes 24580
  28.5 11.0 %all-to-all-start.1 = ((f32[32,8,128]{2,1,0:T(8,128)}), f32[32,8,128]{2,1,0:T(8,128)S(1)}, u32[]{:S(2)}, u32[]{:S(2)}) async-start(f32[32,8,128]{2,1,0:T(8,128)} %get-tuple-element.87), calls=%async_computation.1 | async-start | bytes 262144 | tf_op jit(solution)/shard_map/all_to_all | solution.py:585
  41.6 11.0 %all-to-all-start.2 = ((f32[32,8,128]{2,1,0:T(8,128)}), f32[32,8,128]{2,1,0:T(8,128)S(1)}, u32[]{:S(2)}, u32[]{:S(2)}) async-start(f32[32,8,128]{2,1,0:T(8,128)} %get-tuple-element.94), calls=%async_computation.2 | async-start | bytes 262144 | tf_op jit(solution)/shard_map/all_to_all | solution.py:585
  54.7 11.0 %all-to-all-start.3 = ((f32[32,8,128]{2,1,0:T(8,128)}), f32[32,8,128]{2,1,0:T(8,128)S(1)}, u32[]{:S(2)}, u32[]{:S(2)}) async-start(f32[32,8,128]{2,1,0:T(8,128)} %get-tuple-element.101), calls=%async_computation.3 | async-start | bytes 262144 | tf_op jit(solution)/shard_map/all_to_all | solution.py:585
  67.8 11.0 %all-to-all-start.4 = ((f32[32,8,128]{2,1,0:T(8,128)}), f32[32,8,128]{2,1,0:T(8,128)S(1)}, u32[]{:S(2)}, u32[]{:S(2)}) async-start(f32[32,8,128]{2,1,0:T(8,128)} %get-tuple-element.108), calls=%async_computation.4 | async-start | bytes 262144 | tf_op jit(solution)/shard_map/all_to_all | solution.py:585
  81.0 11.0 %all-to-all-start.5 = ((f32[32,8,128]{2,1,0:T(8,128)}), f32[32,8,128]{2,1,0:T(8,128)S(1)}, u32[]{:S(2)}, u32[]{:S(2)}) async-start(f32[32,8,128]{2,1,0:T(8,128)} %get-tuple-element.115), calls=%async_computation.5 | async-start | bytes 262144 | tf_op jit(solution)/shard_map/all_to_all | solution.py:585
  94.1 11.0 %all-to-all-start.6 = ((f32[32,8,128]{2,1,0:T(8,128)}), f32[32,8,128]{2,1,0:T(8,128)S(1)}, u32[]{:S(2)}, u32[]{:S(2)}) async-start(f32[32,8,128]{2,1,0:T(8,128)} %get-tuple-element.122), calls=%async_computation.6 | async-start | bytes 262144 | tf_op jit(solution)/shard_map/all_to_all | solution.py:585
  107.2 11.0 %all-to-all-start.7 = ((f32[32,8,128]{2,1,0:T(8,128)}), f32[32,8,128]{2,1,0:T(8,128)S(1)}, u32[]{:S(2)}, u32[]{:S(2)}) async-start(f32[32,8,128]{2,1,0:T(8,128)} %get-tuple-element.129), calls=%async_computation.7 | async-start | bytes 262144 | tf_op jit(solution)/shard_map/all_to_all | solution.py:585

commit v5 on v4

--- a/solution.py
+++ b/solution.py
@@ -38,7 +38,7 @@
     )
 
 
-def pack_kernel(history, packed):
+def pack_kernel(history, copies_out, packed, sems):
     lags, clusters, unknowns = history.shape
     halves = packed.shape[1] // clusters
     for half in range(halves):
@@ -49,6 +49,8 @@
                 [part, jnp.zeros((lags, clusters, LANE - (high - low)), jnp.float32)], axis=2
             )
         packed[:, half * clusters : (half + 1) * clusters, :] = part
+    peers = copies_out.shape[0]
+    wait_all(start_all([(packed, copies_out.at[peer]) for peer in range(peers)], sems))
 
 
 def in_hbm(*arrays):
@@ -221,11 +223,11 @@
         table_in, base, blended, known = refs[:4]
         refs = refs[4:]
     else:
-        mid, core_swap, chip_swap, base, blended, known, table_out = refs[:7]
-        refs = refs[7:]
+        plane, chip_swap, base, blended, known, table_out = refs[:6]
+        refs = refs[6:]
     (
         table, held, tall, field, spectra, incident, near_idx, near_cnt, near_lag, near_frac,
-        old_plan, sems, more_sems, out_sem,
+        old_plan, sems, more_sems, wide_sems, out_sem,
     ) = refs
     clusters, slots = near_idx.shape
     unknowns = incident.shape[1]
@@ -247,10 +249,19 @@
         wide_pairs = [(table_in.at[pl.ds(0, now)], table.at[pl.ds(0, now)])]
     else:
         odd = lax.rem(slab, 2)
+        sides = [1 + core - odd for core in range(2)] + [2 * odd]
+        each = side_rows // clus_count
         wide_pairs = []
-        for source, side in ((mid, 1), (core_swap, 2 - 2 * odd), (chip_swap, 2 * odd)):
-            start = pl.multiple_of(side * side_rows, side_rows)
-            wide_pairs.append((source, table.at[pl.ds(0, lags), pl.ds(start, side_rows)]))
+        for number in range(3 * clus_count):
+            source = plane if number < 2 * clus_count else chip_swap
+            core, member = divmod(number, clus_count)
+            start = pl.multiple_of(sides[core] * side_rows + member * each, each)
+            wide_pairs.append(
+                (
+                    source.at[number % source.shape[0]],
+                    table.at[pl.ds(0, lags), pl.ds(start, each)],
+                )
+            )
     small = start_all(
         (
             (near_cnt_in, near_cnt), (near_idx_in, near_idx), (near_lag_in, near_lag),
@@ -258,11 +269,11 @@
         ),
         more_sems,
     )
-    wide = start_all(wide_pairs, more_sems.at[pl.ds(4, 3)])
+    wide = start_all(wide_pairs, wide_sems)
     pairs = [(incident_in.at[step], incident)]
     if not last:
         pairs.append((old_plan_in, old_plan))
-    others = start_all(pairs, more_sems.at[pl.ds(7, 2)])
+    others = start_all(pairs, more_sems.at[pl.ds(4, 2)])
     for cluster in range(clusters):
         block_copy(cluster, 0).start()
     tall[...] = jnp.zeros(tall.shape, jnp.float32)
@@ -473,11 +484,6 @@
     wait_all(kept_copies)
 
 
-def exchange(block, axis, bit):
-    count = lax.axis_size(axis)
-    return lax.ppermute(block, axis, [(i, i ^ bit) for i in range(count)])
-
-
 def local(
     incident,
     history,
@@ -507,24 +513,26 @@
     far_entries = groups * entries
     slab_count = lax.axis_size("slab")
     clus_count = lax.axis_size("clus")
-    clus_index = lax.axis_index("clus")
     params = pltpu.CompilerParams(vmem_limit_bytes=VMEM_LIMIT)
     rays = jnp.swapaxes(rays, 1, 2)
 
+    dma = pltpu.SemaphoreType.DMA
+    peers = 2 * clus_count
     packed = pl.pallas_call(
         pack_kernel,
-        out_shape=shaped((lags, msg_rows, LANE), f32),
+        out_shape=shaped((peers, lags, msg_rows, LANE), f32),
         in_specs=[VMEM],
-        out_specs=VMEM,
+        out_specs=HBM,
+        scratch_shapes=[pltpu.VMEM((lags, msg_rows, LANE), f32), dma((peers,))],
         compiler_params=params,
         name="pack_history",
     )(*in_hbm(history))
-    pieces = [packed] + [exchange(packed, "clus", bit) for bit in range(1, clus_count)]
-    stacked = jnp.stack(pieces, axis=0)
-    mid = jnp.stack(
-        [lax.dynamic_index_in_dim(stacked, clus_index ^ c, 0, False) for c in range(clus_count)],
-        axis=1,
-    )
+    planes = [list(range(first, first + peers)) for first in range(0, groups, peers)]
+    plane = lax.all_to_all(
+        packed, ("slab", "clus"), 0, 0, tiled=True, axis_index_groups=planes
+    )
+    own_side = lax.rem(lax.axis_index("slab"), 2) * clus_count
+    own = lax.dynamic_slice_in_dim(plane, own_side, clus_count, axis=0)
 
     smem_lists = [
         pltpu.SMEM((clusters, slots), i32),
@@ -532,7 +540,6 @@
         pltpu.SMEM((clusters, slots), i32),
         pltpu.SMEM((clusters, slots), f32),
     ]
-    dma = pltpu.SemaphoreType.DMA
     near_lists = in_hbm(near_idx, near_cnt, near_lag, near_frac)
     (blocks,) = in_hbm(near_blocks)
     spectra, message, weights, fresh_weights, kept, kept_weight, kept_plan, near_plan, old_plan = (
@@ -571,11 +578,9 @@
             blocks,
         )
     )
-    mid, message = lax.optimization_barrier((mid, message))
-    mid = mid.reshape(lags, clus_count * msg_rows, LANE)
-    core_swap = lax.ppermute(mid, "slab", [(i, i ^ 1) for i in range(slab_count)])
+    own, message = lax.optimization_barrier((own, message))
     chips = [(i, i + 1) for i in range(1, slab_count - 1, 2)]
-    chip_swap = lax.ppermute(mid, "slab", chips + [(b, a) for a, b in chips])
+    chip_swap = lax.ppermute(own, "slab", chips + [(b, a) for a, b in chips])
 
     table_shape = (lags + steps, 3 * clus_count * msg_rows, LANE)
     tall_rows = -(-slots // PACK) * PACK
@@ -589,7 +594,7 @@
             shaped((near_entries, wide), f32),
             shaped((groups, dir_rows, LANE), f32),
         ]
-        currents_in = in_hbm(table) if step else in_hbm(mid, core_swap, chip_swap)
+        currents_in = in_hbm(table) if step else in_hbm(plane, chip_swap)
         results = pl.pallas_call(
             functools.partial(near_kernel, step, last, clus_count, lags),
             out_shape=out_shape if step else out_shape + [pltpu.HBM(table_shape, f32)],
@@ -605,7 +610,8 @@
                 *smem_lists,
                 pltpu.SMEM(old_plan.shape, i32),
                 dma((near_entries,)),
-                dma((9,)),
+                dma((6,)),
+                dma((3 * clus_count,)),
                 dma,
             ],
             compiler_params=params,
@@ -633,7 +639,7 @@
             out_shape.append(pltpu.HBM(table_shape, f32))
         whole = len(out_shape)
         if not last:
-            out_shape += [shaped((dir_rows, LANE), f32), pltpu.VMEM(message.shape, f32)]
+            out_shape += [shaped((dir_rows, LANE), f32), shaped(message.shape, f32)]
         results = pl.pallas_call(
             functools.partial(march_kernel, step, last, clus_count, slab_count, lags),
             out_shape=out_shape,

time: 121 us -> 125 us (1.033)
  Pallas kernels: 52.7 us -> 55.9 us
  waiting for transfers between devices: 34.6 us -> 37.5 us
    ppermute x5 -> x1, starting transfers between devices: 8.43 us -> 0.68 us  [local(): chip_swap = lax.ppermute(own, 'slab', chips + [(b, a) for a, b in chips])]
    all_to_all x0 -> x1, waiting for transfers between devices: none -> 5.77 us  [local(): lax.all_to_all(packed, ('slab', 'clus'), 0, 0, tiled=True, axis_index_gro...]
    all_to_all x0 -> x1, starting transfers between devices: none -> 5.18 us  [local(): lax.all_to_all(packed, ('slab', 'clus'), 0, 0, tiled=True, axis_index_gro...]
    pallas_call x8, Pallas kernels: 32.6 us -> 34.8 us  [local(): pl.pallas_call(functools.partial(near_kernel, step, last, clus_count, lag...]
    all_to_all x8, waiting for transfers between devices: 33.8 us -> 31.7 us  [local(): arrived = lax.all_to_all(message, ('slab', 'clus'), 0, 0, tiled=True)]
    all_to_all x8, starting transfers between devices: 22.8 us -> 24.1 us  [local(): arrived = lax.all_to_all(message, ('slab', 'clus'), 0, 0, tiled=True)]
  transfers between devices with their start and end apart: 13 -> 10, of which waited for: 10 -> 9; matrix products, arithmetic and copies ran while one was open for 0% -> 0% of each run, Pallas kernels for 30% -> 31%
where the time goes in v5:
time: 125 us; the launch traced here: 124 us
  Pallas kernels  55.9 us (45%)
  waiting for transfers between devices  37.5 us (30%)
  starting transfers between devices  30 us (24%)
    pallas_call x8, Pallas kernels, local(): pl.pallas_call(functools.partial(near_kernel, step, last, clus_count, lag...  34.8 us
    all_to_all x8, waiting for transfers between devices, local(): arrived = lax.all_to_all(message, ('slab', 'clus'), 0, 0, tiled=True)  31.7 us
    all_to_all x8, starting transfers between devices, local(): arrived = lax.all_to_all(message, ('slab', 'clus'), 0, 0, tiled=True)  24.1 us
    pallas_call x8, Pallas kernels, local(): pl.pallas_call(functools.partial(march_kernel, step, last, clus_count, sl...  15.9 us
    all_to_all x1, waiting for transfers between devices, local(): lax.all_to_all(packed, ('slab', 'clus'), 0, 0, tiled=True, axis_index_gro...  5.77 us
    all_to_all x1, starting transfers between devices, local(): lax.all_to_all(packed, ('slab', 'clus'), 0, 0, tiled=True, axis_index_gro...  5.18 us
    pallas_call x1, Pallas kernels, local(): pl.pallas_call(functools.partial(begin_kernel, clus_count), out_shape=(sh...  3.49 us
  transfers between devices with their start and end apart: 10, of which 9 were waited for; matrix products, arithmetic and copies ran while one was open for 0% of the time, Pallas kernels for 31%

profile of v5, /device:TPU:0, one launch (start us, length us, event | category | flops | bytes accessed | tf_op | source)
XLA Modules:
  0.0 124.4 jit_solution(7084292675161694146)
XLA Ops:
  1.7 5.2 %all-to-all-start = ((f32[8,16,8,128]{3,2,1,0:T(8,128)}), f32[8,16,8,128]{3,2,1,0:T(8,128)S(1)}, u32[]{:S(2)}, u32[]{:S(2)}) async-start(f32[8,16,8,128]{3,2,1,0:T(8,128)} %pack_history.1), calls=%async_computation | async-start | bytes 1048576 | tf_op jit(solution)/shard_map/all_to_all | solution.py:531
  6.9 3.5 %past_spectra.1 = (f32[16,4,128]{2,1,0:T(4,128)S(1)}, f32[32,8,128]{2,1,0:T(8,128)}, f32[256,4,128]{2,1,0:T(4,128)S(1)}, f32[32,4,128]{2,1,0:T(4,128)S(1)}, bf16...) custom-call(bf16[4,200,512]{2,1,0:T(8,128)(2,1)} %bitcast.11, ...), custom_call_target="tpu_custom_call" | custom-call | tf_op jit(solution)/shard_map/past_spectra/pallas_call | solution.py:546
  10.4 5.8 %all-to-all-done.refs_9_ = f32[8,16,8,128]{3,2,1,0:T(8,128)S(1)} async-done(((f32[8,16,8,128]{3,2,1,0:T(8,128)}), f32[8,16,8,128]{3,2,1,0:T(8,128)S(1)}, u32[]{:S(2)}, u32[]{:S(2)}) %all-to-all-start) | async-done | bytes 524320 | tf_op jit(solution)/shard_map/all_to_all | solution.py:531
  16.9 6.0 %all-to-all-start.1 = ((f32[32,8,128]{2,1,0:T(8,128)}), f32[32,8,128]{2,1,0:T(8,128)S(1)}, u32[]{:S(2)}, u32[]{:S(2)}) async-start(f32[32,8,128]{2,1,0:T(8,128)} %get-tuple-element.81), calls=%async_computation.1 | async-start | bytes 262144 | tf_op jit(solution)/shard_map/all_to_all | solution.py:590
  23.6 4.6 %known_near_field_0.1 = (f32[4,200]{1,0:T(4,128)S(1)}, f32[48,256]{1,0:T(8,128)S(1)}, f32[32,4,128]{2,1,0:T(4,128)S(1)}, f32[24,96,128]{2,1,0:T(8,128)}) custom-call(s32[4,12]{1,0:T(4,128)} %refs_0_.15, s32[4]{0:T(128)} %refs_1_.15, s32[4,12]{1,0:T(4,128)} %refs_2_.15, f32[4,12]{1,0:T(4,128)} %refs_3_.15, s32[772]{0:T(1024)} %get-tuple-element.70.refs_4_, ...), custom_call_target="tpu_custom_call" | custom-call | flops 3840000 | bytes 5760000 | tf_op jit(solution)/shard_map/known_near_field_0/pallas_call | solution.py:598
  28.2 3.1 %all-to-all-done.1 = f32[32,8,128]{2,1,0:T(8,128)S(1)} async-done(((f32[32,8,128]{2,1,0:T(8,128)}), f32[32,8,128]{2,1,0:T(8,128)S(1)}, u32[]{:S(2)}, u32[]{:S(2)}) %all-to-all-start.1) | async-done | bytes 131104 | tf_op jit(solution)/shard_map/all_to_all | solution.py:590
  35.8 4.3 %known_near_field_1.1 = (f32[4,200]{1,0:T(4,128)S(1)}, f32[48,256]{1,0:T(8,128)S(1)}, f32[32,4,128]{2,1,0:T(4,128)S(1)}) custom-call(s32[4,12]{1,0:T(4,128)} %refs_0_.15, s32[4]{0:T(128)} %refs_1_.15, s32[4,12]{1,0:T(4,128)} %refs_2_.15, f32[4,12]{1,0:T(4,128)} %refs_3_.15, s32[772]{0:T(1024)} %get-tuple-element.70.refs_4_, f32[8,4,200]{2,1,0:T(4,128)} %refs_5_.15, ...), custom_call_target="tpu_custom_call" | custom-call | flops 3840000 | bytes 5760000 | tf_op jit(solution)/shard_map/known_near_field_1/pallas_call | solution.py:598
  40.0 4.1 %all-to-all-done.2 = f32[32,8,128]{2,1,0:T(8,128)S(1)} async-done(((f32[32,8,128]{2,1,0:T(8,128)}), f32[32,8,128]{2,1,0:T(8,128)S(1)}, u32[]{:S(2)}, u32[]{:S(2)}) %all-to-all-start.2) | async-done | bytes 131104 | tf_op jit(solution)/shard_map/all_to_all | solution.py:590
  46.3 2.6 %all-to-all-start.3 = ((f32[32,8,128]{2,1,0:T(8,128)}), f32[32,8,128]{2,1,0:T(8,128)S(1)}, u32[]{:S(2)}, u32[]{:S(2)}) async-start(f32[32,8,128]{2,1,0:T(8,128)} %get-tuple-element.94), calls=%async_computation.3 | async-start | bytes 262144 | tf_op jit(solution)/shard_map/all_to_all | solution.py:590
  48.9 4.3 %known_near_field_2.1 = (f32[4,200]{1,0:T(4,128)S(1)}, f32[48,256]{1,0:T(8,128)S(1)}, f32[32,4,128]{2,1,0:T(4,128)S(1)}) custom-call(s32[4,12]{1,0:T(4,128)} %refs_0_.15, s32[4]{0:T(128)} %refs_1_.15, s32[4,12]{1,0:T(4,128)} %refs_2_.15, f32[4,12]{1,0:T(4,128)} %refs_3_.15, s32[772]{0:T(1024)} %get-tuple-element.70.refs_4_, f32[8,4,200]{2,1,0:T(4,128)} %refs_5_.15, ...), custom_call_target="tpu_custom_call" | custom-call | flops 3840000 | bytes 5760000 | tf_op jit(solution)/shard_map/known_near_field_2/pallas_call | solution.py:598
  53.1 4.1 %all-to-all-done.3 = f32[32,8,128]{2,1,0:T(8,128)S(1)} async-done(((f32[32,8,128]{2,1,0:T(8,128)}), f32[32,8,128]{2,1,0:T(8,128)S(1)}, u32[]{:S(2)}, u32[]{:S(2)}) %all-to-all-start.3) | async-done | bytes 131104 | tf_op jit(solution)/shard_map/all_to_all | solution.py:590
  59.3 2.6 %all-to-all-start.4 = ((f32[32,8,128]{2,1,0:T(8,128)}), f32[32,8,128]{2,1,0:T(8,128)S(1)}, u32[]{:S(2)}, u32[]{:S(2)}) async-start(f32[32,8,128]{2,1,0:T(8,128)} %get-tuple-element.101), calls=%async_computation.4 | async-start | bytes 262144 | tf_op jit(solution)/shard_map/all_to_all | solution.py:590
  61.9 4.3 %known_near_field_3.1 = (f32[4,200]{1,0:T(4,128)S(1)}, f32[48,256]{1,0:T(8,128)S(1)}, f32[32,4,128]{2,1,0:T(4,128)S(1)}) custom-call(s32[4,12]{1,0:T(4,128)} %refs_0_.15, s32[4]{0:T(128)} %refs_1_.15, s32[4,12]{1,0:T(4,128)} %refs_2_.15, f32[4,12]{1,0:T(4,128)} %refs_3_.15, s32[772]{0:T(1024)} %get-tuple-element.70.refs_4_, f32[8,4,200]{2,1,0:T(4,128)} %refs_5_.15, ...), custom_call_target="tpu_custom_call" | custom-call | flops 3840000 | bytes 5760000 | tf_op jit(solution)/shard_map/known_near_field_3/pallas_call | solution.py:598
  66.3 4.1 %all-to-all-done.4 = f32[32,8,128]{2,1,0:T(8,128)S(1)} async-done(((f32[32,8,128]{2,1,0:T(8,128)}), f32[32,8,128]{2,1,0:T(8,128)S(1)}, u32[]{:S(2)}, u32[]{:S(2)}) %all-to-all-start.4) | async-done | bytes 131104 | tf_op jit(solution)/shard_map/all_to_all | solution.py:590
  72.4 2.6 %all-to-all-start.5 = ((f32[32,8,128]{2,1,0:T(8,128)}), f32[32,8,128]{2,1,0:T(8,128)S(1)}, u32[]{:S(2)}, u32[]{:S(2)}) async-start(f32[32,8,128]{2,1,0:T(8,128)} %get-tuple-element.108), calls=%async_computation.5 | async-start | bytes 262144 | tf_op jit(solution)/shard_map/all_to_all | solution.py:590
  75.0 4.3 %known_near_field_4.1 = (f32[4,200]{1,0:T(4,128)S(1)}, f32[48,256]{1,0:T(8,128)S(1)}, f32[32,4,128]{2,1,0:T(4,128)S(1)}) custom-call(s32[4,12]{1,0:T(4,128)} %refs_0_.15, s32[4]{0:T(128)} %refs_1_.15, s32[4,12]{1,0:T(4,128)} %refs_2_.15, f32[4,12]{1,0:T(4,128)} %refs_3_.15, s32[772]{0:T(1024)} %get-tuple-element.70.refs_4_, f32[8,4,200]{2,1,0:T(4,128)} %refs_5_.15, ...), custom_call_target="tpu_custom_call" | custom-call | flops 3840000 | bytes 5760000 | tf_op jit(solution)/shard_map/known_near_field_4/pallas_call | solution.py:598
  79.4 4.1 %all-to-all-done.5 = f32[32,8,128]{2,1,0:T(8,128)S(1)} async-done(((f32[32,8,128]{2,1,0:T(8,128)}), f32[32,8,128]{2,1,0:T(8,128)S(1)}, u32[]{:S(2)}, u32[]{:S(2)}) %all-to-all-start.5) | async-done | bytes 131104 | tf_op jit(solution)/shard_map/all_to_all | solution.py:590
  85.6 2.6 %all-to-all-start.6 = ((f32[32,8,128]{2,1,0:T(8,128)}), f32[32,8,128]{2,1,0:T(8,128)S(1)}, u32[]{:S(2)}, u32[]{:S(2)}) async-start(f32[32,8,128]{2,1,0:T(8,128)} %get-tuple-element.115), calls=%async_computation.6 | async-start | bytes 262144 | tf_op jit(solution)/shard_map/all_to_all | solution.py:590
  88.2 4.3 %known_near_field_5.1 = (f32[4,200]{1,0:T(4,128)S(1)}, f32[48,256]{1,0:T(8,128)S(1)}, f32[32,4,128]{2,1,0:T(4,128)S(1)}) custom-call(s32[4,12]{1,0:T(4,128)} %refs_0_.15, s32[4]{0:T(128)} %refs_1_.15, s32[4,12]{1,0:T(4,128)} %refs_2_.15, f32[4,12]{1,0:T(4,128)} %refs_3_.15, s32[772]{0:T(1024)} %get-tuple-element.70.refs_4_, f32[8,4,200]{2,1,0:T(4,128)} %refs_5_.15, ...), custom_call_target="tpu_custom_call" | custom-call | flops 3840000 | bytes 5760000 | tf_op jit(solution)/shard_map/known_near_field_5/pallas_call | solution.py:598
  92.6 4.1 %all-to-all-done.6 = f32[32,8,128]{2,1,0:T(8,128)S(1)} async-done(((f32[32,8,128]{2,1,0:T(8,128)}), f32[32,8,128]{2,1,0:T(8,128)S(1)}, u32[]{:S(2)}, u32[]{:S(2)}) %all-to-all-start.6) | async-done | bytes 131104 | tf_op jit(solution)/shard_map/all_to_all | solution.py:590
  101.3 4.4 %known_near_field_6.1 = (f32[4,200]{1,0:T(4,128)S(1)}, f32[48,256]{1,0:T(8,128)S(1)}, f32[32,4,128]{2,1,0:T(4,128)S(1)}) custom-call(s32[4,12]{1,0:T(4,128)} %refs_0_.15, s32[4]{0:T(128)} %refs_1_.15, s32[4,12]{1,0:T(4,128)} %refs_2_.15, f32[4,12]{1,0:T(4,128)} %refs_3_.15, s32[772]{0:T(1024)} %get-tuple-element.70.refs_4_, f32[8,4,200]{2,1,0:T(4,128)} %refs_5_.15, ...), custom_call_target="tpu_custom_call" | custom-call | flops 3840000 | bytes 5760000 | tf_op jit(solution)/shard_map/known_near_field_6/pallas_call | solution.py:598
  105.7 4.0 %all-to-all-done.7 = f32[32,8,128]{2,1,0:T(8,128)S(1)} async-done(((f32[32,8,128]{2,1,0:T(8,128)}), f32[32,8,128]{2,1,0:T(8,128)S(1)}, u32[]{:S(2)}, u32[]{:S(2)}) %all-to-all-start.7) | async-done | bytes 131104 | tf_op jit(solution)/shard_map/all_to_all | solution.py:590
  114.4 4.3 %known_near_field_7.1 = (f32[4,200]{1,0:T(4,128)S(1)}, f32[48,256]{1,0:T(8,128)S(1)}, f32[32,4,128]{2,1,0:T(4,128)S(1)}) custom-call(s32[4,12]{1,0:T(4,128)} %refs_0_.15, s32[4]{0:T(128)} %refs_1_.15, s32[4,12]{1,0:T(4,128)} %refs_2_.15, f32[4,12]{1,0:T(4,128)} %refs_3_.15, s32[772]{0:T(1024)} %get-tuple-element.70.refs_4_, f32[8,4,200]{2,1,0:T(4,128)} %refs_5_.15, ...), custom_call_target="tpu_custom_call" | custom-call | flops 3840000 | bytes 5760000 | tf_op jit(solution)/shard_map/known_near_field_7/pallas_call | solution.py:598
  118.7 4.1 %all-to-all-done.8 = f32[32,8,128]{2,1,0:T(8,128)S(1)} async-done(((f32[32,8,128]{2,1,0:T(8,128)}), f32[32,8,128]{2,1,0:T(8,128)S(1)}, u32[]{:S(2)}, u32[]{:S(2)}) %all-to-all-start.8) | async-done | bytes 131104 | tf_op jit(solution)/shard_map/all_to_all | solution.py:590
  (25 shorter events, 26.8 us)
Async XLA Ops:
  1.7 14.4 %all-to-all-start = ((f32[8,16,8,128]{3,2,1,0:T(8,128)}), f32[8,16,8,128]{3,2,1,0:T(8,128)S(1)}, u32[]{:S(2)}, u32[]{:S(2)}) async-start(f32[8,16,8,128]{3,2,1,0:T(8,128)} %pack_history.1), calls=%async_computation | async-start | bytes 1048576 | tf_op jit(solution)/shard_map/all_to_all | solution.py:531
  16.2 7.4 %copy-start.3 = (f32[8,16,8,128]{3,2,1,0:T(8,128)}, f32[8,16,8,128]{3,2,1,0:T(8,128)S(1)}, u32[]{:S(2)}) copy-start(f32[8,16,8,128]{3,2,1,0:T(8,128)S(1)} %all-to-all-done.refs_9_) | copy-start | bytes 1572868
  16.2 6.7 %collective-permute-start = (f32[4,16,8,128]{3,2,1,0:T(8,128)S(1)}, f32[4,16,8,128]{3,2,1,0:T(8,128)S(1)}, u32[]{:S(2)}, u32[]{:S(2)}) collective-permute-start(f32[4,16,8,128]{3,2,1,0:T(8,128)S(1)} %constant_dynamic-slice_fusion), channel_id=1, source_target_pairs={{4,8},{12,16},{20,24},{8,4},{16,12},{24,20},{5,9},{13,17},{21,25},... | collective-permute-start | bytes 786440 | tf_op jit(solution)/shard_map/ppermute | solution.py:583
  16.9 14.4 %all-to-all-start.1 = ((f32[32,8,128]{2,1,0:T(8,128)}), f32[32,8,128]{2,1,0:T(8,128)S(1)}, u32[]{:S(2)}, u32[]{:S(2)}) async-start(f32[32,8,128]{2,1,0:T(8,128)} %get-tuple-element.81), calls=%async_computation.1 | async-start | bytes 262144 | tf_op jit(solution)/shard_map/all_to_all | solution.py:590
  22.9 0.7 copy-start.4
  23.6 7.7 %copy-start = (bf16[4,512,200]{1,2,0:T(8,128)(2,1)S(1)}, bf16[4,512,200]{1,2,0:T(8,128)(2,1)}, u32[]{:S(2)}) copy-start(bf16[4,512,200]{1,2,0:T(8,128)(2,1)} %param.21) | copy-start | bytes 2457604
  23.6 7.7 %copy-start.1 = (bf16[4,200,200]{2,1,0:T(8,128)(2,1)S(1)}, bf16[4,200,200]{2,1,0:T(8,128)(2,1)}, u32[]{:S(2)}) copy-start(bf16[4,200,200]{2,1,0:T(8,128)(2,1)} %refs_8_.31) | copy-start | bytes 960004
  23.6 7.7 %copy-start.2 = (f32[4,512]{1,0:T(4,128)S(1)}, f32[4,512]{1,0:T(4,128)}, u32[]{:S(2)}) copy-start(f32[4,512]{1,0:T(4,128)} %refs_9_.15) | copy-start | bytes 24580
  33.2 11.0 %all-to-all-start.2 = ((f32[32,8,128]{2,1,0:T(8,128)}), f32[32,8,128]{2,1,0:T(8,128)S(1)}, u32[]{:S(2)}, u32[]{:S(2)}) async-start(f32[32,8,128]{2,1,0:T(8,128)} %get-tuple-element.87), calls=%async_computation.2 | async-start | bytes 262144 | tf_op jit(solution)/shard_map/all_to_all | solution.py:590
  46.3 11.0 %all-to-all-start.3 = ((f32[32,8,128]{2,1,0:T(8,128)}), f32[32,8,128]{2,1,0:T(8,128)S(1)}, u32[]{:S(2)}, u32[]{:S(2)}) async-start(f32[32,8,128]{2,1,0:T(8,128)} %get-tuple-element.94), calls=%async_computation.3 | async-start | bytes 262144 | tf_op jit(solution)/shard_map/all_to_all | solution.py:590
  59.3 11.0 %all-to-all-start.4 = ((f32[32,8,128]{2,1,0:T(8,128)}), f32[32,8,128]{2,1,0:T(8,128)S(1)}, u32[]{:S(2)}, u32[]{:S(2)}) async-start(f32[32,8,128]{2,1,0:T(8,128)} %get-tuple-element.101), calls=%async_computation.4 | async-start | bytes 262144 | tf_op jit(solution)/shard_map/all_to_all | solution.py:590
  72.4 11.0 %all-to-all-start.5 = ((f32[32,8,128]{2,1,0:T(8,128)}), f32[32,8,128]{2,1,0:T(8,128)S(1)}, u32[]{:S(2)}, u32[]{:S(2)}) async-start(f32[32,8,128]{2,1,0:T(8,128)} %get-tuple-element.108), calls=%async_computation.5 | async-start | bytes 262144 | tf_op jit(solution)/shard_map/all_to_all | solution.py:590
  85.6 11.0 %all-to-all-start.6 = ((f32[32,8,128]{2,1,0:T(8,128)}), f32[32,8,128]{2,1,0:T(8,128)S(1)}, u32[]{:S(2)}, u32[]{:S(2)}) async-start(f32[32,8,128]{2,1,0:T(8,128)} %get-tuple-element.115), calls=%async_computation.6 | async-start | bytes 262144 | tf_op jit(solution)/shard_map/all_to_all | solution.py:590
  98.7 11.0 %all-to-all-start.7 = ((f32[32,8,128]{2,1,0:T(8,128)}), f32[32,8,128]{2,1,0:T(8,128)S(1)}, u32[]{:S(2)}, u32[]{:S(2)}) async-start(f32[32,8,128]{2,1,0:T(8,128)} %get-tuple-element.122), calls=%async_computation.7 | async-start | bytes 262144 | tf_op jit(solution)/shard_map/all_to_all | solution.py:590
  111.8 11.0 %all-to-all-start.8 = ((f32[32,8,128]{2,1,0:T(8,128)}), f32[32,8,128]{2,1,0:T(8,128)S(1)}, u32[]{:S(2)}, u32[]{:S(2)}) async-start(f32[32,8,128]{2,1,0:T(8,128)} %get-tuple-element.129), calls=%async_computation.8 | async-start | bytes 262144 | tf_op jit(solution)/shard_map/all_to_all | solution.py:590

commit v6 on v4

--- a/solution.py
+++ b/solution.py
@@ -51,6 +51,28 @@
         packed[:, half * clusters : (half + 1) * clusters, :] = part
 
 
+def join_tails(tails, size):
+    lane = lax.broadcasted_iota(jnp.int32, (1, LANE), 1)
+    spare = LANE - size
+    rest = tails[3:4]
+    return jnp.concatenate(
+        [
+            jnp.where(lane < size, tails[0:1], pltpu.roll(rest, size, 1)),
+            jnp.where(lane < size, tails[1:2], pltpu.roll(rest, size - spare, 1)),
+            tails[2:3],
+        ],
+        axis=0,
+    )
+
+
+def last_tail(first, second, size):
+    lane = lax.broadcasted_iota(jnp.int32, (1, LANE), 1)
+    spare = LANE - size
+    return jnp.where(
+        lane < spare, pltpu.roll(first, spare, 1), pltpu.roll(second, 2 * spare, 1)
+    )
+
+
 def in_hbm(*arrays):
     return [pltpu.with_memory_space_constraint(array, pltpu.HBM) for array in arrays]
 
@@ -91,7 +113,7 @@
     near_lag_in, near_frac_in, blocks,
     spectra, message, weights, fresh_weights, kept, kept_weight, kept_plan, near_plan, old_plan,
     rays, history, shift, trans, far_idx, far_lag, near_idx, near_cnt, near_lag, near_frac,
-    far_list, sem, sems,
+    far_list, outgoing, sem, sems,
 ):
     small = start_all(
         (
@@ -108,7 +130,7 @@
     dir_rows = spectra.shape[1]
     entries, groups = far_idx.shape
     slots = near_idx.shape[1]
-    halves = message.shape[1] // clusters
+    halves = pl.cdiv(unknowns, LANE)
     myself = lax.axis_index("slab") * clus_count + lax.axis_index("clus")
 
     def kept_copy(place, entry):
@@ -120,7 +142,7 @@
     kept_weight[...] = jnp.zeros(kept_weight.shape, jnp.float32)
     kept_plan[...] = jnp.zeros(kept_plan.shape, jnp.int32)
     lane = lax.broadcasted_iota(jnp.int32, (1, LANE), 1)
-    message[...] = jnp.zeros(message.shape, jnp.float32)
+    outgoing[...] = jnp.zeros(outgoing.shape, jnp.float32)
     fresh_weights[...] = jnp.zeros(fresh_weights.shape, jnp.float32)
     wait_all(small)
     near_plan[0] = 0
@@ -199,16 +221,19 @@
 
     def add_past(place, carry):
         group, lag = far_list[2 * place], far_list[2 * place + 1]
-        message[group, :dir_rows, :] += weights[place] * spectra[lags - lag]
+        outgoing[group, :dir_rows, :] += weights[place] * spectra[lags - lag]
         return carry
 
     lax.fori_loop(0, counts[0], add_past, 0)
+    send = pltpu.make_async_copy(outgoing, message.at[:, :, 0, :], sems.at[0])
+    send.start()
 
     def finish(place, carry):
         kept_copy(place, near_plan[3 * place + 1]).wait()
         return carry
 
     lax.fori_loop(0, jnp.minimum(near_plan[0], KEPT), finish, 0)
+    send.wait()
 
 
 def near_kernel(step, last, clus_count, lags, *refs):
@@ -371,36 +396,45 @@
     else:
         output, spectrum, message = refs[13:16]
         refs = refs[16:]
-    near_plan, current, values, extra, field, sem, sems = refs
+    near_plan, current, values, extra, field, window, outgoing, sem, sems = refs
     clusters, unknowns = base.shape
     slots = blocks.shape[1]
     groups, dir_rows = fresh_weights.shape[:2]
-    rows_each = arrived.shape[0] // groups
-    halves = rows_each // clusters
-    side_rows = clus_count * rows_each
+    sent_rows = arrived.shape[0] // groups
+    halves = pl.cdiv(unknowns, LANE)
+    rows_each = halves * clusters
+    tail = unknowns - LANE
     slab = lax.axis_index("slab")
     which = lax.broadcasted_iota(jnp.int32, (clusters, unknowns), 0)
-    kept_copies = []
+    first_row = (slab - 1) * clus_count * rows_each
+    if step:
+        for member in range(3 * clus_count):
+            side, place = divmod(member, clus_count)
+            other = jnp.clip(slab + (side - 1), 0, slab_count - 1)
+            start = (other * clus_count + place) * sent_rows
+            for row in range(sent_rows):
+                window[member * rows_each + row : member * rows_each + row + 1, :] = arrived[
+                    start + row
+                ]
+            window[(member + 1) * rows_each - 1 : (member + 1) * rows_each, :] = last_tail(
+                arrived[start + clusters], arrived[start + clusters + 1], tail
+            )
+    keep = None
     if step and not last:
-        for side in range(3):
-            other = jnp.clip(slab + (side - 1), 0, slab_count - 1)
-            copy = pltpu.make_async_copy(
-                arrived.at[pl.ds(pl.multiple_of(other * side_rows, side_rows), side_rows)],
-                table.at[lags + step - 1, pl.ds(side * side_rows, side_rows)],
-                sems.at[1 + side],
-            )
-            copy.start()
-            kept_copies.append(copy)
+        keep = pltpu.make_async_copy(window, table.at[lags + step - 1], sems.at[2])
+        keep.start()
 
     def is_near(group):
         return jnp.abs(group // clus_count - slab) <= 1
 
-    sums = [jnp.zeros((dir_rows, LANE), jnp.float32) for _ in range(4)]
+    sums = [jnp.zeros((1, LANE), jnp.float32) for _ in range(2 * dir_rows)]
     for group in range(groups):
-        first = group * rows_each
-        sums[group % 4] += jnp.where(is_near(group), 0.0, arrived[first : first + dir_rows, :])
-    incoming = (sums[0] + sums[1]) + (sums[2] + sums[3])
-    row_in = jnp.concatenate([incoming[r : r + 1] for r in range(dir_rows)], axis=1)
+        near = is_near(group)
+        for row in range(dir_rows):
+            sums[2 * row + group % 2] += jnp.where(near, 0.0, arrived[group * sent_rows + row])
+    row_in = jnp.concatenate(
+        [sums[2 * row] + sums[2 * row + 1] for row in range(dir_rows)], axis=1
+    )
     inbound = (shift[...] * row_in).astype(jnp.bfloat16)
     far = jnp.zeros((clusters, unknowns), jnp.float32)
     for cluster in range(clusters):
@@ -409,7 +443,8 @@
 
     def fresh_row(place, entry, row):
         newest = jnp.concatenate(
-            [arrived[pl.ds(row + half * clusters, 1), :] for half in range(halves)], axis=1
+            [window[pl.ds(row + half * clusters - first_row, 1), :] for half in range(halves)],
+            axis=1,
         )
         return blended[pl.ds(entry, 1), :] + kept_weight[pl.ds(place, 1), :] * newest
 
@@ -418,7 +453,8 @@
         count = plan[0, 3]
         values[...] = jnp.zeros(values.shape, jnp.float32)
         for place in range(KEPT):
-            values[place : place + 1, :] = fresh_row(place, plan[place, 0], plan[place, 2])
+            row = jnp.where(place < count, plan[place, 2], first_row)
+            values[place : place + 1, :] = fresh_row(place, plan[place, 0], row)
         rows = values[...].astype(jnp.bfloat16)[:, :unknowns]
         for place in range(KEPT):
             product = dot_t(rows, kept[place])[place : place + 1]
@@ -465,12 +501,17 @@
             ray_vals = jnp.where(which_dir == cluster, dot(rounded, rays[cluster]), ray_vals)
         newest = rows_of(jnp.sum(ray_vals * shift[...], axis=0, keepdims=True), dir_rows)
         spectrum[...] = newest
+        tails = join_tails(own[clusters:], tail)
         for group in range(groups):
             far_sum = known[group] + fresh_weights[group] * newest
-            message[group, :dir_rows, :] = jnp.where(is_near(group), own[:dir_rows], far_sum)
-            message[group, dir_rows:, :] = own[dir_rows:]
+            outgoing[group, :dir_rows, :] = jnp.where(is_near(group), own[:dir_rows], far_sum)
+            outgoing[group, dir_rows:, :] = tails
+        send = pltpu.make_async_copy(outgoing, message.at[:, :, 0, :], sems.at[1])
+        send.start()
+        send.wait()
     out_copy.wait()
-    wait_all(kept_copies)
+    if keep is not None:
+        keep.wait()
 
 
 def exchange(block, axis, bit):
@@ -502,6 +543,7 @@
     dir_rows = dirs // LANE
     halves = pl.cdiv(unknowns, LANE)
     msg_rows = halves * clusters
+    sent_rows = msg_rows - 1
     wide = halves * LANE
     near_entries = clusters * slots
     far_entries = groups * entries
@@ -540,7 +582,7 @@
             functools.partial(begin_kernel, clus_count),
             out_shape=(
                 shaped((lags, dir_rows, LANE), f32),
-                shaped((groups, msg_rows, LANE), f32),
+                pltpu.HBM((groups, sent_rows, 1, LANE), f32),
                 shaped((far_entries, dir_rows, LANE), f32),
                 shaped((groups, dir_rows, LANE), f32),
                 shaped((KEPT, unknowns, unknowns), bf16),
@@ -550,7 +592,7 @@
                 pltpu.HBM((3 * far_entries + 4,), i32),
             ),
             in_specs=[HBM] * 11,
-            out_specs=[VMEM] * 7 + [SMEM] * 2,
+            out_specs=[VMEM, HBM] + [VMEM] * 5 + [SMEM] * 2,
             scratch_shapes=[
                 pltpu.VMEM(rays.shape, bf16),
                 pltpu.VMEM(history.shape, f32),
@@ -560,6 +602,7 @@
                 pltpu.SMEM((entries, groups), i32),
                 *smem_lists,
                 pltpu.SMEM((2 * far_entries + 2,), i32),
+                pltpu.VMEM((groups, sent_rows, LANE), f32),
                 dma,
                 dma((10,)),
             ],
@@ -583,7 +626,7 @@
     for step in range(steps):
         last = step == steps - 1
         arrived = lax.all_to_all(message, ("slab", "clus"), 0, 0, tiled=True)
-        arrived = arrived.reshape(groups * msg_rows, LANE)
+        arrived = arrived.reshape(groups * sent_rows, 1, LANE)
         out_shape = [
             shaped((clusters, unknowns), f32),
             shaped((near_entries, wide), f32),
@@ -633,18 +676,20 @@
             out_shape.append(pltpu.HBM(table_shape, f32))
         whole = len(out_shape)
         if not last:
-            out_shape += [shaped((dir_rows, LANE), f32), pltpu.VMEM(message.shape, f32)]
+            out_shape += [shaped((dir_rows, LANE), f32), pltpu.HBM(message.shape, f32)]
         results = pl.pallas_call(
             functools.partial(march_kernel, step, last, clus_count, slab_count, lags),
             out_shape=out_shape,
             in_specs=[HBM] + [VMEM] * 11 + [HBM] * (1 + len(changed)),
-            out_specs=[HBM] * whole + [VMEM] * (len(out_shape) - whole),
+            out_specs=[HBM] * whole + ([] if last else [VMEM, HBM]),
             scratch_shapes=[
                 pltpu.SMEM(near_plan.shape, i32),
                 pltpu.VMEM((clusters, unknowns), f32),
                 pltpu.VMEM((8, wide), f32),
                 pltpu.VMEM((unknowns, unknowns), bf16),
                 pltpu.VMEM((clusters, unknowns), f32),
+                pltpu.VMEM((3 * clus_count * msg_rows, LANE), f32),
+                pltpu.VMEM((groups, sent_rows, LANE), f32),
                 dma,
                 dma((5,)),
             ],

time: 121 us -> 117 us (0.967)
  waiting for transfers between devices: 34.6 us -> 31.1 us
    all_to_all x8, waiting for transfers between devices: 33.8 us -> 31.1 us  [local(): arrived = lax.all_to_all(message, ('slab', 'clus'), 0, 0, tiled=True)]
    pallas_call x8, Pallas kernels: 16 us -> 13.3 us  [local(): pl.pallas_call(functools.partial(march_kernel, step, last, clus_count, sl...]
    pallas_call x1, Pallas kernels: 3.3 us -> 4.63 us  [local(): pl.pallas_call(functools.partial(begin_kernel, clus_count), out_shape=(sh...]
  transfers between devices with their start and end apart: 13 -> 13, of which waited for: 10 -> 8; matrix products, arithmetic and copies ran while one was open for 0% -> 0% of each run, Pallas kernels for 30% -> 33%
where the time goes in v6:
time: 117 us; the launch traced here: 116 us
  Pallas kernels  52.2 us (45%)
  starting transfers between devices  31.7 us (27%)
  waiting for transfers between devices  31.1 us (27%)
    pallas_call x8, Pallas kernels, local(): pl.pallas_call(functools.partial(near_kernel, step, last, clus_count, lag...  33.4 us
    all_to_all x8, waiting for transfers between devices, local(): arrived = lax.all_to_all(message, ('slab', 'clus'), 0, 0, tiled=True)  31.1 us
    all_to_all x8, starting transfers between devices, local(): arrived = lax.all_to_all(message, ('slab', 'clus'), 0, 0, tiled=True)  23.3 us
    pallas_call x8, Pallas kernels, local(): pl.pallas_call(functools.partial(march_kernel, step, last, clus_count, sl...  13.3 us
    pallas_call x1, Pallas kernels, local(): pl.pallas_call(functools.partial(begin_kernel, clus_count), out_shape=(sh...  4.63 us
    ppermute x3, starting transfers between devices, exchange(): return lax.ppermute(block, axis, [(i, i ^ bit) for i in range(count)])  4.6 us
    ppermute x1, starting transfers between devices, local(): lax.ppermute(mid, 'slab', [(i, i ^ 1) for i in range(slab_count)])  3.2 us
  transfers between devices with their start and end apart: 13, of which 8 were waited for; matrix products, arithmetic and copies ran while one was open for 0% of the time, Pallas kernels for 33%

profile of v6, /device:TPU:0, one launch (start us, length us, event | category | flops | bytes accessed | tf_op | source)
XLA Modules:
  0.0 116.4 jit_solution(13427612736272531160)
XLA Ops:
  0.9 4.0 %collective-permute-start.2 = (f32[16,8,128]{2,1,0:T(8,128)S(1)}, f32[16,8,128]{2,1,0:T(8,128)S(1)}, u32[]{:S(2)}, u32[]{:S(2)}) collective-permute-start(f32[16,8,128]{2,1,0:T(8,128)S(1)} %pack_history.1), channel_id=1, source_target_pairs={{0,3},{1,2},{2,1},{3,0},{4,7},{5,6},{6,5},{7,4},{8,11},{9,10},{10,... | collective-permute-start | bytes 196616 | tf_op jit(solution)/shard_map/ppermute | solution.py:519
  5.5 4.6 %past_spectra.1 = (f32[16,4,128]{2,1,0:T(4,128)S(1)}, f32[32,7,1,128]{3,2,1,0:T(1,128)}, f32[256,4,128]{2,1,0:T(4,128)S(1)}, f32[32,4,128]{2,1,0:T(4,128)S(1)}, ...) custom-call(bf16[4,200,512]{2,1,0:T(8,128)(2,1)} %bitcast.24, ...), custom_call_target="tpu_custom_call" | custom-call | tf_op jit(solution)/shard_map/past_spectra/pallas_call | solution.py:581
  10.9 3.2 %collective-permute-start.3 = (f32[16,32,128]{2,1,0:T(8,128)S(1)}, f32[16,32,128]{2,1,0:T(8,128)S(1)}, u32[]{:S(2)}, u32[]{:S(2)}) collective-permute-start(f32[16,32,128]{2,1,0:T(8,128)S(1)} %bitcast.43), channel_id=1, source_target_pairs={{0,4},{4,0},{8,12},{12,8},{16,20},{20,16},{24,28},{28,24},{1,5},{5... | collective-permute-start | bytes 786440 | tf_op jit(solution)/shard_map/ppermute | solution.py:619
  14.1 4.8 %all-to-all-start = ((f32[32,7,1,128]{3,2,1,0:T(1,128)}), f32[32,7,1,128]{3,2,1,0:T(1,128)S(1)}, u32[]{:S(2)}, u32[]{:S(2)}) async-start(f32[32,7,1,128]{3,2,1,0:T(1,128)} %get-tuple-element.81), calls=%async_computation | async-start | bytes 229376 | tf_op jit(solution)/shard_map/all_to_all | solution.py:628
  19.8 4.4 %known_near_field_0.1 = (f32[4,200]{1,0:T(4,128)S(1)}, f32[48,256]{1,0:T(8,128)S(1)}, f32[32,4,128]{2,1,0:T(4,128)S(1)}, f32[24,96,128]{2,1,0:T(8,128)}) custom-call(s32[4,12]{1,0:T(4,128)} %refs_0_.15, s32[4]{0:T(128)} %refs_1_.15, s32[4,12]{1,0:T(4,128)} %refs_2_.15, f32[4,12]{1,0:T(4,128)} %refs_3_.15, s32[772]{0:T(1024)} %get-tuple-element.70.refs_4_, ...), custom_call_target="tpu_custom_call" | custom-call | flops 3840000 | bytes 5760000 | tf_op jit(solution)/shard_map/known_near_field_0/pallas_call | solution.py:636
  24.2 2.9 %all-to-all-done = f32[32,7,1,128]{3,2,1,0:T(1,128)S(1)} async-done(((f32[32,7,1,128]{3,2,1,0:T(1,128)}), f32[32,7,1,128]{3,2,1,0:T(1,128)S(1)}, u32[]{:S(2)}, u32[]{:S(2)}) %all-to-all-start) | async-done | bytes 114720 | tf_op jit(solution)/shard_map/all_to_all | solution.py:628
  28.6 2.9 %all-to-all-start.1 = ((f32[32,7,1,128]{3,2,1,0:T(1,128)}), f32[32,7,1,128]{3,2,1,0:T(1,128)S(1)}, u32[]{:S(2)}, u32[]{:S(2)}) async-start(f32[32,7,1,128]{3,2,1,0:T(1,128)} %get-tuple-element.87), calls=%async_computation.1 | async-start | bytes 229376 | tf_op jit(solution)/shard_map/all_to_all | solution.py:628
  31.5 4.1 %known_near_field_1.1 = (f32[4,200]{1,0:T(4,128)S(1)}, f32[48,256]{1,0:T(8,128)S(1)}, f32[32,4,128]{2,1,0:T(4,128)S(1)}) custom-call(s32[4,12]{1,0:T(4,128)} %refs_0_.15, s32[4]{0:T(128)} %refs_1_.15, s32[4,12]{1,0:T(4,128)} %refs_2_.15, f32[4,12]{1,0:T(4,128)} %refs_3_.15, s32[772]{0:T(1024)} %get-tuple-element.70.refs_4_, f32[8,4,200]{2,1,0:T(4,128)} %refs_5_.15, ...), custom_call_target="tpu_custom_call" | custom-call | flops 3840000 | bytes 5760000 | tf_op jit(solution)/shard_map/known_near_field_1/pallas_call | solution.py:636
  35.6 4.1 %all-to-all-done.1 = f32[32,7,1,128]{3,2,1,0:T(1,128)S(1)} async-done(((f32[32,7,1,128]{3,2,1,0:T(1,128)}), f32[32,7,1,128]{3,2,1,0:T(1,128)S(1)}, u32[]{:S(2)}, u32[]{:S(2)}) %all-to-all-start.1) | async-done | bytes 114720 | tf_op jit(solution)/shard_map/all_to_all | solution.py:628
  41.4 2.6 %all-to-all-start.2 = ((f32[32,7,1,128]{3,2,1,0:T(1,128)}), f32[32,7,1,128]{3,2,1,0:T(1,128)S(1)}, u32[]{:S(2)}, u32[]{:S(2)}) async-start(f32[32,7,1,128]{3,2,1,0:T(1,128)} %get-tuple-element.94), calls=%async_computation.2 | async-start | bytes 229376 | tf_op jit(solution)/shard_map/all_to_all | solution.py:628
  44.0 4.1 %known_near_field_2.1 = (f32[4,200]{1,0:T(4,128)S(1)}, f32[48,256]{1,0:T(8,128)S(1)}, f32[32,4,128]{2,1,0:T(4,128)S(1)}) custom-call(s32[4,12]{1,0:T(4,128)} %refs_0_.15, s32[4]{0:T(128)} %refs_1_.15, s32[4,12]{1,0:T(4,128)} %refs_2_.15, f32[4,12]{1,0:T(4,128)} %refs_3_.15, s32[772]{0:T(1024)} %get-tuple-element.70.refs_4_, f32[8,4,200]{2,1,0:T(4,128)} %refs_5_.15, ...), custom_call_target="tpu_custom_call" | custom-call | flops 3840000 | bytes 5760000 | tf_op jit(solution)/shard_map/known_near_field_2/pallas_call | solution.py:636
  48.1 4.1 %all-to-all-done.2 = f32[32,7,1,128]{3,2,1,0:T(1,128)S(1)} async-done(((f32[32,7,1,128]{3,2,1,0:T(1,128)}), f32[32,7,1,128]{3,2,1,0:T(1,128)S(1)}, u32[]{:S(2)}, u32[]{:S(2)}) %all-to-all-start.2) | async-done | bytes 114720 | tf_op jit(solution)/shard_map/all_to_all | solution.py:628
  53.9 2.6 %all-to-all-start.3 = ((f32[32,7,1,128]{3,2,1,0:T(1,128)}), f32[32,7,1,128]{3,2,1,0:T(1,128)S(1)}, u32[]{:S(2)}, u32[]{:S(2)}) async-start(f32[32,7,1,128]{3,2,1,0:T(1,128)} %get-tuple-element.101), calls=%async_computation.3 | async-start | bytes 229376 | tf_op jit(solution)/shard_map/all_to_all | solution.py:628
  56.5 4.1 %known_near_field_3.1 = (f32[4,200]{1,0:T(4,128)S(1)}, f32[48,256]{1,0:T(8,128)S(1)}, f32[32,4,128]{2,1,0:T(4,128)S(1)}) custom-call(s32[4,12]{1,0:T(4,128)} %refs_0_.15, s32[4]{0:T(128)} %refs_1_.15, s32[4,12]{1,0:T(4,128)} %refs_2_.15, f32[4,12]{1,0:T(4,128)} %refs_3_.15, s32[772]{0:T(1024)} %get-tuple-element.70.refs_4_, f32[8,4,200]{2,1,0:T(4,128)} %refs_5_.15, ...), custom_call_target="tpu_custom_call" | custom-call | flops 3840000 | bytes 5760000 | tf_op jit(solution)/shard_map/known_near_field_3/pallas_call | solution.py:636
  60.6 4.1 %all-to-all-done.3 = f32[32,7,1,128]{3,2,1,0:T(1,128)S(1)} async-done(((f32[32,7,1,128]{3,2,1,0:T(1,128)}), f32[32,7,1,128]{3,2,1,0:T(1,128)S(1)}, u32[]{:S(2)}, u32[]{:S(2)}) %all-to-all-start.3) | async-done | bytes 114720 | tf_op jit(solution)/shard_map/all_to_all | solution.py:628
  66.5 2.6 %all-to-all-start.4 = ((f32[32,7,1,128]{3,2,1,0:T(1,128)}), f32[32,7,1,128]{3,2,1,0:T(1,128)S(1)}, u32[]{:S(2)}, u32[]{:S(2)}) async-start(f32[32,7,1,128]{3,2,1,0:T(1,128)} %get-tuple-element.108), calls=%async_computation.4 | async-start | bytes 229376 | tf_op jit(solution)/shard_map/all_to_all | solution.py:628
  69.1 4.3 %known_near_field_4.1 = (f32[4,200]{1,0:T(4,128)S(1)}, f32[48,256]{1,0:T(8,128)S(1)}, f32[32,4,128]{2,1,0:T(4,128)S(1)}) custom-call(s32[4,12]{1,0:T(4,128)} %refs_0_.15, s32[4]{0:T(128)} %refs_1_.15, s32[4,12]{1,0:T(4,128)} %refs_2_.15, f32[4,12]{1,0:T(4,128)} %refs_3_.15, s32[772]{0:T(1024)} %get-tuple-element.70.refs_4_, f32[8,4,200]{2,1,0:T(4,128)} %refs_5_.15, ...), custom_call_target="tpu_custom_call" | custom-call | flops 3840000 | bytes 5760000 | tf_op jit(solution)/shard_map/known_near_field_4/pallas_call | solution.py:636
  73.3 3.9 %all-to-all-done.4 = f32[32,7,1,128]{3,2,1,0:T(1,128)S(1)} async-done(((f32[32,7,1,128]{3,2,1,0:T(1,128)}), f32[32,7,1,128]{3,2,1,0:T(1,128)S(1)}, u32[]{:S(2)}, u32[]{:S(2)}) %all-to-all-start.4) | async-done | bytes 114720 | tf_op jit(solution)/shard_map/all_to_all | solution.py:628
  81.6 4.1 %known_near_field_5.1 = (f32[4,200]{1,0:T(4,128)S(1)}, f32[48,256]{1,0:T(8,128)S(1)}, f32[32,4,128]{2,1,0:T(4,128)S(1)}) custom-call(s32[4,12]{1,0:T(4,128)} %refs_0_.15, s32[4]{0:T(128)} %refs_1_.15, s32[4,12]{1,0:T(4,128)} %refs_2_.15, f32[4,12]{1,0:T(4,128)} %refs_3_.15, s32[772]{0:T(1024)} %get-tuple-element.70.refs_4_, f32[8,4,200]{2,1,0:T(4,128)} %refs_5_.15, ...), custom_call_target="tpu_custom_call" | custom-call | flops 3840000 | bytes 5760000 | tf_op jit(solution)/shard_map/known_near_field_5/pallas_call | solution.py:636
  85.7 4.0 %all-to-all-done.5 = f32[32,7,1,128]{3,2,1,0:T(1,128)S(1)} async-done(((f32[32,7,1,128]{3,2,1,0:T(1,128)}), f32[32,7,1,128]{3,2,1,0:T(1,128)S(1)}, u32[]{:S(2)}, u32[]{:S(2)}) %all-to-all-start.5) | async-done | bytes 114720 | tf_op jit(solution)/shard_map/all_to_all | solution.py:628
  94.1 4.2 %known_near_field_6.1 = (f32[4,200]{1,0:T(4,128)S(1)}, f32[48,256]{1,0:T(8,128)S(1)}, f32[32,4,128]{2,1,0:T(4,128)S(1)}) custom-call(s32[4,12]{1,0:T(4,128)} %refs_0_.15, s32[4]{0:T(128)} %refs_1_.15, s32[4,12]{1,0:T(4,128)} %refs_2_.15, f32[4,12]{1,0:T(4,128)} %refs_3_.15, s32[772]{0:T(1024)} %get-tuple-element.70.refs_4_, f32[8,4,200]{2,1,0:T(4,128)} %refs_5_.15, ...), custom_call_target="tpu_custom_call" | custom-call | flops 3840000 | bytes 5760000 | tf_op jit(solution)/shard_map/known_near_field_6/pallas_call | solution.py:636
  98.3 4.0 %all-to-all-done.6 = f32[32,7,1,128]{3,2,1,0:T(1,128)S(1)} async-done(((f32[32,7,1,128]{3,2,1,0:T(1,128)}), f32[32,7,1,128]{3,2,1,0:T(1,128)S(1)}, u32[]{:S(2)}, u32[]{:S(2)}) %all-to-all-start.6) | async-done | bytes 114720 | tf_op jit(solution)/shard_map/all_to_all | solution.py:628
  106.6 4.2 %known_near_field_7.1 = (f32[4,200]{1,0:T(4,128)S(1)}, f32[48,256]{1,0:T(8,128)S(1)}, f32[32,4,128]{2,1,0:T(4,128)S(1)}) custom-call(s32[4,12]{1,0:T(4,128)} %refs_0_.15, s32[4]{0:T(128)} %refs_1_.15, s32[4,12]{1,0:T(4,128)} %refs_2_.15, f32[4,12]{1,0:T(4,128)} %refs_3_.15, s32[772]{0:T(1024)} %get-tuple-element.70.refs_4_, f32[8,4,200]{2,1,0:T(4,128)} %refs_5_.15, ...), custom_call_target="tpu_custom_call" | custom-call | flops 3840000 | bytes 5760000 | tf_op jit(solution)/shard_map/known_near_field_7/pallas_call | solution.py:636
  110.8 4.0 %all-to-all-done.7 = f32[32,7,1,128]{3,2,1,0:T(1,128)S(1)} async-done(((f32[32,7,1,128]{3,2,1,0:T(1,128)}), f32[32,7,1,128]{3,2,1,0:T(1,128)S(1)}, u32[]{:S(2)}, u32[]{:S(2)}) %all-to-all-start.7) | async-done | bytes 114720 | tf_op jit(solution)/shard_map/all_to_all | solution.py:628
  (35 shorter events, 24.1 us)
Async XLA Ops:
  0.9 9.2 %collective-permute-start.2 = (f32[16,8,128]{2,1,0:T(8,128)S(1)}, f32[16,8,128]{2,1,0:T(8,128)S(1)}, u32[]{:S(2)}, u32[]{:S(2)}) collective-permute-start(f32[16,8,128]{2,1,0:T(8,128)S(1)} %pack_history.1), channel_id=1, source_target_pairs={{0,3},{1,2},{2,1},{3,0},{4,7},{5,6},{6,5},{7,4},{8,11},{9,10},{10,... | collective-permute-start | bytes 196616 | tf_op jit(solution)/shard_map/ppermute | solution.py:519
  4.8 5.3 %collective-permute-start.1 = (f32[16,8,128]{2,1,0:T(8,128)S(1)}, f32[16,8,128]{2,1,0:T(8,128)S(1)}, u32[]{:S(2)}, u32[]{:S(2)}) collective-permute-start(f32[16,8,128]{2,1,0:T(8,128)S(1)} %pack_history.1), channel_id=1, source_target_pairs={{0,2},{1,3},{2,0},{3,1},{4,6},{5,7},{6,4},{7,5},{8,10},{9,11},{10,... | collective-permute-start | bytes 196616 | tf_op jit(solution)/shard_map/ppermute | solution.py:519
  5.3 4.8 %collective-permute-start = (f32[16,8,128]{2,1,0:T(8,128)S(1)}, f32[16,8,128]{2,1,0:T(8,128)S(1)}, u32[]{:S(2)}, u32[]{:S(2)}) collective-permute-start(f32[16,8,128]{2,1,0:T(8,128)S(1)} %pack_history.1), channel_id=1, source_target_pairs={{0,1},{1,0},{2,3},{3,2},{4,5},{5,4},{6,7},{7,6},{8,9},{9,8},{10,11... | collective-permute-start | bytes 196616 | tf_op jit(solution)/shard_map/ppermute | solution.py:519
  10.2 9.5 %copy-start.3 = (f32[16,4,8,128]{3,2,1,0:T(8,128)}, f32[16,4,8,128]{3,2,1,0:T(8,128)S(1)}, u32[]{:S(2)}) copy-start(f32[16,4,8,128]{3,2,1,0:T(8,128)S(1)} %pad_maximum_fusion.1) | copy-start | bytes 786436
  10.2 8.7 %collective-permute-start.4 = (f32[16,32,128]{2,1,0:T(8,128)S(1)}, f32[16,32,128]{2,1,0:T(8,128)S(1)}, u32[]{:S(2)}, u32[]{:S(2)}) collective-permute-start(f32[16,32,128]{2,1,0:T(8,128)S(1)} %bitcast.42), channel_id=1, source_target_pairs={{4,8},{12,16},{20,24},{8,4},{16,12},{24,20},{5,9},{13,17},{21,25},... | collective-permute-start | bytes 786440 | tf_op jit(solution)/shard_map/ppermute | solution.py:621
  10.9 8.1 %collective-permute-start.3 = (f32[16,32,128]{2,1,0:T(8,128)S(1)}, f32[16,32,128]{2,1,0:T(8,128)S(1)}, u32[]{:S(2)}, u32[]{:S(2)}) collective-permute-start(f32[16,32,128]{2,1,0:T(8,128)S(1)} %bitcast.43), channel_id=1, source_target_pairs={{0,4},{4,0},{8,12},{12,8},{16,20},{20,16},{24,28},{28,24},{1,5},{5... | collective-permute-start | bytes 786440 | tf_op jit(solution)/shard_map/ppermute | solution.py:619
  14.1 13.0 %all-to-all-start = ((f32[32,7,1,128]{3,2,1,0:T(1,128)}), f32[32,7,1,128]{3,2,1,0:T(1,128)S(1)}, u32[]{:S(2)}, u32[]{:S(2)}) async-start(f32[32,7,1,128]{3,2,1,0:T(1,128)} %get-tuple-element.81), calls=%async_computation | async-start | bytes 229376 | tf_op jit(solution)/shard_map/all_to_all | solution.py:628
  19.0 0.8 copy-start.4
  19.0 0.8 copy-start.5
  19.8 7.4 %copy-start = (bf16[4,512,200]{1,2,0:T(8,128)(2,1)S(1)}, bf16[4,512,200]{1,2,0:T(8,128)(2,1)}, u32[]{:S(2)}) copy-start(bf16[4,512,200]{1,2,0:T(8,128)(2,1)} %param.21) | copy-start | bytes 2457604
  19.8 7.4 %copy-start.1 = (bf16[4,200,200]{2,1,0:T(8,128)(2,1)S(1)}, bf16[4,200,200]{2,1,0:T(8,128)(2,1)}, u32[]{:S(2)}) copy-start(bf16[4,200,200]{2,1,0:T(8,128)(2,1)} %refs_8_.31) | copy-start | bytes 960004
  19.8 7.4 %copy-start.2 = (f32[4,512]{1,0:T(4,128)S(1)}, f32[4,512]{1,0:T(4,128)}, u32[]{:S(2)}) copy-start(f32[4,512]{1,0:T(4,128)} %refs_9_.15) | copy-start | bytes 24580
  28.6 11.1 %all-to-all-start.1 = ((f32[32,7,1,128]{3,2,1,0:T(1,128)}), f32[32,7,1,128]{3,2,1,0:T(1,128)S(1)}, u32[]{:S(2)}, u32[]{:S(2)}) async-start(f32[32,7,1,128]{3,2,1,0:T(1,128)} %get-tuple-element.87), calls=%async_computation.1 | async-start | bytes 229376 | tf_op jit(solution)/shard_map/all_to_all | solution.py:628
  41.4 10.8 %all-to-all-start.2 = ((f32[32,7,1,128]{3,2,1,0:T(1,128)}), f32[32,7,1,128]{3,2,1,0:T(1,128)S(1)}, u32[]{:S(2)}, u32[]{:S(2)}) async-start(f32[32,7,1,128]{3,2,1,0:T(1,128)} %get-tuple-element.94), calls=%async_computation.2 | async-start | bytes 229376 | tf_op jit(solution)/shard_map/all_to_all | solution.py:628
  53.9 10.8 %all-to-all-start.3 = ((f32[32,7,1,128]{3,2,1,0:T(1,128)}), f32[32,7,1,128]{3,2,1,0:T(1,128)S(1)}, u32[]{:S(2)}, u32[]{:S(2)}) async-start(f32[32,7,1,128]{3,2,1,0:T(1,128)} %get-tuple-element.101), calls=%async_computation.3 | async-start | bytes 229376 | tf_op jit(solution)/shard_map/all_to_all | solution.py:628
  66.5 10.8 %all-to-all-start.4 = ((f32[32,7,1,128]{3,2,1,0:T(1,128)}), f32[32,7,1,128]{3,2,1,0:T(1,128)S(1)}, u32[]{:S(2)}, u32[]{:S(2)}) async-start(f32[32,7,1,128]{3,2,1,0:T(1,128)} %get-tuple-element.108), calls=%async_computation.4 | async-start | bytes 229376 | tf_op jit(solution)/shard_map/all_to_all | solution.py:628
  79.0 10.8 %all-to-all-start.5 = ((f32[32,7,1,128]{3,2,1,0:T(1,128)}), f32[32,7,1,128]{3,2,1,0:T(1,128)S(1)}, u32[]{:S(2)}, u32[]{:S(2)}) async-start(f32[32,7,1,128]{3,2,1,0:T(1,128)} %get-tuple-element.115), calls=%async_computation.5 | async-start | bytes 229376 | tf_op jit(solution)/shard_map/all_to_all | solution.py:628
  91.5 10.8 %all-to-all-start.6 = ((f32[32,7,1,128]{3,2,1,0:T(1,128)}), f32[32,7,1,128]{3,2,1,0:T(1,128)S(1)}, u32[]{:S(2)}, u32[]{:S(2)}) async-start(f32[32,7,1,128]{3,2,1,0:T(1,128)} %get-tuple-element.122), calls=%async_computation.6 | async-start | bytes 229376 | tf_op jit(solution)/shard_map/all_to_all | solution.py:628
  104.0 10.8 %all-to-all-start.7 = ((f32[32,7,1,128]{3,2,1,0:T(1,128)}), f32[32,7,1,128]{3,2,1,0:T(1,128)S(1)}, u32[]{:S(2)}, u32[]{:S(2)}) async-start(f32[32,7,1,128]{3,2,1,0:T(1,128)} %get-tuple-element.129), calls=%async_computation.7 | async-start | bytes 229376 | tf_op jit(solution)/shard_map/all_to_all | solution.py:628

commit v7 on v6

--- a/solution.py
+++ b/solution.py
@@ -103,7 +103,10 @@
 
 
 def row_of(cluster_number, clusters, halves):
-    place = lax.rem(cluster_number, clusters)
+    if clusters & (clusters - 1):
+        place = lax.rem(cluster_number, clusters)
+    else:
+        place = cluster_number & (clusters - 1)
     return (cluster_number - place) * halves + place
 
 
@@ -111,9 +114,9 @@
     clus_count,
     rays_in, history_in, shift_in, trans_in, far_idx_in, far_lag_in, near_idx_in, near_cnt_in,
     near_lag_in, near_frac_in, blocks,
-    spectra, message, weights, fresh_weights, kept, kept_weight, kept_plan, near_plan, old_plan,
-    rays, history, shift, trans, far_idx, far_lag, near_idx, near_cnt, near_lag, near_frac,
-    far_list, outgoing, sem, sems,
+    spectra, message, weights, fresh_weights, kept, kept_weight, kept_plan, near_plan_out,
+    old_plan_out, rays, history, shift, trans, far_idx, far_lag, near_idx, near_cnt, near_lag, near_frac,
+    far_list, outgoing, near_plan, old_plan, sem, sems,
 ):
     small = start_all(
         (
@@ -211,6 +214,9 @@
     counts = lax.fori_loop(0, groups, one, (jnp.int32(0), jnp.int32(0)))
     old_plan[0] = counts[1]
 
+    sends = start_all(
+        ((near_plan, near_plan_out), (old_plan, old_plan_out)), sems.at[pl.ds(10, 2)]
+    )
     wait_all(large)
     total = jnp.zeros((lags, dir_rows * LANE), jnp.float32)
     for cluster in range(clusters):
@@ -225,15 +231,14 @@
         return carry
 
     lax.fori_loop(0, counts[0], add_past, 0)
-    send = pltpu.make_async_copy(outgoing, message.at[:, :, 0, :], sems.at[0])
-    send.start()
+    sends += start_all(((outgoing, message.at[:, :, 0, :]),), sems.at[pl.ds(12, 1)])
 
     def finish(place, carry):
         kept_copy(place, near_plan[3 * place + 1]).wait()
         return carry
 
     lax.fori_loop(0, jnp.minimum(near_plan[0], KEPT), finish, 0)
-    send.wait()
+    wait_all(sends)
 
 
 def near_kernel(step, last, clus_count, lags, *refs):
@@ -307,6 +312,21 @@
             def _():
                 block_copy(cluster, number).start()
 
+    wait_all(others)
+    if not last:
+
+        def one(place, carry):
+            before, total = carry
+            group = old_plan[3 * place + 1]
+            slot = step + 1 + lags - old_plan[3 * place + 3]
+            term = weights[old_plan[3 * place + 2]] * spectra[slot]
+            total = jnp.where(group == before, total, 0.0) + term
+            known[group] = total
+            return group, total
+
+        lax.fori_loop(
+            0, old_plan[0], one, (jnp.int32(-1), jnp.zeros(known.shape[1:], jnp.float32))
+        )
     wait_all(wide)
     if not step:
         keep = pltpu.make_async_copy(
@@ -329,21 +349,6 @@
                 )
     for cluster in range(clusters):
         blended[cluster * slots : (cluster + 1) * slots, :] = tall[cluster, :slots, :]
-    wait_all(others)
-    if not last:
-
-        def one(place, carry):
-            before, total = carry
-            group = old_plan[3 * place + 1]
-            slot = step + 1 + lags - old_plan[3 * place + 3]
-            term = weights[old_plan[3 * place + 2]] * spectra[slot]
-            total = jnp.where(group == before, total, 0.0) + term
-            known[group] = total
-            return group, total
-
-        lax.fori_loop(
-            0, old_plan[0], one, (jnp.int32(-1), jnp.zeros(known.shape[1:], jnp.float32))
-        )
     which = lax.broadcasted_iota(jnp.int32, (tall.shape[1], unknowns), 0)
 
     def part(number, cluster):
@@ -592,7 +597,7 @@
                 pltpu.HBM((3 * far_entries + 4,), i32),
             ),
             in_specs=[HBM] * 11,
-            out_specs=[VMEM, HBM] + [VMEM] * 5 + [SMEM] * 2,
+            out_specs=[VMEM, HBM] + [VMEM] * 5 + [HBM] * 2,
             scratch_shapes=[
                 pltpu.VMEM(rays.shape, bf16),
                 pltpu.VMEM(history.shape, f32),
@@ -603,8 +608,10 @@
                 *smem_lists,
                 pltpu.SMEM((2 * far_entries + 2,), i32),
                 pltpu.VMEM((groups, sent_rows, LANE), f32),
+                pltpu.SMEM((3 * near_entries + 4,), i32),
+                pltpu.SMEM((3 * far_entries + 4,), i32),
                 dma,
-                dma((10,)),
+                dma((13,)),
             ],
             compiler_params=params,
             name="past_spectra",

time: 117 us -> 117 us (level)
  Pallas kernels: 52.2 us -> 50.8 us
    pallas_call x1, Pallas kernels: 4.63 us -> 3.31 us  [local(): pl.pallas_call(functools.partial(begin_kernel, clus_count), out_shape=(sh...]
  transfers between devices with their start and end apart: 13 -> 13, of which waited for: 8 -> 10; matrix products, arithmetic and copies ran while one was open for 0% -> 0% of each run, Pallas kernels for 33% -> 32%
where the time goes in v7:
time: 117 us; the launch traced here: 116 us
  Pallas kernels  50.8 us (43%)
  waiting for transfers between devices  32.1 us (27%)
  starting transfers between devices  31.3 us (27%)
    pallas_call x8, Pallas kernels, local(): pl.pallas_call(functools.partial(near_kernel, step, last, clus_count, lag...  33.2 us
    all_to_all x8, waiting for transfers between devices, local(): arrived = lax.all_to_all(message, ('slab', 'clus'), 0, 0, tiled=True)  31.3 us
    all_to_all x8, starting transfers between devices, local(): arrived = lax.all_to_all(message, ('slab', 'clus'), 0, 0, tiled=True)  23 us
    pallas_call x8, Pallas kernels, local(): pl.pallas_call(functools.partial(march_kernel, step, last, clus_count, sl...  13.4 us
    ppermute x3, starting transfers between devices, exchange(): return lax.ppermute(block, axis, [(i, i ^ bit) for i in range(count)])  4.6 us
    pallas_call x1, Pallas kernels, local(): pl.pallas_call(functools.partial(begin_kernel, clus_count), out_shape=(sh...  3.31 us
    ppermute x1, starting transfers between devices, local(): lax.ppermute(mid, 'slab', [(i, i ^ 1) for i in range(slab_count)])  3.05 us
  transfers between devices with their start and end apart: 13, of which 10 were waited for; matrix products, arithmetic and copies ran while one was open for 0% of the time, Pallas kernels for 32%

profile of v7, /device:TPU:0, one launch (start us, length us, event | category | flops | bytes accessed | tf_op | source)
XLA Modules:
  0.0 115.5 jit_solution(10295076332410381509)
XLA Ops:
  0.9 4.0 %collective-permute-start.2 = (f32[16,8,128]{2,1,0:T(8,128)S(1)}, f32[16,8,128]{2,1,0:T(8,128)S(1)}, u32[]{:S(2)}, u32[]{:S(2)}) collective-permute-start(f32[16,8,128]{2,1,0:T(8,128)S(1)} %pack_history.1), channel_id=1, source_target_pairs={{0,3},{1,2},{2,1},{3,0},{4,7},{5,6},{6,5},{7,4},{8,11},{9,10},{10,... | collective-permute-start | bytes 196616 | tf_op jit(solution)/shard_map/ppermute | solution.py:524
  5.5 3.3 %past_spectra.1 = (f32[16,4,128]{2,1,0:T(4,128)S(1)}, f32[32,7,1,128]{3,2,1,0:T(1,128)}, f32[256,4,128]{2,1,0:T(4,128)S(1)}, f32[32,4,128]{2,1,0:T(4,128)S(1)}, ...) custom-call(bf16[4,200,512]{2,1,0:T(8,128)(2,1)} %bitcast.24, ...), custom_call_target="tpu_custom_call" | custom-call | tf_op jit(solution)/shard_map/past_spectra/pallas_call | solution.py:586
  10.4 3.1 %collective-permute-start.3 = (f32[16,32,128]{2,1,0:T(8,128)S(1)}, f32[16,32,128]{2,1,0:T(8,128)S(1)}, u32[]{:S(2)}, u32[]{:S(2)}) collective-permute-start(f32[16,32,128]{2,1,0:T(8,128)S(1)} %bitcast.43), channel_id=1, source_target_pairs={{0,4},{4,0},{8,12},{12,8},{16,20},{20,16},{24,28},{28,24},{1,5},{5... | collective-permute-start | bytes 786440 | tf_op jit(solution)/shard_map/ppermute | solution.py:626
  13.4 4.9 %all-to-all-start = ((f32[32,7,1,128]{3,2,1,0:T(1,128)}), f32[32,7,1,128]{3,2,1,0:T(1,128)S(1)}, u32[]{:S(2)}, u32[]{:S(2)}) async-start(f32[32,7,1,128]{3,2,1,0:T(1,128)} %get-tuple-element.81), calls=%async_computation | async-start | bytes 229376 | tf_op jit(solution)/shard_map/all_to_all | solution.py:635
  19.1 4.5 %known_near_field_0.1 = (f32[4,200]{1,0:T(4,128)S(1)}, f32[48,256]{1,0:T(8,128)S(1)}, f32[32,4,128]{2,1,0:T(4,128)S(1)}, f32[24,96,128]{2,1,0:T(8,128)}) custom-call(s32[4,12]{1,0:T(4,128)} %refs_0_.15, s32[4]{0:T(128)} %refs_1_.15, s32[4,12]{1,0:T(4,128)} %refs_2_.15, f32[4,12]{1,0:T(4,128)} %refs_3_.15, s32[772]{0:T(1024)} %get-tuple-element.70.refs_4_, ...), custom_call_target="tpu_custom_call" | custom-call | flops 3840000 | bytes 5760000 | tf_op jit(solution)/shard_map/known_near_field_0/pallas_call | solution.py:643
  23.6 2.9 %all-to-all-done = f32[32,7,1,128]{3,2,1,0:T(1,128)S(1)} async-done(((f32[32,7,1,128]{3,2,1,0:T(1,128)}), f32[32,7,1,128]{3,2,1,0:T(1,128)S(1)}, u32[]{:S(2)}, u32[]{:S(2)}) %all-to-all-start) | async-done | bytes 114720 | tf_op jit(solution)/shard_map/all_to_all | solution.py:635
  27.9 2.6 %all-to-all-start.1 = ((f32[32,7,1,128]{3,2,1,0:T(1,128)}), f32[32,7,1,128]{3,2,1,0:T(1,128)S(1)}, u32[]{:S(2)}, u32[]{:S(2)}) async-start(f32[32,7,1,128]{3,2,1,0:T(1,128)} %get-tuple-element.87), calls=%async_computation.1 | async-start | bytes 229376 | tf_op jit(solution)/shard_map/all_to_all | solution.py:635
  30.5 4.1 %known_near_field_1.1 = (f32[4,200]{1,0:T(4,128)S(1)}, f32[48,256]{1,0:T(8,128)S(1)}, f32[32,4,128]{2,1,0:T(4,128)S(1)}) custom-call(s32[4,12]{1,0:T(4,128)} %refs_0_.15, s32[4]{0:T(128)} %refs_1_.15, s32[4,12]{1,0:T(4,128)} %refs_2_.15, f32[4,12]{1,0:T(4,128)} %refs_3_.15, s32[772]{0:T(1024)} %get-tuple-element.70.refs_4_, f32[8,4,200]{2,1,0:T(4,128)} %refs_5_.15, ...), custom_call_target="tpu_custom_call" | custom-call | flops 3840000 | bytes 5760000 | tf_op jit(solution)/shard_map/known_near_field_1/pallas_call | solution.py:643
  34.6 4.1 %all-to-all-done.1 = f32[32,7,1,128]{3,2,1,0:T(1,128)S(1)} async-done(((f32[32,7,1,128]{3,2,1,0:T(1,128)}), f32[32,7,1,128]{3,2,1,0:T(1,128)S(1)}, u32[]{:S(2)}, u32[]{:S(2)}) %all-to-all-start.1) | async-done | bytes 114720 | tf_op jit(solution)/shard_map/all_to_all | solution.py:635
  40.4 2.6 %all-to-all-start.2 = ((f32[32,7,1,128]{3,2,1,0:T(1,128)}), f32[32,7,1,128]{3,2,1,0:T(1,128)S(1)}, u32[]{:S(2)}, u32[]{:S(2)}) async-start(f32[32,7,1,128]{3,2,1,0:T(1,128)} %get-tuple-element.94), calls=%async_computation.2 | async-start | bytes 229376 | tf_op jit(solution)/shard_map/all_to_all | solution.py:635
  43.0 4.1 %known_near_field_2.1 = (f32[4,200]{1,0:T(4,128)S(1)}, f32[48,256]{1,0:T(8,128)S(1)}, f32[32,4,128]{2,1,0:T(4,128)S(1)}) custom-call(s32[4,12]{1,0:T(4,128)} %refs_0_.15, s32[4]{0:T(128)} %refs_1_.15, s32[4,12]{1,0:T(4,128)} %refs_2_.15, f32[4,12]{1,0:T(4,128)} %refs_3_.15, s32[772]{0:T(1024)} %get-tuple-element.70.refs_4_, f32[8,4,200]{2,1,0:T(4,128)} %refs_5_.15, ...), custom_call_target="tpu_custom_call" | custom-call | flops 3840000 | bytes 5760000 | tf_op jit(solution)/shard_map/known_near_field_2/pallas_call | solution.py:643
  47.1 4.1 %all-to-all-done.2 = f32[32,7,1,128]{3,2,1,0:T(1,128)S(1)} async-done(((f32[32,7,1,128]{3,2,1,0:T(1,128)}), f32[32,7,1,128]{3,2,1,0:T(1,128)S(1)}, u32[]{:S(2)}, u32[]{:S(2)}) %all-to-all-start.2) | async-done | bytes 114720 | tf_op jit(solution)/shard_map/all_to_all | solution.py:635
  55.6 4.1 %known_near_field_3.1 = (f32[4,200]{1,0:T(4,128)S(1)}, f32[48,256]{1,0:T(8,128)S(1)}, f32[32,4,128]{2,1,0:T(4,128)S(1)}) custom-call(s32[4,12]{1,0:T(4,128)} %refs_0_.15, s32[4]{0:T(128)} %refs_1_.15, s32[4,12]{1,0:T(4,128)} %refs_2_.15, f32[4,12]{1,0:T(4,128)} %refs_3_.15, s32[772]{0:T(1024)} %get-tuple-element.70.refs_4_, f32[8,4,200]{2,1,0:T(4,128)} %refs_5_.15, ...), custom_call_target="tpu_custom_call" | custom-call | flops 3840000 | bytes 5760000 | tf_op jit(solution)/shard_map/known_near_field_3/pallas_call | solution.py:643
  59.6 4.1 %all-to-all-done.3 = f32[32,7,1,128]{3,2,1,0:T(1,128)S(1)} async-done(((f32[32,7,1,128]{3,2,1,0:T(1,128)}), f32[32,7,1,128]{3,2,1,0:T(1,128)S(1)}, u32[]{:S(2)}, u32[]{:S(2)}) %all-to-all-start.3) | async-done | bytes 114720 | tf_op jit(solution)/shard_map/all_to_all | solution.py:635
  65.5 2.6 %all-to-all-start.4 = ((f32[32,7,1,128]{3,2,1,0:T(1,128)}), f32[32,7,1,128]{3,2,1,0:T(1,128)S(1)}, u32[]{:S(2)}, u32[]{:S(2)}) async-start(f32[32,7,1,128]{3,2,1,0:T(1,128)} %get-tuple-element.108), calls=%async_computation.4 | async-start | bytes 229376 | tf_op jit(solution)/shard_map/all_to_all | solution.py:635
  68.1 4.2 %known_near_field_4.1 = (f32[4,200]{1,0:T(4,128)S(1)}, f32[48,256]{1,0:T(8,128)S(1)}, f32[32,4,128]{2,1,0:T(4,128)S(1)}) custom-call(s32[4,12]{1,0:T(4,128)} %refs_0_.15, s32[4]{0:T(128)} %refs_1_.15, s32[4,12]{1,0:T(4,128)} %refs_2_.15, f32[4,12]{1,0:T(4,128)} %refs_3_.15, s32[772]{0:T(1024)} %get-tuple-element.70.refs_4_, f32[8,4,200]{2,1,0:T(4,128)} %refs_5_.15, ...), custom_call_target="tpu_custom_call" | custom-call | flops 3840000 | bytes 5760000 | tf_op jit(solution)/shard_map/known_near_field_4/pallas_call | solution.py:643
  72.3 4.0 %all-to-all-done.4 = f32[32,7,1,128]{3,2,1,0:T(1,128)S(1)} async-done(((f32[32,7,1,128]{3,2,1,0:T(1,128)}), f32[32,7,1,128]{3,2,1,0:T(1,128)S(1)}, u32[]{:S(2)}, u32[]{:S(2)}) %all-to-all-start.4) | async-done | bytes 114720 | tf_op jit(solution)/shard_map/all_to_all | solution.py:635
  78.1 2.6 %all-to-all-start.5 = ((f32[32,7,1,128]{3,2,1,0:T(1,128)}), f32[32,7,1,128]{3,2,1,0:T(1,128)S(1)}, u32[]{:S(2)}, u32[]{:S(2)}) async-start(f32[32,7,1,128]{3,2,1,0:T(1,128)} %get-tuple-element.115), calls=%async_computation.5 | async-start | bytes 229376 | tf_op jit(solution)/shard_map/all_to_all | solution.py:635
  80.7 4.1 %known_near_field_5.1 = (f32[4,200]{1,0:T(4,128)S(1)}, f32[48,256]{1,0:T(8,128)S(1)}, f32[32,4,128]{2,1,0:T(4,128)S(1)}) custom-call(s32[4,12]{1,0:T(4,128)} %refs_0_.15, s32[4]{0:T(128)} %refs_1_.15, s32[4,12]{1,0:T(4,128)} %refs_2_.15, f32[4,12]{1,0:T(4,128)} %refs_3_.15, s32[772]{0:T(1024)} %get-tuple-element.70.refs_4_, f32[8,4,200]{2,1,0:T(4,128)} %refs_5_.15, ...), custom_call_target="tpu_custom_call" | custom-call | flops 3840000 | bytes 5760000 | tf_op jit(solution)/shard_map/known_near_field_5/pallas_call | solution.py:643
  84.8 4.1 %all-to-all-done.5 = f32[32,7,1,128]{3,2,1,0:T(1,128)S(1)} async-done(((f32[32,7,1,128]{3,2,1,0:T(1,128)}), f32[32,7,1,128]{3,2,1,0:T(1,128)S(1)}, u32[]{:S(2)}, u32[]{:S(2)}) %all-to-all-start.5) | async-done | bytes 114720 | tf_op jit(solution)/shard_map/all_to_all | solution.py:635
  93.2 4.1 %known_near_field_6.1 = (f32[4,200]{1,0:T(4,128)S(1)}, f32[48,256]{1,0:T(8,128)S(1)}, f32[32,4,128]{2,1,0:T(4,128)S(1)}) custom-call(s32[4,12]{1,0:T(4,128)} %refs_0_.15, s32[4]{0:T(128)} %refs_1_.15, s32[4,12]{1,0:T(4,128)} %refs_2_.15, f32[4,12]{1,0:T(4,128)} %refs_3_.15, s32[772]{0:T(1024)} %get-tuple-element.70.refs_4_, f32[8,4,200]{2,1,0:T(4,128)} %refs_5_.15, ...), custom_call_target="tpu_custom_call" | custom-call | flops 3840000 | bytes 5760000 | tf_op jit(solution)/shard_map/known_near_field_6/pallas_call | solution.py:643
  97.3 4.1 %all-to-all-done.6 = f32[32,7,1,128]{3,2,1,0:T(1,128)S(1)} async-done(((f32[32,7,1,128]{3,2,1,0:T(1,128)}), f32[32,7,1,128]{3,2,1,0:T(1,128)S(1)}, u32[]{:S(2)}, u32[]{:S(2)}) %all-to-all-start.6) | async-done | bytes 114720 | tf_op jit(solution)/shard_map/all_to_all | solution.py:635
  105.7 4.2 %known_near_field_7.1 = (f32[4,200]{1,0:T(4,128)S(1)}, f32[48,256]{1,0:T(8,128)S(1)}, f32[32,4,128]{2,1,0:T(4,128)S(1)}) custom-call(s32[4,12]{1,0:T(4,128)} %refs_0_.15, s32[4]{0:T(128)} %refs_1_.15, s32[4,12]{1,0:T(4,128)} %refs_2_.15, f32[4,12]{1,0:T(4,128)} %refs_3_.15, s32[772]{0:T(1024)} %get-tuple-element.70.refs_4_, f32[8,4,200]{2,1,0:T(4,128)} %refs_5_.15, ...), custom_call_target="tpu_custom_call" | custom-call | flops 3840000 | bytes 5760000 | tf_op jit(solution)/shard_map/known_near_field_7/pallas_call | solution.py:643
  110.0 4.0 %all-to-all-done.7 = f32[32,7,1,128]{3,2,1,0:T(1,128)S(1)} async-done(((f32[32,7,1,128]{3,2,1,0:T(1,128)}), f32[32,7,1,128]{3,2,1,0:T(1,128)S(1)}, u32[]{:S(2)}, u32[]{:S(2)}) %all-to-all-start.7) | async-done | bytes 114720 | tf_op jit(solution)/shard_map/all_to_all | solution.py:635
  (35 shorter events, 25.0 us)
Async XLA Ops:
  0.9 7.9 %collective-permute-start.2 = (f32[16,8,128]{2,1,0:T(8,128)S(1)}, f32[16,8,128]{2,1,0:T(8,128)S(1)}, u32[]{:S(2)}, u32[]{:S(2)}) collective-permute-start(f32[16,8,128]{2,1,0:T(8,128)S(1)} %pack_history.1), channel_id=1, source_target_pairs={{0,3},{1,2},{2,1},{3,0},{4,7},{5,6},{6,5},{7,4},{8,11},{9,10},{10,... | collective-permute-start | bytes 196616 | tf_op jit(solution)/shard_map/ppermute | solution.py:524
  4.8 4.3 %collective-permute-start.1 = (f32[16,8,128]{2,1,0:T(8,128)S(1)}, f32[16,8,128]{2,1,0:T(8,128)S(1)}, u32[]{:S(2)}, u32[]{:S(2)}) collective-permute-start(f32[16,8,128]{2,1,0:T(8,128)S(1)} %pack_history.1), channel_id=1, source_target_pairs={{0,2},{1,3},{2,0},{3,1},{4,6},{5,7},{6,4},{7,5},{8,10},{9,11},{10,... | collective-permute-start | bytes 196616 | tf_op jit(solution)/shard_map/ppermute | solution.py:524
  5.3 4.3 %collective-permute-start = (f32[16,8,128]{2,1,0:T(8,128)S(1)}, f32[16,8,128]{2,1,0:T(8,128)S(1)}, u32[]{:S(2)}, u32[]{:S(2)}) collective-permute-start(f32[16,8,128]{2,1,0:T(8,128)S(1)} %pack_history.1), channel_id=1, source_target_pairs={{0,1},{1,0},{2,3},{3,2},{4,5},{5,4},{6,7},{7,6},{8,9},{9,8},{10,11... | collective-permute-start | bytes 196616 | tf_op jit(solution)/shard_map/ppermute | solution.py:524
  9.7 9.4 %copy-start.3 = (f32[16,4,8,128]{3,2,1,0:T(8,128)}, f32[16,4,8,128]{3,2,1,0:T(8,128)S(1)}, u32[]{:S(2)}) copy-start(f32[16,4,8,128]{3,2,1,0:T(8,128)S(1)} %pad_maximum_fusion.1) | copy-start | bytes 786436
  9.7 8.6 %collective-permute-start.4 = (f32[16,32,128]{2,1,0:T(8,128)S(1)}, f32[16,32,128]{2,1,0:T(8,128)S(1)}, u32[]{:S(2)}, u32[]{:S(2)}) collective-permute-start(f32[16,32,128]{2,1,0:T(8,128)S(1)} %bitcast.42), channel_id=1, source_target_pairs={{4,8},{12,16},{20,24},{8,4},{16,12},{24,20},{5,9},{13,17},{21,25},... | collective-permute-start | bytes 786440 | tf_op jit(solution)/shard_map/ppermute | solution.py:628
  10.4 7.9 %collective-permute-start.3 = (f32[16,32,128]{2,1,0:T(8,128)S(1)}, f32[16,32,128]{2,1,0:T(8,128)S(1)}, u32[]{:S(2)}, u32[]{:S(2)}) collective-permute-start(f32[16,32,128]{2,1,0:T(8,128)S(1)} %bitcast.43), channel_id=1, source_target_pairs={{0,4},{4,0},{8,12},{12,8},{16,20},{20,16},{24,28},{28,24},{1,5},{5... | collective-permute-start | bytes 786440 | tf_op jit(solution)/shard_map/ppermute | solution.py:626
  13.4 13.0 %all-to-all-start = ((f32[32,7,1,128]{3,2,1,0:T(1,128)}), f32[32,7,1,128]{3,2,1,0:T(1,128)S(1)}, u32[]{:S(2)}, u32[]{:S(2)}) async-start(f32[32,7,1,128]{3,2,1,0:T(1,128)} %get-tuple-element.81), calls=%async_computation | async-start | bytes 229376 | tf_op jit(solution)/shard_map/all_to_all | solution.py:635
  18.3 0.8 copy-start.4
  18.3 0.8 copy-start.5
  19.1 7.4 %copy-start = (bf16[4,512,200]{1,2,0:T(8,128)(2,1)S(1)}, bf16[4,512,200]{1,2,0:T(8,128)(2,1)}, u32[]{:S(2)}) copy-start(bf16[4,512,200]{1,2,0:T(8,128)(2,1)} %param.21) | copy-start | bytes 2457604
  19.1 7.4 %copy-start.1 = (bf16[4,200,200]{2,1,0:T(8,128)(2,1)S(1)}, bf16[4,200,200]{2,1,0:T(8,128)(2,1)}, u32[]{:S(2)}) copy-start(bf16[4,200,200]{2,1,0:T(8,128)(2,1)} %refs_8_.31) | copy-start | bytes 960004
  19.1 7.4 %copy-start.2 = (f32[4,512]{1,0:T(4,128)S(1)}, f32[4,512]{1,0:T(4,128)}, u32[]{:S(2)}) copy-start(f32[4,512]{1,0:T(4,128)} %refs_9_.15) | copy-start | bytes 24580
  27.9 10.8 %all-to-all-start.1 = ((f32[32,7,1,128]{3,2,1,0:T(1,128)}), f32[32,7,1,128]{3,2,1,0:T(1,128)S(1)}, u32[]{:S(2)}, u32[]{:S(2)}) async-start(f32[32,7,1,128]{3,2,1,0:T(1,128)} %get-tuple-element.87), calls=%async_computation.1 | async-start | bytes 229376 | tf_op jit(solution)/shard_map/all_to_all | solution.py:635
  40.4 10.8 %all-to-all-start.2 = ((f32[32,7,1,128]{3,2,1,0:T(1,128)}), f32[32,7,1,128]{3,2,1,0:T(1,128)S(1)}, u32[]{:S(2)}, u32[]{:S(2)}) async-start(f32[32,7,1,128]{3,2,1,0:T(1,128)} %get-tuple-element.94), calls=%async_computation.2 | async-start | bytes 229376 | tf_op jit(solution)/shard_map/all_to_all | solution.py:635
  53.0 10.8 %all-to-all-start.3 = ((f32[32,7,1,128]{3,2,1,0:T(1,128)}), f32[32,7,1,128]{3,2,1,0:T(1,128)S(1)}, u32[]{:S(2)}, u32[]{:S(2)}) async-start(f32[32,7,1,128]{3,2,1,0:T(1,128)} %get-tuple-element.101), calls=%async_computation.3 | async-start | bytes 229376 | tf_op jit(solution)/shard_map/all_to_all | solution.py:635
  65.5 10.8 %all-to-all-start.4 = ((f32[32,7,1,128]{3,2,1,0:T(1,128)}), f32[32,7,1,128]{3,2,1,0:T(1,128)S(1)}, u32[]{:S(2)}, u32[]{:S(2)}) async-start(f32[32,7,1,128]{3,2,1,0:T(1,128)} %get-tuple-element.108), calls=%async_computation.4 | async-start | bytes 229376 | tf_op jit(solution)/shard_map/all_to_all | solution.py:635
  78.1 10.8 %all-to-all-start.5 = ((f32[32,7,1,128]{3,2,1,0:T(1,128)}), f32[32,7,1,128]{3,2,1,0:T(1,128)S(1)}, u32[]{:S(2)}, u32[]{:S(2)}) async-start(f32[32,7,1,128]{3,2,1,0:T(1,128)} %get-tuple-element.115), calls=%async_computation.5 | async-start | bytes 229376 | tf_op jit(solution)/shard_map/all_to_all | solution.py:635
  90.6 10.8 %all-to-all-start.6 = ((f32[32,7,1,128]{3,2,1,0:T(1,128)}), f32[32,7,1,128]{3,2,1,0:T(1,128)S(1)}, u32[]{:S(2)}, u32[]{:S(2)}) async-start(f32[32,7,1,128]{3,2,1,0:T(1,128)} %get-tuple-element.122), calls=%async_computation.6 | async-start | bytes 229376 | tf_op jit(solution)/shard_map/all_to_all | solution.py:635
  103.1 10.8 %all-to-all-start.7 = ((f32[32,7,1,128]{3,2,1,0:T(1,128)}), f32[32,7,1,128]{3,2,1,0:T(1,128)S(1)}, u32[]{:S(2)}, u32[]{:S(2)}) async-start(f32[32,7,1,128]{3,2,1,0:T(1,128)} %get-tuple-element.129), calls=%async_computation.7 | async-start | bytes 229376 | tf_op jit(solution)/shard_map/all_to_all | solution.py:635

commit v8 on v7

--- a/solution.py
+++ b/solution.py
@@ -10,7 +10,7 @@
 LANE = 128
 PACK = 16
 KEPT = 8
-CHUNK = 3
+CHUNK = 6
 VMEM_LIMIT = 24 * 1024 * 1024
 HBM = pl.BlockSpec(memory_space=pltpu.HBM)
 ANY = pl.BlockSpec(memory_space=pl.ANY)

time: 117 us -> 116 us (level)
  transfers between devices with their start and end apart: 13 -> 13, of which waited for: 10 -> 9; matrix products, arithmetic and copies ran while one was open for 0% -> 0% of each run, Pallas kernels for 32% -> 32%
where the time goes in v8:
time: 116 us
  Pallas kernels  50.7 us (44%)
  waiting for transfers between devices  32.1 us (28%)
  starting transfers between devices  31.5 us (27%)
    pallas_call x8, Pallas kernels, local(): pl.pallas_call(functools.partial(near_kernel, step, last, clus_count, lag...  32.6 us
    all_to_all x8, waiting for transfers between devices, local(): arrived = lax.all_to_all(message, ('slab', 'clus'), 0, 0, tiled=True)  31.9 us
    all_to_all x8, starting transfers between devices, local(): arrived = lax.all_to_all(message, ('slab', 'clus'), 0, 0, tiled=True)  23.2 us
    pallas_call x8, Pallas kernels, local(): pl.pallas_call(functools.partial(march_kernel, step, last, clus_count, sl...  13.3 us
    ppermute x3, starting transfers between devices, exchange(): return lax.ppermute(block, axis, [(i, i ^ bit) for i in range(count)])  4.6 us
    pallas_call x1, Pallas kernels, local(): pl.pallas_call(functools.partial(begin_kernel, clus_count), out_shape=(sh...  3.95 us
    ppermute x1, starting transfers between devices, local(): lax.ppermute(mid, 'slab', [(i, i ^ 1) for i in range(slab_count)])  2.99 us
  transfers between devices with their start and end apart: 13, of which 9 were waited for; matrix products, arithmetic and copies ran while one was open for 0% of the time, Pallas kernels for 32%

profile of v8, /device:TPU:0, one launch (start us, length us, event | category | flops | bytes accessed | tf_op | source)
XLA Modules:
  0.0 115.6 jit_solution(13704396853786341855)
XLA Ops:
  0.9 4.0 %collective-permute-start.2 = (f32[16,8,128]{2,1,0:T(8,128)S(1)}, f32[16,8,128]{2,1,0:T(8,128)S(1)}, u32[]{:S(2)}, u32[]{:S(2)}) collective-permute-start(f32[16,8,128]{2,1,0:T(8,128)S(1)} %pack_history.1), channel_id=1, source_target_pairs={{0,3},{1,2},{2,1},{3,0},{4,7},{5,6},{6,5},{7,4},{8,11},{9,10},{10,... | collective-permute-start | bytes 196616 | tf_op jit(solution)/shard_map/ppermute | solution.py:524
  5.5 4.0 %past_spectra.1 = (f32[16,4,128]{2,1,0:T(4,128)S(1)}, f32[32,7,1,128]{3,2,1,0:T(1,128)}, f32[256,4,128]{2,1,0:T(4,128)S(1)}, f32[32,4,128]{2,1,0:T(4,128)S(1)}, ...) custom-call(bf16[4,200,512]{2,1,0:T(8,128)(2,1)} %bitcast.24, ...), custom_call_target="tpu_custom_call" | custom-call | tf_op jit(solution)/shard_map/past_spectra/pallas_call | solution.py:586
  10.4 3.0 %collective-permute-start.3 = (f32[16,32,128]{2,1,0:T(8,128)S(1)}, f32[16,32,128]{2,1,0:T(8,128)S(1)}, u32[]{:S(2)}, u32[]{:S(2)}) collective-permute-start(f32[16,32,128]{2,1,0:T(8,128)S(1)} %bitcast.43), channel_id=1, source_target_pairs={{0,4},{4,0},{8,12},{12,8},{16,20},{20,16},{24,28},{28,24},{1,5},{5... | collective-permute-start | bytes 786440 | tf_op jit(solution)/shard_map/ppermute | solution.py:626
  13.4 4.8 %all-to-all-start = ((f32[32,7,1,128]{3,2,1,0:T(1,128)}), f32[32,7,1,128]{3,2,1,0:T(1,128)S(1)}, u32[]{:S(2)}, u32[]{:S(2)}) async-start(f32[32,7,1,128]{3,2,1,0:T(1,128)} %get-tuple-element.81), calls=%async_computation | async-start | bytes 229376 | tf_op jit(solution)/shard_map/all_to_all | solution.py:635
  19.0 4.3 %known_near_field_0.1 = (f32[4,200]{1,0:T(4,128)S(1)}, f32[48,256]{1,0:T(8,128)S(1)}, f32[32,4,128]{2,1,0:T(4,128)S(1)}, f32[24,96,128]{2,1,0:T(8,128)}) custom-call(s32[4,12]{1,0:T(4,128)} %refs_0_.15, s32[4]{0:T(128)} %refs_1_.15, s32[4,12]{1,0:T(4,128)} %refs_2_.15, f32[4,12]{1,0:T(4,128)} %refs_3_.15, s32[772]{0:T(1024)} %get-tuple-element.70.refs_4_, ...), custom_call_target="tpu_custom_call" | custom-call | flops 3840000 | bytes 5760000 | tf_op jit(solution)/shard_map/known_near_field_0/pallas_call | solution.py:643
  23.3 3.0 %all-to-all-done = f32[32,7,1,128]{3,2,1,0:T(1,128)S(1)} async-done(((f32[32,7,1,128]{3,2,1,0:T(1,128)}), f32[32,7,1,128]{3,2,1,0:T(1,128)S(1)}, u32[]{:S(2)}, u32[]{:S(2)}) %all-to-all-start) | async-done | bytes 114720 | tf_op jit(solution)/shard_map/all_to_all | solution.py:635
  27.8 2.8 %all-to-all-start.1 = ((f32[32,7,1,128]{3,2,1,0:T(1,128)}), f32[32,7,1,128]{3,2,1,0:T(1,128)S(1)}, u32[]{:S(2)}, u32[]{:S(2)}) async-start(f32[32,7,1,128]{3,2,1,0:T(1,128)} %get-tuple-element.87), calls=%async_computation.1 | async-start | bytes 229376 | tf_op jit(solution)/shard_map/all_to_all | solution.py:635
  30.7 4.0 %known_near_field_1.1 = (f32[4,200]{1,0:T(4,128)S(1)}, f32[48,256]{1,0:T(8,128)S(1)}, f32[32,4,128]{2,1,0:T(4,128)S(1)}) custom-call(s32[4,12]{1,0:T(4,128)} %refs_0_.15, s32[4]{0:T(128)} %refs_1_.15, s32[4,12]{1,0:T(4,128)} %refs_2_.15, f32[4,12]{1,0:T(4,128)} %refs_3_.15, s32[772]{0:T(1024)} %get-tuple-element.70.refs_4_, f32[8,4,200]{2,1,0:T(4,128)} %refs_5_.15, ...), custom_call_target="tpu_custom_call" | custom-call | flops 3840000 | bytes 5760000 | tf_op jit(solution)/shard_map/known_near_field_1/pallas_call | solution.py:643
  34.7 4.2 %all-to-all-done.1 = f32[32,7,1,128]{3,2,1,0:T(1,128)S(1)} async-done(((f32[32,7,1,128]{3,2,1,0:T(1,128)}), f32[32,7,1,128]{3,2,1,0:T(1,128)S(1)}, u32[]{:S(2)}, u32[]{:S(2)}) %all-to-all-start.1) | async-done | bytes 114720 | tf_op jit(solution)/shard_map/all_to_all | solution.py:635
  43.2 4.0 %known_near_field_2.1 = (f32[4,200]{1,0:T(4,128)S(1)}, f32[48,256]{1,0:T(8,128)S(1)}, f32[32,4,128]{2,1,0:T(4,128)S(1)}) custom-call(s32[4,12]{1,0:T(4,128)} %refs_0_.15, s32[4]{0:T(128)} %refs_1_.15, s32[4,12]{1,0:T(4,128)} %refs_2_.15, f32[4,12]{1,0:T(4,128)} %refs_3_.15, s32[772]{0:T(1024)} %get-tuple-element.70.refs_4_, f32[8,4,200]{2,1,0:T(4,128)} %refs_5_.15, ...), custom_call_target="tpu_custom_call" | custom-call | flops 3840000 | bytes 5760000 | tf_op jit(solution)/shard_map/known_near_field_2/pallas_call | solution.py:643
  47.2 4.2 %all-to-all-done.2 = f32[32,7,1,128]{3,2,1,0:T(1,128)S(1)} async-done(((f32[32,7,1,128]{3,2,1,0:T(1,128)}), f32[32,7,1,128]{3,2,1,0:T(1,128)S(1)}, u32[]{:S(2)}, u32[]{:S(2)}) %all-to-all-start.2) | async-done | bytes 114720 | tf_op jit(solution)/shard_map/all_to_all | solution.py:635
  53.1 2.6 %all-to-all-start.3 = ((f32[32,7,1,128]{3,2,1,0:T(1,128)}), f32[32,7,1,128]{3,2,1,0:T(1,128)S(1)}, u32[]{:S(2)}, u32[]{:S(2)}) async-start(f32[32,7,1,128]{3,2,1,0:T(1,128)} %get-tuple-element.101), calls=%async_computation.3 | async-start | bytes 229376 | tf_op jit(solution)/shard_map/all_to_all | solution.py:635
  55.7 4.0 %known_near_field_3.1 = (f32[4,200]{1,0:T(4,128)S(1)}, f32[48,256]{1,0:T(8,128)S(1)}, f32[32,4,128]{2,1,0:T(4,128)S(1)}) custom-call(s32[4,12]{1,0:T(4,128)} %refs_0_.15, s32[4]{0:T(128)} %refs_1_.15, s32[4,12]{1,0:T(4,128)} %refs_2_.15, f32[4,12]{1,0:T(4,128)} %refs_3_.15, s32[772]{0:T(1024)} %get-tuple-element.70.refs_4_, f32[8,4,200]{2,1,0:T(4,128)} %refs_5_.15, ...), custom_call_target="tpu_custom_call" | custom-call | flops 3840000 | bytes 5760000 | tf_op jit(solution)/shard_map/known_near_field_3/pallas_call | solution.py:643
  59.8 4.1 %all-to-all-done.3 = f32[32,7,1,128]{3,2,1,0:T(1,128)S(1)} async-done(((f32[32,7,1,128]{3,2,1,0:T(1,128)}), f32[32,7,1,128]{3,2,1,0:T(1,128)S(1)}, u32[]{:S(2)}, u32[]{:S(2)}) %all-to-all-start.3) | async-done | bytes 114720 | tf_op jit(solution)/shard_map/all_to_all | solution.py:635
  65.6 2.6 %all-to-all-start.4 = ((f32[32,7,1,128]{3,2,1,0:T(1,128)}), f32[32,7,1,128]{3,2,1,0:T(1,128)S(1)}, u32[]{:S(2)}, u32[]{:S(2)}) async-start(f32[32,7,1,128]{3,2,1,0:T(1,128)} %get-tuple-element.108), calls=%async_computation.4 | async-start | bytes 229376 | tf_op jit(solution)/shard_map/all_to_all | solution.py:635
  68.2 4.0 %known_near_field_4.1 = (f32[4,200]{1,0:T(4,128)S(1)}, f32[48,256]{1,0:T(8,128)S(1)}, f32[32,4,128]{2,1,0:T(4,128)S(1)}) custom-call(s32[4,12]{1,0:T(4,128)} %refs_0_.15, s32[4]{0:T(128)} %refs_1_.15, s32[4,12]{1,0:T(4,128)} %refs_2_.15, f32[4,12]{1,0:T(4,128)} %refs_3_.15, s32[772]{0:T(1024)} %get-tuple-element.70.refs_4_, f32[8,4,200]{2,1,0:T(4,128)} %refs_5_.15, ...), custom_call_target="tpu_custom_call" | custom-call | flops 3840000 | bytes 5760000 | tf_op jit(solution)/shard_map/known_near_field_4/pallas_call | solution.py:643
  72.3 4.1 %all-to-all-done.4 = f32[32,7,1,128]{3,2,1,0:T(1,128)S(1)} async-done(((f32[32,7,1,128]{3,2,1,0:T(1,128)}), f32[32,7,1,128]{3,2,1,0:T(1,128)S(1)}, u32[]{:S(2)}, u32[]{:S(2)}) %all-to-all-start.4) | async-done | bytes 114720 | tf_op jit(solution)/shard_map/all_to_all | solution.py:635
  78.2 2.6 %all-to-all-start.5 = ((f32[32,7,1,128]{3,2,1,0:T(1,128)}), f32[32,7,1,128]{3,2,1,0:T(1,128)S(1)}, u32[]{:S(2)}, u32[]{:S(2)}) async-start(f32[32,7,1,128]{3,2,1,0:T(1,128)} %get-tuple-element.115), calls=%async_computation.5 | async-start | bytes 229376 | tf_op jit(solution)/shard_map/all_to_all | solution.py:635
  80.8 4.1 %known_near_field_5.1 = (f32[4,200]{1,0:T(4,128)S(1)}, f32[48,256]{1,0:T(8,128)S(1)}, f32[32,4,128]{2,1,0:T(4,128)S(1)}) custom-call(s32[4,12]{1,0:T(4,128)} %refs_0_.15, s32[4]{0:T(128)} %refs_1_.15, s32[4,12]{1,0:T(4,128)} %refs_2_.15, f32[4,12]{1,0:T(4,128)} %refs_3_.15, s32[772]{0:T(1024)} %get-tuple-element.70.refs_4_, f32[8,4,200]{2,1,0:T(4,128)} %refs_5_.15, ...), custom_call_target="tpu_custom_call" | custom-call | flops 3840000 | bytes 5760000 | tf_op jit(solution)/shard_map/known_near_field_5/pallas_call | solution.py:643
  84.8 4.1 %all-to-all-done.5 = f32[32,7,1,128]{3,2,1,0:T(1,128)S(1)} async-done(((f32[32,7,1,128]{3,2,1,0:T(1,128)}), f32[32,7,1,128]{3,2,1,0:T(1,128)S(1)}, u32[]{:S(2)}, u32[]{:S(2)}) %all-to-all-start.5) | async-done | bytes 114720 | tf_op jit(solution)/shard_map/all_to_all | solution.py:635
  93.3 4.1 %known_near_field_6.1 = (f32[4,200]{1,0:T(4,128)S(1)}, f32[48,256]{1,0:T(8,128)S(1)}, f32[32,4,128]{2,1,0:T(4,128)S(1)}) custom-call(s32[4,12]{1,0:T(4,128)} %refs_0_.15, s32[4]{0:T(128)} %refs_1_.15, s32[4,12]{1,0:T(4,128)} %refs_2_.15, f32[4,12]{1,0:T(4,128)} %refs_3_.15, s32[772]{0:T(1024)} %get-tuple-element.70.refs_4_, f32[8,4,200]{2,1,0:T(4,128)} %refs_5_.15, ...), custom_call_target="tpu_custom_call" | custom-call | flops 3840000 | bytes 5760000 | tf_op jit(solution)/shard_map/known_near_field_6/pallas_call | solution.py:643
  97.3 4.1 %all-to-all-done.6 = f32[32,7,1,128]{3,2,1,0:T(1,128)S(1)} async-done(((f32[32,7,1,128]{3,2,1,0:T(1,128)}), f32[32,7,1,128]{3,2,1,0:T(1,128)S(1)}, u32[]{:S(2)}, u32[]{:S(2)}) %all-to-all-start.6) | async-done | bytes 114720 | tf_op jit(solution)/shard_map/all_to_all | solution.py:635
  105.8 4.1 %known_near_field_7.1 = (f32[4,200]{1,0:T(4,128)S(1)}, f32[48,256]{1,0:T(8,128)S(1)}, f32[32,4,128]{2,1,0:T(4,128)S(1)}) custom-call(s32[4,12]{1,0:T(4,128)} %refs_0_.15, s32[4]{0:T(128)} %refs_1_.15, s32[4,12]{1,0:T(4,128)} %refs_2_.15, f32[4,12]{1,0:T(4,128)} %refs_3_.15, s32[772]{0:T(1024)} %get-tuple-element.70.refs_4_, f32[8,4,200]{2,1,0:T(4,128)} %refs_5_.15, ...), custom_call_target="tpu_custom_call" | custom-call | flops 3840000 | bytes 5760000 | tf_op jit(solution)/shard_map/known_near_field_7/pallas_call | solution.py:643
  109.9 4.1 %all-to-all-done.7 = f32[32,7,1,128]{3,2,1,0:T(1,128)S(1)} async-done(((f32[32,7,1,128]{3,2,1,0:T(1,128)}), f32[32,7,1,128]{3,2,1,0:T(1,128)S(1)}, u32[]{:S(2)}, u32[]{:S(2)}) %all-to-all-start.7) | async-done | bytes 114720 | tf_op jit(solution)/shard_map/all_to_all | solution.py:635
  (35 shorter events, 24.3 us)
Async XLA Ops:
  0.9 8.6 %collective-permute-start.2 = (f32[16,8,128]{2,1,0:T(8,128)S(1)}, f32[16,8,128]{2,1,0:T(8,128)S(1)}, u32[]{:S(2)}, u32[]{:S(2)}) collective-permute-start(f32[16,8,128]{2,1,0:T(8,128)S(1)} %pack_history.1), channel_id=1, source_target_pairs={{0,3},{1,2},{2,1},{3,0},{4,7},{5,6},{6,5},{7,4},{8,11},{9,10},{10,... | collective-permute-start | bytes 196616 | tf_op jit(solution)/shard_map/ppermute | solution.py:524
  4.8 4.6 %collective-permute-start.1 = (f32[16,8,128]{2,1,0:T(8,128)S(1)}, f32[16,8,128]{2,1,0:T(8,128)S(1)}, u32[]{:S(2)}, u32[]{:S(2)}) collective-permute-start(f32[16,8,128]{2,1,0:T(8,128)S(1)} %pack_history.1), channel_id=1, source_target_pairs={{0,2},{1,3},{2,0},{3,1},{4,6},{5,7},{6,4},{7,5},{8,10},{9,11},{10,... | collective-permute-start | bytes 196616 | tf_op jit(solution)/shard_map/ppermute | solution.py:524
  5.3 4.3 %collective-permute-start = (f32[16,8,128]{2,1,0:T(8,128)S(1)}, f32[16,8,128]{2,1,0:T(8,128)S(1)}, u32[]{:S(2)}, u32[]{:S(2)}) collective-permute-start(f32[16,8,128]{2,1,0:T(8,128)S(1)} %pack_history.1), channel_id=1, source_target_pairs={{0,1},{1,0},{2,3},{3,2},{4,5},{5,4},{6,7},{7,6},{8,9},{9,8},{10,11... | collective-permute-start | bytes 196616 | tf_op jit(solution)/shard_map/ppermute | solution.py:524
  9.7 9.3 %copy-start.3 = (f32[16,4,8,128]{3,2,1,0:T(8,128)}, f32[16,4,8,128]{3,2,1,0:T(8,128)S(1)}, u32[]{:S(2)}) copy-start(f32[16,4,8,128]{3,2,1,0:T(8,128)S(1)} %pad_maximum_fusion.1) | copy-start | bytes 786436
  9.7 8.5 %collective-permute-start.4 = (f32[16,32,128]{2,1,0:T(8,128)S(1)}, f32[16,32,128]{2,1,0:T(8,128)S(1)}, u32[]{:S(2)}, u32[]{:S(2)}) collective-permute-start(f32[16,32,128]{2,1,0:T(8,128)S(1)} %bitcast.42), channel_id=1, source_target_pairs={{4,8},{12,16},{20,24},{8,4},{16,12},{24,20},{5,9},{13,17},{21,25},... | collective-permute-start | bytes 786440 | tf_op jit(solution)/shard_map/ppermute | solution.py:628
  10.4 7.8 %collective-permute-start.3 = (f32[16,32,128]{2,1,0:T(8,128)S(1)}, f32[16,32,128]{2,1,0:T(8,128)S(1)}, u32[]{:S(2)}, u32[]{:S(2)}) collective-permute-start(f32[16,32,128]{2,1,0:T(8,128)S(1)} %bitcast.43), channel_id=1, source_target_pairs={{0,4},{4,0},{8,12},{12,8},{16,20},{20,16},{24,28},{28,24},{1,5},{5... | collective-permute-start | bytes 786440 | tf_op jit(solution)/shard_map/ppermute | solution.py:626
  13.4 13.0 %all-to-all-start = ((f32[32,7,1,128]{3,2,1,0:T(1,128)}), f32[32,7,1,128]{3,2,1,0:T(1,128)S(1)}, u32[]{:S(2)}, u32[]{:S(2)}) async-start(f32[32,7,1,128]{3,2,1,0:T(1,128)} %get-tuple-element.81), calls=%async_computation | async-start | bytes 229376 | tf_op jit(solution)/shard_map/all_to_all | solution.py:635
  18.2 0.8 copy-start.4
  18.2 0.8 copy-start.5
  19.0 7.4 %copy-start = (bf16[4,512,200]{1,2,0:T(8,128)(2,1)S(1)}, bf16[4,512,200]{1,2,0:T(8,128)(2,1)}, u32[]{:S(2)}) copy-start(bf16[4,512,200]{1,2,0:T(8,128)(2,1)} %param.21) | copy-start | bytes 2457604
  19.0 7.4 %copy-start.1 = (bf16[4,200,200]{2,1,0:T(8,128)(2,1)S(1)}, bf16[4,200,200]{2,1,0:T(8,128)(2,1)}, u32[]{:S(2)}) copy-start(bf16[4,200,200]{2,1,0:T(8,128)(2,1)} %refs_8_.31) | copy-start | bytes 960004
  19.0 7.4 %copy-start.2 = (f32[4,512]{1,0:T(4,128)S(1)}, f32[4,512]{1,0:T(4,128)}, u32[]{:S(2)}) copy-start(f32[4,512]{1,0:T(4,128)} %refs_9_.15) | copy-start | bytes 24580
  27.8 11.0 %all-to-all-start.1 = ((f32[32,7,1,128]{3,2,1,0:T(1,128)}), f32[32,7,1,128]{3,2,1,0:T(1,128)S(1)}, u32[]{:S(2)}, u32[]{:S(2)}) async-start(f32[32,7,1,128]{3,2,1,0:T(1,128)} %get-tuple-element.87), calls=%async_computation.1 | async-start | bytes 229376 | tf_op jit(solution)/shard_map/all_to_all | solution.py:635
  40.6 10.8 %all-to-all-start.2 = ((f32[32,7,1,128]{3,2,1,0:T(1,128)}), f32[32,7,1,128]{3,2,1,0:T(1,128)S(1)}, u32[]{:S(2)}, u32[]{:S(2)}) async-start(f32[32,7,1,128]{3,2,1,0:T(1,128)} %get-tuple-element.94), calls=%async_computation.2 | async-start | bytes 229376 | tf_op jit(solution)/shard_map/all_to_all | solution.py:635
  53.1 10.8 %all-to-all-start.3 = ((f32[32,7,1,128]{3,2,1,0:T(1,128)}), f32[32,7,1,128]{3,2,1,0:T(1,128)S(1)}, u32[]{:S(2)}, u32[]{:S(2)}) async-start(f32[32,7,1,128]{3,2,1,0:T(1,128)} %get-tuple-element.101), calls=%async_computation.3 | async-start | bytes 229376 | tf_op jit(solution)/shard_map/all_to_all | solution.py:635
  65.6 10.8 %all-to-all-start.4 = ((f32[32,7,1,128]{3,2,1,0:T(1,128)}), f32[32,7,1,128]{3,2,1,0:T(1,128)S(1)}, u32[]{:S(2)}, u32[]{:S(2)}) async-start(f32[32,7,1,128]{3,2,1,0:T(1,128)} %get-tuple-element.108), calls=%async_computation.4 | async-start | bytes 229376 | tf_op jit(solution)/shard_map/all_to_all | solution.py:635
  78.2 10.8 %all-to-all-start.5 = ((f32[32,7,1,128]{3,2,1,0:T(1,128)}), f32[32,7,1,128]{3,2,1,0:T(1,128)S(1)}, u32[]{:S(2)}, u32[]{:S(2)}) async-start(f32[32,7,1,128]{3,2,1,0:T(1,128)} %get-tuple-element.115), calls=%async_computation.5 | async-start | bytes 229376 | tf_op jit(solution)/shard_map/all_to_all | solution.py:635
  90.7 10.8 %all-to-all-start.6 = ((f32[32,7,1,128]{3,2,1,0:T(1,128)}), f32[32,7,1,128]{3,2,1,0:T(1,128)S(1)}, u32[]{:S(2)}, u32[]{:S(2)}) async-start(f32[32,7,1,128]{3,2,1,0:T(1,128)} %get-tuple-element.122), calls=%async_computation.6 | async-start | bytes 229376 | tf_op jit(solution)/shard_map/all_to_all | solution.py:635
  103.2 10.8 %all-to-all-start.7 = ((f32[32,7,1,128]{3,2,1,0:T(1,128)}), f32[32,7,1,128]{3,2,1,0:T(1,128)S(1)}, u32[]{:S(2)}, u32[]{:S(2)}) async-start(f32[32,7,1,128]{3,2,1,0:T(1,128)} %get-tuple-element.129), calls=%async_computation.7 | async-start | bytes 229376 | tf_op jit(solution)/shard_map/all_to_all | solution.py:635
